TPU v7x, 128 devices: a whole 4x4x4 slice. The times are simulated.
128 devices in a mesh: ctx: 32 (over y_lo, z, x), shard: 4 (over y_hi, core).
Axes of the slice: x: 4, y: 4 (y_hi: 2, y_lo: 2; y = y_hi * 2 + y_lo), z: 4, core: 2. Of those that a mesh axis runs over, the one named last changes fastest.
Arguments:
- inputs: bfloat16 [8, 2048, 1024], P('shard', 'ctx'), may hold values from -6 to 6
- cotangent: bfloat16 [8, 2048, 1024], P('shard', 'ctx'), may hold values from -6 to 6
- w_qkv: bfloat16 [1024, 3072], P('shard'), may hold values from -0.1875 to 0.1875
- bias_qv: bfloat16 [2, 1024], P(None, 'shard'), may hold values from -3 to 3
- w_out: bfloat16 [1024, 1024], P('shard'), may hold values from -4 to 4
- bias_out: bfloat16 [1024], P('shard'), may hold values from -3 to 3
- ln1_gain: bfloat16 [1024], P('shard'), may hold values from 0.099609375 to 1.8984375
- ln1_bias: bfloat16 [1024], P('shard'), may hold values from -3 to 3
- w_in: bfloat16 [1024, 4096], P('shard'), may hold values from -0.1875 to 0.1875
- bias_in: bfloat16 [4096], P('shard'), may hold values from -3 to 3
- w_ff_out: bfloat16 [4096, 1024], P('shard'), may hold values from -0.09375 to 0.09375
- bias_ff_out: bfloat16 [1024], P('shard'), may hold values from -3 to 3
- ln2_gain: bfloat16 [1024], P('shard'), may hold values from 0.099609375 to 1.8984375
- ln2_bias: bfloat16 [1024], P('shard'), may hold values from -3 to 3
Outputs:
- result: bfloat16 [8, 2048, 1024], P('shard', 'ctx')
- grad_inputs: float32 [8, 2048, 1024], P('shard', 'ctx')
- grad_w_qkv: float32 [1024, 3072], P('shard')
- grad_bias_qv: float32 [2, 1024], P(None, 'shard')
- grad_w_out: float32 [1024, 1024], P('shard')
- grad_bias_out: float32 [1024], P('shard')
- grad_ln1_gain: float32 [1024], P('shard')
- grad_ln1_bias: float32 [1024], P('shard')
- grad_w_in: float32 [1024, 4096], P('shard')
- grad_bias_in: float32 [4096], P('shard')
- grad_w_ff_out: float32 [4096, 1024], P('shard')
- grad_bias_ff_out: float32 [1024], P('shard')
- grad_ln2_gain: float32 [1024], P('shard')
- grad_ln2_bias: float32 [1024], P('shard')
All inputs are finite; a program needn't handle non-finite values.
Results may differ from a plain program's by a relative error of at most 0.03.
Values may be sent and summed in bfloat16 or wider, within the bound.
A program may use at most 192 MiB of HBM per device.

v0:
```python
import math

import jax
import jax.numpy as jnp
from jax import lax
from jax.sharding import PartitionSpec as P

D = 1024
H = 16
DH = 64


NORM_EPS = 1e-05
NEG_LARGE = -1e30


def in_one_piece(arrays, axis, dim, along):
    ends, at = ([], 0)
    for a in arrays[:-1]:
        at += a.shape[along]
        ends.append(at)
    both = jnp.concatenate(arrays, axis=along)
    return tuple(jnp.split(lax.all_gather(both, axis, axis=dim, tiled=True), ends, axis=along))


def in_one_piece_2(arrays, axis, dim, along):
    widths = [math.prod(a.shape[along:]) for a in arrays]
    both = jnp.concatenate(
        [a.reshape(*a.shape[:along], w) for a, w in zip(arrays, widths)], axis=along
    )
    out = lax.psum_scatter(both, axis, scatter_dimension=dim, tiled=True)
    pieces = jnp.split(out, [sum(widths[:k]) for k in range(1, len(widths))], axis=along)
    return tuple((b.reshape(*out.shape[:along], *a.shape[along:]) for a, b in zip(arrays, pieces)))


def layer_norm(values, norm_gain, norm_shift):
    row_mean = jnp.mean(values, axis=-1, keepdims=True)
    centered = values - row_mean
    row_var = jnp.mean(centered * centered, axis=-1, keepdims=True)
    return centered * lax.rsqrt(row_var + NORM_EPS) * norm_gain + norm_shift


def gelu_exact(values):
    return 0.5 * values * (1.0 + lax.erf(values * 0.7071067811865476))


def outer_sum(left, right):
    return lax.dot_general(
        left, right, (((0,), (0,)), ((), ())), preferred_element_type=jnp.float32
    )


def times_transposed(left, right):
    return lax.dot_general(
        left, right, (((1,), (1,)), ((), ())), preferred_element_type=jnp.float32
    )


def fold_keys(running, incoming, queries, score_scale):
    groups = incoming.shape[0]
    row_count = incoming.shape[1]
    step_rows = min(512, row_count)

    def one_block(state_now, block_index):
        run_max, run_sum, totals = state_now
        key_block = lax.dynamic_slice_in_dim(incoming, block_index * step_rows, step_rows, 1)
        key_part = key_block[:, :, :D].reshape(groups, step_rows, H, DH)
        value_part = key_block[:, :, D:].reshape(groups, step_rows, H, DH)
        scores = (
            jnp.einsum("gqhd,gkhd->gqhk", queries, key_part, preferred_element_type=jnp.float32)
            * score_scale
        )
        new_max = jnp.maximum(run_max, jnp.max(scores, axis=-1))
        factor = jnp.exp(run_max - new_max)
        expo = jnp.exp(scores - new_max[..., None])
        new_sum = run_sum * factor + jnp.sum(expo, axis=-1)
        added = jnp.einsum(
            "gqhk,gkhd->gqhd",
            expo.astype(jnp.bfloat16),
            value_part,
            preferred_element_type=jnp.float32,
        )
        return ((new_max, new_sum, totals * factor[..., None] + added), None)

    state_end, unused_out = lax.scan(
        one_block, running, jnp.arange(row_count // step_rows, dtype=jnp.int32)
    )
    return state_end


def local(
    inputs,
    cotangent,
    w_qkv,
    bias_qv,
    w_out,
    bias_out,
    ln1_gain,
    ln1_bias,
    w_in,
    bias_in,
    w_ff_out,
    bias_ff_out,
    ln2_gain,
    ln2_bias,
):
    score_scale = DH ** (-0.5)
    (
        w_qkv_all,
        bias_qv_all,
        w_out_all,
        bias_out_all,
        gain_one,
        shift_one,
        w_in_all,
        bias_in_all,
        w_ff_all,
        bias_ff_all,
        gain_two,
        shift_two,
    ) = (
        lax.all_gather(w_qkv, "shard", axis=0, tiled=True),
        lax.all_gather(bias_qv, "shard", axis=1, tiled=True),
        lax.all_gather(w_out, "shard", axis=0, tiled=True),
        lax.all_gather(bias_out, "shard", axis=0, tiled=True),
        lax.all_gather(ln1_gain, "shard", axis=0, tiled=True),
        lax.all_gather(ln1_bias, "shard", axis=0, tiled=True),
        lax.all_gather(w_in, "shard", axis=0, tiled=True),
        lax.all_gather(bias_in, "shard", axis=0, tiled=True),
        lax.all_gather(w_ff_out, "shard", axis=0, tiled=True),
        lax.all_gather(bias_ff_out, "shard", axis=0, tiled=True),
        lax.all_gather(ln2_gain, "shard", axis=0, tiled=True),
        lax.all_gather(ln2_bias, "shard", axis=0, tiled=True),
    )
    groups = inputs.shape[0]
    rows_dev = inputs.shape[1]
    token_count = groups * rows_dev
    tokens_in = inputs.reshape(token_count, D)
    bias_full = jnp.concatenate(
        [
            bias_qv_all[0].astype(jnp.float32),
            jnp.zeros((D,), jnp.float32),
            bias_qv_all[1].astype(jnp.float32),
        ]
    )
    projected = (
        jnp.dot(tokens_in, w_qkv_all, preferred_element_type=jnp.float32) + bias_full
    ).astype(jnp.bfloat16)
    queries = projected[:, :D].reshape(groups, rows_dev, H, DH)
    key_value = projected[:, D:].reshape(groups, rows_dev, 2 * D)
    start_state = (
        jnp.full((groups, rows_dev, H), NEG_LARGE, jnp.float32),
        jnp.zeros((groups, rows_dev, H), jnp.float32),
        jnp.zeros((groups, rows_dev, H, DH), jnp.float32),
    )
    all_keys = lax.all_gather(key_value, "ctx", axis=1, tiled=True)
    run_max, run_sum, totals = fold_keys(start_state, all_keys, queries, score_scale)
    log_total = run_max + jnp.log(run_sum)
    context = totals / run_sum[..., None]
    flat_context = context.astype(jnp.bfloat16).reshape(token_count, D)
    attended = jnp.dot(
        flat_context, w_out_all, preferred_element_type=jnp.float32
    ) + bias_out_all.astype(jnp.float32)
    first_sum = tokens_in.astype(jnp.float32) + attended
    hidden = layer_norm(first_sum, gain_one.astype(jnp.float32), shift_one.astype(jnp.float32))
    hidden_low = hidden.astype(jnp.bfloat16)
    pre_act = jnp.dot(
        hidden_low, w_in_all, preferred_element_type=jnp.float32
    ) + bias_in_all.astype(jnp.float32)
    act_low = gelu_exact(pre_act).astype(jnp.bfloat16)
    branch = jnp.dot(act_low, w_ff_all, preferred_element_type=jnp.float32) + bias_ff_all.astype(
        jnp.float32
    )
    second_sum = hidden + branch
    result_rows = layer_norm(
        second_sum, gain_two.astype(jnp.float32), shift_two.astype(jnp.float32)
    )
    w_qkv_back, w_out_back, gain_one_back, shift_one_back = (
        w_qkv_all,
        w_out_all,
        gain_one,
        shift_one,
    )
    w_in_back, w_ff_back, gain_two_back, shift_two_back = (w_in_all, w_ff_all, gain_two, shift_two)
    upstream = cotangent.reshape(token_count, D).astype(jnp.float32)
    unused_two, pull_two = jax.vjp(
        layer_norm,
        second_sum,
        gain_two_back.astype(jnp.float32),
        shift_two_back.astype(jnp.float32),
    )
    d_second, d_gain_two, d_shift_two = pull_two(upstream)
    d_branch = d_second.astype(jnp.bfloat16)
    grad_ff = outer_sum(act_low, d_branch)
    grad_bias_ff = jnp.sum(d_branch.astype(jnp.float32), axis=0)
    d_act = times_transposed(d_branch, w_ff_back)
    unused_act, pull_gelu = jax.vjp(gelu_exact, pre_act)
    d_pre_act = pull_gelu(d_act)[0].astype(jnp.bfloat16)
    grad_in = outer_sum(hidden_low, d_pre_act)
    grad_bias_in = jnp.sum(d_pre_act.astype(jnp.float32), axis=0)
    d_hidden = d_second + times_transposed(d_pre_act, w_in_back)
    unused_one, pull_one = jax.vjp(
        layer_norm, first_sum, gain_one_back.astype(jnp.float32), shift_one_back.astype(jnp.float32)
    )
    d_first, d_gain_one, d_shift_one = pull_one(d_hidden)
    d_attended = d_first.astype(jnp.bfloat16)
    grad_out = outer_sum(flat_context, d_attended)
    grad_bias_out = jnp.sum(d_attended.astype(jnp.float32), axis=0)
    d_context = (
        times_transposed(d_attended, w_out_back)
        .astype(jnp.bfloat16)
        .reshape(groups, rows_dev, H, DH)
    )
    row_delta = jnp.sum(d_context.astype(jnp.float32) * context, axis=-1)
    seq_len = all_keys.shape[1]
    step_rows = min(512, seq_len)
    block_count = seq_len // step_rows
    block_ids = jnp.arange(block_count, dtype=jnp.int32)

    def query_terms(d_query, block_index):
        key_block = lax.dynamic_slice_in_dim(all_keys, block_index * step_rows, step_rows, 1)
        key_part = key_block[:, :, :D].reshape(groups, step_rows, H, DH)
        value_part = key_block[:, :, D:].reshape(groups, step_rows, H, DH)
        scores = (
            jnp.einsum("gqhd,gkhd->gqhk", queries, key_part, preferred_element_type=jnp.float32)
            * score_scale
        )
        probs = jnp.exp(scores - log_total[..., None])
        d_probs = jnp.einsum(
            "gqhd,gkhd->gqhk", d_context, value_part, preferred_element_type=jnp.float32
        )
        d_scores = (probs * (d_probs - row_delta[..., None])).astype(jnp.bfloat16)
        return (
            d_query
            + jnp.einsum("gqhk,gkhd->gqhd", d_scores, key_part, preferred_element_type=jnp.float32)
            * score_scale,
            None,
        )

    d_query, unused_rows = lax.scan(
        query_terms, jnp.zeros((groups, rows_dev, H, DH), jnp.float32), block_ids
    )
    all_queries, all_d_context = in_one_piece(
        (projected[:, :D].reshape(groups, rows_dev, D), d_context.reshape(groups, rows_dev, D)),
        "ctx",
        1,
        0,
    )
    all_lse, all_delta = in_one_piece((log_total, row_delta), "ctx", 1, 0)
    own_keys = key_value[:, :, :D].reshape(groups, rows_dev, H, DH)
    own_values = key_value[:, :, D:].reshape(groups, rows_dev, H, DH)

    def own_terms(carried, block_index):
        d_keys, d_values = carried
        first = block_index * step_rows
        query_block = lax.dynamic_slice_in_dim(all_queries, first, step_rows, 1).reshape(
            groups, step_rows, H, DH
        )
        d_context_block = lax.dynamic_slice_in_dim(all_d_context, first, step_rows, 1).reshape(
            groups, step_rows, H, DH
        )
        lse_block = lax.dynamic_slice_in_dim(all_lse, first, step_rows, 1)
        delta_block = lax.dynamic_slice_in_dim(all_delta, first, step_rows, 1)
        scores = (
            jnp.einsum("gqhd,gkhd->gqhk", query_block, own_keys, preferred_element_type=jnp.float32)
            * score_scale
        )
        probs = jnp.exp(scores - lse_block[..., None])
        d_probs = jnp.einsum(
            "gqhd,gkhd->gqhk", d_context_block, own_values, preferred_element_type=jnp.float32
        )
        d_scores = (probs * (d_probs - delta_block[..., None])).astype(jnp.bfloat16)
        d_keys = (
            d_keys
            + jnp.einsum(
                "gqhk,gqhd->gkhd", d_scores, query_block, preferred_element_type=jnp.float32
            )
            * score_scale
        )
        d_values = d_values + jnp.einsum(
            "gqhk,gqhd->gkhd",
            probs.astype(jnp.bfloat16),
            d_context_block,
            preferred_element_type=jnp.float32,
        )
        return ((d_keys, d_values), None)

    zero_rows = jnp.zeros((groups, rows_dev, H, DH), jnp.float32)
    (own_d_keys, own_d_values), unused_keys = lax.scan(own_terms, (zero_rows, zero_rows), block_ids)
    d_key_value = jnp.concatenate(
        [own_d_keys.reshape(groups, rows_dev, D), own_d_values.reshape(groups, rows_dev, D)], axis=2
    )
    d_projected = jnp.concatenate(
        [d_query.reshape(token_count, D), d_key_value.reshape(token_count, 2 * D)], axis=1
    ).astype(jnp.bfloat16)
    grad_qkv = outer_sum(tokens_in, d_projected)
    column_sums = jnp.sum(d_projected.astype(jnp.float32), axis=0)
    grad_bias_qv = jnp.stack([column_sums[:D], column_sums[2 * D :]])
    d_inputs = d_first + times_transposed(d_projected, w_qkv_back)
    (
        own_qkv,
        own_bias_qv,
        own_out,
        own_bias_out,
        own_gain_one,
        own_shift_one,
        own_in,
        own_bias_in,
        own_ff,
        own_bias_ff,
        own_gain_two,
        own_shift_two,
    ) = (
        lax.psum_scatter(
            grad_qkv.astype(jnp.bfloat16), "shard", scatter_dimension=0, tiled=True
        ).astype(jnp.float32),
        lax.psum_scatter(
            grad_bias_qv.astype(jnp.bfloat16), "shard", scatter_dimension=1, tiled=True
        ).astype(jnp.float32),
        *tuple(
            (
                part.astype(jnp.float32)
                for part in in_one_piece_2(
                    (
                        grad_out.astype(jnp.bfloat16),
                        grad_bias_out.astype(jnp.bfloat16),
                        d_gain_one.astype(jnp.bfloat16),
                        d_shift_one.astype(jnp.bfloat16),
                        grad_in.astype(jnp.bfloat16),
                    ),
                    "shard",
                    0,
                    1,
                )
            )
        ),
        *tuple(
            (
                part.astype(jnp.float32)
                for part in in_one_piece_2(
                    (grad_bias_in.astype(jnp.bfloat16), grad_ff.astype(jnp.bfloat16)), "shard", 0, 1
                )
            )
        ),
        lax.psum_scatter(
            grad_bias_ff.astype(jnp.bfloat16), "shard", scatter_dimension=0, tiled=True
        ).astype(jnp.float32),
        lax.psum_scatter(
            d_gain_two.astype(jnp.bfloat16), "shard", scatter_dimension=0, tiled=True
        ).astype(jnp.float32),
        lax.psum_scatter(
            d_shift_two.astype(jnp.bfloat16), "shard", scatter_dimension=0, tiled=True
        ).astype(jnp.float32),
    )
    summed = (
        lax.psum(own_qkv.astype(jnp.bfloat16), "ctx").astype(jnp.float32),
        lax.psum(own_bias_qv.astype(jnp.bfloat16), "ctx").astype(jnp.float32),
        lax.psum(own_out.astype(jnp.bfloat16), "ctx").astype(jnp.float32),
        lax.psum(own_bias_out.astype(jnp.bfloat16), "ctx").astype(jnp.float32),
        lax.psum(own_gain_one.astype(jnp.bfloat16), "ctx").astype(jnp.float32),
        lax.psum(own_shift_one.astype(jnp.bfloat16), "ctx").astype(jnp.float32),
        lax.psum(own_in.astype(jnp.bfloat16), "ctx").astype(jnp.float32),
        lax.psum(own_bias_in.astype(jnp.bfloat16), "ctx").astype(jnp.float32),
        lax.psum(own_ff.astype(jnp.bfloat16), "ctx").astype(jnp.float32),
        lax.psum(own_bias_ff.astype(jnp.bfloat16), "ctx").astype(jnp.float32),
        lax.psum(own_gain_two.astype(jnp.bfloat16), "ctx").astype(jnp.float32),
        lax.psum(own_shift_two.astype(jnp.bfloat16), "ctx").astype(jnp.float32),
    )
    return (
        result_rows.astype(jnp.bfloat16).reshape(groups, rows_dev, D),
        d_inputs.reshape(groups, rows_dev, D),
        summed[0],
        summed[1],
        summed[2],
        summed[3],
        summed[4],
        summed[5],
        summed[6],
        summed[7],
        summed[8],
        summed[9],
        summed[10],
        summed[11],
    )


def solution(mesh):
    in_specs = (
        P("shard", "ctx", None),
        P("shard", "ctx", None),
        P("shard", None),
        P(None, "shard"),
        P("shard", None),
        P("shard"),
        P("shard"),
        P("shard"),
        P("shard", None),
        P("shard"),
        P("shard", None),
        P("shard"),
        P("shard"),
        P("shard"),
    )
    out_specs = (
        P("shard", "ctx", None),
        P("shard", "ctx", None),
        P("shard", None),
        P(None, "shard"),
        P("shard", None),
        P("shard"),
        P("shard"),
        P("shard"),
        P("shard", None),
        P("shard"),
        P("shard", None),
        P("shard"),
        P("shard"),
        P("shard"),
    )
    return jax.shard_map(local, mesh=mesh, in_specs=in_specs, out_specs=out_specs, check_vma=False)
```

profile of v0, /device:TPU:0, one launch (start us, length us, event | category | flops | bytes accessed | tf_op | source)
XLA Modules:
  0.0 1305.5 jit_solution(9905278094842168943)
XLA Ops:
  8.0 6.8 all_gather.46
  14.8 47.8 %all-gather.13.cloned.1.call-done = bf16[1024,3072]{1,0:T(8,128)(2,1)} async-done(((bf16[256,3072]{1,0:T(8,128)(2,1)}), bf16[1024,3072]{1,0:T(8,128)(2,1)}) %all-gather.13.cloned.1.call-update) | async-done | bytes 6291472 | tf_op jit(solution)/shard_map/all_gather | solution.py:122
  77.4 6.7 all_gather.53
  110.4 6.8 all-gather.5
  118.6 143.2 %all-gather.15.cloned.1.call-done = bf16[2,2048,2048]{2,0,1:T(2,128)(2,1)} async-done(((bf16[2,64,2048]{2,0,1:T(2,128)(2,1)}), bf16[2,2048,2048]{2,0,1:T(2,128)(2,1)}) %all-gather.15.cloned.1.call-update) | async-done | bytes 16777232 | tf_op jit(solution)/shard_map/all_gather | solution.py:156
  261.8 41.3 %copy.143 = bf16[2,2048,2048]{1,2,0:T(8,128)(2,1)} copy(bf16[2,2048,2048]{2,0,1:T(2,128)(2,1)} %all-gather.15.cloned.1.call-done) | data formatting | bytes 33554432
  303.1 52.7 %while.39 = (s32[]{:T(128)}, f32[2,64,16]{1,2,0:T(8,128)S(1)}, f32[2,64,16]{1,2,0:T(8,128)S(1)}, f32[2,64,16,64]{1,3,2,0:T(8,128)}, s32[4]{0:T(128)S(1)}, /*inde...) while((s32[]{:T(128)}, f32[2,64,16]{1,2,0:T(8,128)S(1)}, ...), condition=%wide.region_3.4_spmd.clone, body=%wide.region_0.3_spmd.clone.sunk | while | flops 277227520 | bytes 43385072 | solution.py:85
  366.0 49.8 %all-gather.21.cloned.1.call-done = bf16[4096,1024]{1,0:T(8,128)(2,1)} async-done(((bf16[1024,1024]{1,0:T(8,128)(2,1)}), bf16[4096,1024]{1,0:T(8,128)(2,1)}) %all-gather.21.cloned.1.call-update) | async-done | bytes 8388624 | tf_op jit(solution)/shard_map/all_gather | solution.py:130
  440.8 9.7 pad_maximum_fusion
  457.7 7.1 convolution_convert_fusion.1
  464.8 18.9 %concatenate.32 = bf16[1024,5123]{1,0:T(8,128)(2,1)} concatenate(bf16[1024,1024]{1,0:T(8,128)(2,1)S(1)} %copy-done.5, bf16[1024,1]{1,0:T(8,128)(2,1)} %reshape.257, bf16[1024,1]{1,0:T(8,128)(2,1)} %convert_element_type.263, bf16[1024,1]{1,0:T(8,128)(2,1)} %convert_element_type.264, bf16[1024,4096]{1,0:T(8,128)(2,1)} %convolution_convert_fusion.1), dimensions={1} | concatenate | bytes 20983808 | tf_op jit(solution)/shard_map/concatenate | solution.py:28
  488.9 55.9 %while.40 = (s32[]{:T(128)}, f32[2,64,16,64]{1,3,2,0:T(8,128)}, s32[4]{0:T(128)S(1)}, bf16[2,2048,2048]{1,2,0:T(8,128)(2,1)}, bf16[2,64,16,64]{3,1,2,0:T(8,128)(...) while((s32[]{:T(128)}, f32[2,64,16,64]{1,3,2,0:T(8,128)}, ...), condition=%wide.region_14.15_spmd.clone, body=%wide.region_13.14_spmd.clone.sunk | while | flops 408289280 | bytes 24658140 | solution.py:240
  547.1 140.9 %all_gather.59 = f32[4,2048,16]{2,0,1:T(4,128)S(1)} all-gather(f32[4,64,16]{2,0,1:T(4,128)S(1)} %copy.158), channel_id=1, replica_groups=mesh['ctx'=32,'shard'=4] {'ctx'}, dimensions={1}, use_global_device_ids=true | all-gather | bytes 540672 | tf_op jit(solution)/shard_map/all_gather | solution.py:23
  695.9 19.3 %fusion.61 = (bf16[2,2048,1024]{2,0,1:T(2,128)(2,1)}, bf16[2,2048,1024]{2,0,1:T(2,128)(2,1)}) fusion(bf16[4,2048,1024]{2,0,1:T(4,128)(2,1)} %all-gather.23.cloned.1.call-done), kind=kLoop, calls=%fused_computation.118 | loop fusion | bytes 33554432 | tf_op jit(solution)/shard_map/split | solution.py:23
  715.2 136.4 %while.41 = (s32[]{:T(128)}, f32[2,64,16,64]{1,3,2,0:T(8,128)}, f32[2,64,16,64]{1,3,2,0:T(8,128)S(1)}, s32[4]{0:T(128)S(1)}, bf16[2,2048,1024]{2,0,1:T(2,128)(2,...) while((s32[]{:T(128)}, f32[2,64,16,64]{1,3,2,0:T(8,128)}, ...), condition=%wide.region_16.17_spmd.clone, body=%wide.region_15.16_spmd.clone.sunk | while | flops 545914880 | bytes 40829144 | solution.py:289
  716.5 7.4 constant_dynamic-slice_fusion.14
  750.1 7.9 constant_dynamic-slice_fusion.14
  785.1 7.4 constant_dynamic-slice_fusion.14
  819.1 7.1 constant_dynamic-slice_fusion.14
  870.3 50.3 %reduce-scatter.7.cloned.1.call-done = bf16[256,3072]{0,1:T(8,128)(2,1)} async-done(((bf16[1024,3072]{0,1:T(8,128)(2,1)}), bf16[256,3072]{0,1:T(8,128)(2,1)}) %reduce-scatter.7.cloned.1.call-update) | async-done | bytes 1572880 | tf_op jit(solution)/shard_map/reduce_scatter | solution.py:314
  922.9 7.3 all-reduce.5
  938.3 11.9 reduce-scatter.13.cloned.1.call-done
  951.1 83.5 %all-reduce.3 = (bf16[2,256]{1,0:T(2,128)(2,1)S(1)}, bf16[256]{0:T(256)(128)(2,1)S(1)}, bf16[256]{0:T(256)(128)(2,1)S(1)}, bf16[256]{0:T(256)(128)(2,1)S(1)}, bf...) all-reduce(bf16[2,256]{1,0:T(2,128)(2,1)S(1)} %copy.174, ...), channel_id=1, replica_groups=mesh['ctx'=32,'shard'=4] {'ctx'}, use_global_device_ids=true, to_apply=%region_21.22 | all-reduce | flops 3072 | bytes 12288 | tf_op jit(solution)/shard_map/psum | solution.py:357
  1039.2 248.1 %all-reduce.8.cloned.1.call-done = (bf16[256,3072]{0,1:T(8,128)(2,1)}, bf16[1024,1024]{0,1:T(8,128)(2,1)}, bf16[256,1024]{1,0:T(8,128)(2,1)}, bf16[256,4096]{1,0:T(8,128)(2,1)}) async-done(((bf16[256,3072]{0,1:T(8,128)(2,1)}, bf16[1024,1024]{0,1:T(8,128)(2,1)}, bf16[256,1024]{1,0:T(8,128)(2,1)}, bf16[256,4096]{1,0:T(8,128)(2,1)}), (bf16[256,3072]{0,1:T(8,128)(2,1)}, bf16[1024,1024]{0,1:T(8,128)(2,1)}, ...) | async-done | bytes 6291472 | tf_op jit(solution)/shard_map/psum | solution.py:356
  (317 shorter events, 352.3 us)
Async XLA Ops:
  7.2 55.4 %all-gather.13.cloned.1.call-start = ((), (), s32[]{:S(2)}) async-start(), calls=%async_computation.4 | async-start | bytes 7864320 | tf_op jit(solution)/shard_map/all_gather | solution.py:122
  7.9 253.9 %all-gather.15.cloned.1.call-start = ((), (), s32[]{:S(2)}) async-start(), calls=%async_computation.5 | async-start | bytes 17301504 | tf_op jit(solution)/shard_map/all_gather | solution.py:156
  68.7 289.3 %all-gather.17.cloned.1.call-start = ((), (), s32[]{:S(2)}) async-start(), calls=%async_computation.6 | async-start | bytes 2621440 | tf_op jit(solution)/shard_map/all_gather | solution.py:124
  69.4 7.9 copy-start.23
  69.4 14.6 %copy-start.27 = (bf16[256]{0:T(256)(128)(2,1)S(1)}, bf16[256]{0:T(256)(128)(2,1)}, u32[]{:S(2)}) copy-start(bf16[256]{0:T(256)(128)(2,1)} %param.25) | copy-start | bytes 1540
  69.5 21.1 %copy-start.28 = (bf16[256]{0:T(256)(128)(2,1)S(1)}, bf16[256]{0:T(256)(128)(2,1)}, u32[]{:S(2)}) copy-start(bf16[256]{0:T(256)(128)(2,1)} %param.27) | copy-start | bytes 1540
  69.5 27.7 %copy-start.29 = (bf16[256]{0:T(256)(128)(2,1)S(1)}, bf16[256]{0:T(256)(128)(2,1)}, u32[]{:S(2)}) copy-start(bf16[256]{0:T(256)(128)(2,1)} %param.26) | copy-start | bytes 1540
  69.5 34.3 %copy-start.30 = (bf16[256]{0:T(256)(128)(2,1)S(1)}, bf16[256]{0:T(256)(128)(2,1)}, u32[]{:S(2)}) copy-start(bf16[256]{0:T(256)(128)(2,1)} %param.32) | copy-start | bytes 1540
  69.5 40.9 %copy-start.31 = (bf16[256]{0:T(256)(128)(2,1)S(1)}, bf16[256]{0:T(256)(128)(2,1)}, u32[]{:S(2)}) copy-start(bf16[256]{0:T(256)(128)(2,1)} %param.33) | copy-start | bytes 1540
  69.5 290.9 %all-gather.19.cloned.1.call-start = ((), (), s32[]{:S(2)}) async-start(), calls=%async_computation.7 | async-start | bytes 10485760 | tf_op jit(solution)/shard_map/all_gather | solution.py:128
  70.1 345.7 %all-gather.21.cloned.1.call-start = ((), (), s32[]{:S(2)}) async-start(), calls=%async_computation.8 | async-start | bytes 10485760 | tf_op jit(solution)/shard_map/all_gather | solution.py:130
  70.7 625.2 %all-gather.23.cloned.1.call-start = ((), (), s32[]{:S(2)}) async-start(), calls=%async_computation.9 | async-start | bytes 17301504 | tf_op jit(solution)/shard_map/all_gather | solution.py:23
  415.8 7.8 slice-start.2
  415.8 5.3 copy-start.14
  415.8 7.8 slice-start.3
  435.1 425.4 %reduce-scatter.11.cloned.1.call-start = ((), (), s32[]{:S(2)}) async-start(), calls=%async_computation.12 | async-start | bytes 10567680 | tf_op jit(solution)/shard_map/reduce_scatter | solution.py:31
  450.6 413.5 %reduce-scatter.9.cloned.1.call-start = ((), (), s32[]{:S(2)}) async-start(), calls=%async_computation.11 | async-start | bytes 13434880 | tf_op jit(solution)/shard_map/reduce_scatter | solution.py:31
  457.7 7.2 copy-start.5
  483.7 436.9 %reduce-scatter.7.cloned.1.call-start = ((), (), s32[]{:S(2)}) async-start(), calls=%async_computation.10 | async-start | bytes 7864320 | tf_op jit(solution)/shard_map/reduce_scatter | solution.py:314
  695.9 19.4 %copy-start.2 = (f32[2,64,16,64]{1,3,2,0:T(8,128)S(1)}, f32[2,64,16,64]{1,3,2,0:T(8,128)}, u32[]{:S(2)}) copy-start(f32[2,64,16,64]{1,3,2,0:T(8,128)} %custom-call.5) | copy-start | bytes 1572868
  859.2 91.0 %reduce-scatter.13.cloned.1.call-start = ((), (), s32[]{:S(2)}) async-start(), calls=%async_computation.13 | async-start | bytes 327680
  860.4 426.9 %all-reduce.8.cloned.1.call-start = ((), (), s32[]{:S(2)}) async-start(), calls=%async_computation.14 | async-start | bytes 12582912 | tf_op jit(solution)/shard_map/psum | solution.py:356
  920.6 11.8 copy-start.7
  920.6 11.8 copy-start.25
  (27 other events, 63.9 us)
Sparse Core Ops, SparseCore 0:
  9.7 52.8 all-gather.12
  68.8 192.9 all-gather.14
  263.5 25.6 all-gather.16
  290.7 61.7 all-gather.18
  354.0 61.7 all-gather.20
  435.2 222.4 all-gather.22
  660.4 79.7 reduce-scatter.10
  742.9 93.3 reduce-scatter.8
  859.3 61.2 reduce-scatter.6
  923.8 26.3 reduce-scatter.12
  954.1 333.1 all-reduce.7
where the time goes:
time: 1310 us
  waiting for transfers between devices  554 us (42%)
  blocking collectives  285 us (22%)
  local copies, waits for them, and re-layouts  239 us (18%)
  matrix products  161 us (12%)
  other arithmetic  42.3 us (3%)
  between operations  15.6 us (1%)
    psum x1, waiting for transfers between devices, local(): lax.psum(own_qkv.astype(jnp.bfloat16), 'ctx').astype(jnp.float32)  248 us
    all_gather x1, waiting for transfers between devices, local(): all_keys = lax.all_gather(key_value, 'ctx', axis=1, tiled=True)  143 us
    all_gather x1, blocking collectives, in_one_piece(): lax.all_gather(both, axis, axis=dim, tiled=True)  141 us
    psum x1, blocking collectives, local(): lax.psum(own_bias_qv.astype(jnp.bfloat16), 'ctx').astype(jnp.float32)  83.5 us
    unnamed x97, local copies, waits for them, and re-layouts  61.6 us
    dynamic_slice x8, local copies, waits for them, and re-layouts, own_terms(): lax.dynamic_slice_in_dim(all_d_context, first, step_rows, 1)  54.4 us
    reduce_scatter x1, waiting for transfers between devices, local(): lax.psum_scatter(grad_qkv.astype(jnp.bfloat16), 'shard', scatter_dimensio...  50.3 us
    all_gather x1, waiting for transfers between devices, local(): lax.all_gather(w_ff_out, 'shard', axis=0, tiled=True)  49.8 us
  transfers between devices with their start and end apart: 11, of which 6 were waited for; matrix products, arithmetic and copies ran while one was open for 31% of the time, Pallas kernels for 0%

commit v1 on v0

v1 whole, which is shorter than its diff:
```python
import functools

import jax
import jax.numpy as jnp
from jax import lax
from jax.experimental import pallas as pl
from jax.experimental.pallas import tpu as pltpu
from jax.sharding import PartitionSpec as P

D = 1024
H = 16
DH = 64
FF = 4096
NC = 32
SCALE = DH ** (-0.5)
MESH = pl.DeviceIdType.MESH
NORM_EPS = 1e-05
VMEM_LIMIT = 56 * 1024 * 1024
VM = pl.BlockSpec(memory_space=pltpu.VMEM)
ANY = pl.BlockSpec(memory_space=pl.ANY)


def layer_norm(values, norm_gain, norm_shift):
    row_mean = jnp.mean(values, axis=-1, keepdims=True)
    centered = values - row_mean
    row_var = jnp.mean(centered * centered, axis=-1, keepdims=True)
    return centered * lax.rsqrt(row_var + NORM_EPS) * norm_gain + norm_shift


def gelu_exact(values):
    return 0.5 * values * (1.0 + lax.erf(values * 0.7071067811865476))


def outer_sum(left, right):
    return lax.dot_general(
        left, right, (((0,), (0,)), ((), ())), preferred_element_type=jnp.float32
    )


def times_transposed(left, right):
    return lax.dot_general(
        left, right, (((1,), (1,)), ((), ())), preferred_element_type=jnp.float32
    )


def pack_tokens(src, send, parts):
    def step(hp, carry):
        for g in range(2):
            for part in range(parts):
                cols = pl.ds(pl.multiple_of(part * D + hp * 128, 128), 128)
                a = src[pl.ds(g * 64, 32), cols]
                b = src[pl.ds(g * 64 + 32, 32), cols]
                rows = pl.ds(part * 32, 32)
                send[g * 16 + 2 * hp, rows, :] = jnp.concatenate([a[:, :64], b[:, :64]], axis=1)
                send[g * 16 + 2 * hp + 1, rows, :] = jnp.concatenate(
                    [a[:, 64:], b[:, 64:]], axis=1
                )
        return carry

    lax.fori_loop(0, H // 2, step, 0)


def unpack_tokens(recv, dst, parts):
    def step(hp, carry):
        for g in range(2):
            for part in range(parts):
                cols = pl.ds(pl.multiple_of(part * D + hp * 128, 128), 128)
                rows = pl.ds(part * 32, 32)
                even = recv[g * 16 + 2 * hp, rows, :]
                odd = recv[g * 16 + 2 * hp + 1, rows, :]
                dst[pl.ds(g * 64, 32), cols] = jnp.concatenate([even[:, :64], odd[:, :64]], axis=1)
                dst[pl.ds(g * 64 + 32, 32), cols] = jnp.concatenate(
                    [even[:, 64:], odd[:, 64:]], axis=1
                )
        return carry

    lax.fori_loop(0, H // 2, step, 0)


def a2a_start(send, recv, ssem, rsem, me):
    def step(k, carry):
        dest = lax.rem(me + k, NC)
        pltpu.make_async_remote_copy(
            src_ref=send.at[dest],
            dst_ref=recv.at[me],
            send_sem=ssem.at[k],
            recv_sem=rsem.at[k],
            device_id={"ctx": dest},
            device_id_type=MESH,
        ).start()
        return carry

    lax.fori_loop(1, NC, step, 0)


def a2a_wait(send, recv, ssem, rsem, me):
    def step(k, carry):
        source = lax.rem(me + NC - k, NC)
        copy = pltpu.make_async_remote_copy(
            src_ref=send.at[source],
            dst_ref=recv.at[source],
            send_sem=ssem.at[k],
            recv_sem=rsem.at[k],
            device_id={"ctx": source},
            device_id_type=MESH,
        )
        copy.wait_send()
        copy.wait_recv()
        return carry

    lax.fori_loop(1, NC, step, 0)


def signal_ctx_peers(barrier, me):
    def step(k, carry):
        pl.semaphore_signal(
            barrier, inc=1, device_id={"ctx": lax.rem(me + k, NC)}, device_id_type=MESH
        )
        return carry

    lax.fori_loop(1, NC, step, 0)


def halves(packed):
    return jnp.concatenate([packed[:, :64], packed[:, 64:]], axis=0)


def dot_nt(a, b):
    return lax.dot_general(a, b, (((1,), (1,)), ((), ())), preferred_element_type=jnp.float32)


def dot_nn(a, b):
    return jnp.dot(a, b, preferred_element_type=jnp.float32)


QB = 256


def attn_fwd_kernel(
    proj, ctx_out, qkv_out, o_out, lse_out, send, recv, send2, recv2, keys, vt, ssem, rsem, ssem2, rsem2
):
    me = lax.axis_index("ctx")
    barrier = pltpu.get_barrier_semaphore()
    signal_ctx_peers(barrier, me)
    pack_tokens(proj, send, 3)
    pl.semaphore_wait(barrier, NC - 1)
    a2a_start(send, recv, ssem, rsem, me)
    recv[me] = send[me]
    a2a_wait(send, recv, ssem, rsem, me)
    qkv_out[...] = recv[...]
    keys[...] = halves(recv[:, 32:64, :].reshape(1024, 128))
    vp = recv[:, 64:96, :].reshape(1024, 128).astype(jnp.float32).T.astype(jnp.bfloat16)
    vt[...] = jnp.concatenate([vp[:64], vp[64:]], axis=1)

    def step(i, carry):
        qp = recv[pl.ds(i * 8, 8), 0:32, :].reshape(QB, 128) * jnp.bfloat16(SCALE)
        s = dot_nt(keys[...], halves(qp))
        m = jnp.max(s, axis=0, keepdims=True)
        p = jnp.exp(s - m)
        total = jnp.sum(p, axis=0, keepdims=True)
        ot = dot_nn(vt[...], p.astype(jnp.bfloat16)) / total
        o = jnp.concatenate([ot[:, :QB], ot[:, QB:]], axis=0).T
        o_out[pl.ds(pl.multiple_of(i * QB, QB), QB), :] = o
        lse_out[i] = m + jnp.log(total)
        send2[pl.ds(i * 8, 8)] = o.astype(jnp.bfloat16).reshape(8, 32, 128)
        return carry

    lax.fori_loop(0, 4, step, 0)
    a2a_start(send2, recv2, ssem2, rsem2, me)
    recv2[me] = send2[me]
    a2a_wait(send2, recv2, ssem2, rsem2, me)
    unpack_tokens(recv2, ctx_out, 1)


def attn_fwd(projected):
    return pl.pallas_call(
        attn_fwd_kernel,
        out_shape=(
            jax.ShapeDtypeStruct((128, D), jnp.bfloat16),
            jax.ShapeDtypeStruct((NC, 96, 128), jnp.bfloat16),
            jax.ShapeDtypeStruct((1024, 128), jnp.float32),
            jax.ShapeDtypeStruct((4, 1, 2 * QB), jnp.float32),
        ),
        in_specs=[VM],
        out_specs=(VM, VM, VM, VM),
        scratch_shapes=[
            pltpu.VMEM((NC, 96, 128), jnp.bfloat16),
            pltpu.VMEM((NC, 96, 128), jnp.bfloat16),
            pltpu.VMEM((NC, 32, 128), jnp.bfloat16),
            pltpu.VMEM((NC, 32, 128), jnp.bfloat16),
            pltpu.VMEM((2048, DH), jnp.bfloat16),
            pltpu.VMEM((DH, 2048), jnp.bfloat16),
            pltpu.SemaphoreType.DMA((NC,)),
            pltpu.SemaphoreType.DMA((NC,)),
            pltpu.SemaphoreType.DMA((NC,)),
            pltpu.SemaphoreType.DMA((NC,)),
        ],
        compiler_params=pltpu.CompilerParams(
            collective_id=0, has_side_effects=True, vmem_limit_bytes=VMEM_LIMIT
        ),
    )(projected)


def group_ids():
    c = lax.axis_index("ctx")
    s = lax.axis_index("shard")
    core = lax.rem(s, 2)
    other = 2 - 2 * lax.div(s, 2)
    sibling = s + 1 - 2 * core
    cross_c = lax.rem(c + NC // 2, NC)
    return ((c, sibling), (cross_c, other + core), (cross_c, other + 1 - core))


def mesh_id(pair):
    return {"ctx": pair[0], "shard": pair[1]}


def attn_bwd_kernel(
    dctx, qkv, o_in, lse_in, act, dpre, datt, hid, dbr, ctx, xin,
    dproj_out, dproj_g, act_g, dpre_g, datt_g, hid_g, dbr_g, ctx_g, x_g,
    send, recv, send2, recv2, keys, kt, vals, dk, dv, dproj,
    ssem, rsem, ssem2, rsem2, xs, xr, fs, fr, ls, ps, pr, pls,
):
    me = lax.axis_index("ctx")
    shard = lax.axis_index("shard")
    peers = group_ids()
    barrier = pltpu.get_barrier_semaphore()
    signal_ctx_peers(barrier, me)
    for peer in peers:
        pl.semaphore_signal(barrier, inc=1, device_id=mesh_id(peer), device_id_type=MESH)
    pack_tokens(dctx, send, 1)
    pl.semaphore_wait(barrier, NC + 2)
    a2a_start(send, recv, ssem, rsem, me)

    def remote(src, dst, ssem_, rsem_, peer):
        copy = pltpu.make_async_remote_copy(
            src_ref=src, dst_ref=dst, send_sem=ssem_, recv_sem=rsem_,
            device_id=mesh_id(peer), device_id_type=MESH,
        )
        copy.start()
        return copy

    slices = ((act, act_g, 1024), (dpre, dpre_g, 1024), (datt, datt_g, 256))
    whole = ((hid, hid_g), (dbr, dbr_g), (ctx, ctx_g), (xin, x_g))
    pending, arriving = [], []
    for n, (src, dst) in enumerate(whole):
        pending.append(remote(src, dst.at[1], xs.at[n, 0], xr.at[n, 0], peers[0]))
        arriving.append(remote(src, dst.at[2], xs.at[n, 1], xr.at[n, 1], peers[1]))
        local = pltpu.make_async_copy(src, dst.at[0], ls.at[n])
        local.start()
        pending.append(local)
    for n, (src, dst, width) in enumerate(slices):
        for k, peer in enumerate(peers):
            cols = pl.ds(pl.multiple_of(peer[1] * width, width), width)
            pending.append(
                remote(src.at[:, cols], dst.at[k + 1], xs.at[4 + n, k], xr.at[4 + n, k], peer)
            )
        cols = pl.ds(pl.multiple_of(shard * width, width), width)
        local = pltpu.make_async_copy(src.at[:, cols], dst.at[0], ls.at[4 + n])
        local.start()
        pending.append(local)

    recv[me] = send[me]
    keys[...] = halves(qkv[:, 32:64, :].reshape(1024, 128))
    vals[...] = halves(qkv[:, 64:96, :].reshape(1024, 128))
    kp = qkv[:, 32:64, :].reshape(1024, 128).astype(jnp.float32).T.astype(jnp.bfloat16)
    kt[...] = jnp.concatenate([kp[:64], kp[64:]], axis=1)
    dk[...] = jnp.zeros_like(dk)
    dv[...] = jnp.zeros_like(dv)
    a2a_wait(send, recv, ssem, rsem, me)

    def step(i, carry):
        blocks = pl.ds(i * 8, 8)
        qb = halves(qkv[blocks, 0:32, :].reshape(QB, 128) * jnp.bfloat16(SCALE))
        dop = recv[blocks].reshape(QB, 128)
        o = o_in[pl.ds(pl.multiple_of(i * QB, QB), QB), :]
        prod = (dop.astype(jnp.float32) * o).T
        delta = jnp.concatenate(
            [
                jnp.sum(prod[:64], axis=0, keepdims=True),
                jnp.sum(prod[64:], axis=0, keepdims=True),
            ],
            axis=1,
        )
        dob = halves(dop)
        probs = jnp.exp(dot_nt(keys[...], qb) - lse_in[i])
        dv[...] += dot_nn(probs.astype(jnp.bfloat16), dob)
        ds = (probs * (dot_nt(vals[...], dob) - delta)).astype(jnp.bfloat16)
        dk[...] += dot_nn(ds, qb)
        dqt = dot_nn(kt[...], ds) * SCALE
        dq = jnp.concatenate([dqt[:, :QB], dqt[:, QB:]], axis=0).T
        send2[blocks, 0:32, :] = dq.astype(jnp.bfloat16).reshape(8, 32, 128)
        return carry

    lax.fori_loop(0, 4, step, 0)
    for n, total in enumerate((dk, dv)):
        packed = jnp.concatenate([total[0:1024, :], total[1024:2048, :]], axis=1)
        send2[:, 32 + 32 * n : 64 + 32 * n, :] = packed.astype(jnp.bfloat16).reshape(NC, 32, 128)
    a2a_start(send2, recv2, ssem2, rsem2, me)
    recv2[me] = send2[me]
    for n, (src, dst) in enumerate(whole):
        arriving[n].wait()
        pending.append(remote(dst.at[2], dst.at[3], fs.at[n], fr.at[n], peers[0]))
    a2a_wait(send2, recv2, ssem2, rsem2, me)
    unpack_tokens(recv2, dproj, 3)
    for k, peer in enumerate(peers):
        cols = pl.ds(pl.multiple_of(peer[1] * 768, 256), 768)
        pending.append(remote(dproj.at[:, cols], dproj_g.at[k + 1], ps.at[k], pr.at[k], peer))
    cols = pl.ds(pl.multiple_of(shard * 768, 256), 768)
    local = pltpu.make_async_copy(dproj.at[:, cols], dproj_g.at[0], pls.at[0])
    local.start()
    pending.append(local)
    local = pltpu.make_async_copy(dproj, dproj_out, pls.at[1])
    local.start()
    pending.append(local)
    for copy in pending:
        copy.wait()


def attn_bwd(dctx, qkv, o, lse, act, dpre, datt, hid, dbr, ctx, xin):
    bf = jnp.bfloat16
    sds = jax.ShapeDtypeStruct
    dma = pltpu.SemaphoreType.DMA
    return pl.pallas_call(
        attn_bwd_kernel,
        out_shape=(
            sds((128, 3 * D), bf), sds((4, 128, 768), bf), sds((4, 128, 1024), bf),
            sds((4, 128, 1024), bf), sds((4, 128, 256), bf), sds((4, 128, 1024), bf),
            sds((4, 128, 1024), bf), sds((4, 128, 1024), bf), sds((4, 128, 1024), bf),
        ),
        in_specs=[VM] * 4 + [ANY] * 7,
        out_specs=(ANY,) * 9,
        scratch_shapes=[
            pltpu.VMEM((NC, 32, 128), bf),
            pltpu.VMEM((NC, 32, 128), bf),
            pltpu.VMEM((NC, 96, 128), bf),
            pltpu.VMEM((NC, 96, 128), bf),
            pltpu.VMEM((2048, DH), bf),
            pltpu.VMEM((DH, 2048), bf),
            pltpu.VMEM((2048, DH), bf),
            pltpu.VMEM((2048, DH), jnp.float32),
            pltpu.VMEM((2048, DH), jnp.float32),
            pltpu.VMEM((128, 3 * D), bf),
            dma((NC,)), dma((NC,)), dma((NC,)), dma((NC,)),
            dma((7, 3)), dma((7, 3)), dma((4,)), dma((4,)), dma((7,)),
            dma((3,)), dma((3,)), dma((2,)),
        ],
        compiler_params=pltpu.CompilerParams(
            collective_id=1, has_side_effects=True, vmem_limit_bytes=VMEM_LIMIT
        ),
    )(dctx, qkv, o, lse, act, dpre, datt, hid, dbr, ctx, xin)


GW = (1024, 768, 256, 1024)
GO = (0, 1024, 1792, 2048)


def reduce_kernel(
    g_in, g_qkv, g_out, g_ff, cols_out, ff_out,
    recv0, recv1, recv2, recv3, red, redf, s0, r0, s1, r1, s2, r2, ls
):
    me = lax.axis_index("ctx")
    shard = lax.axis_index("shard")
    owner = lax.div(me, 8)
    barrier = pltpu.get_barrier_semaphore()
    signal_ctx_peers(barrier, me)

    def greet(k, carry):
        source_c = shard * 8 + lax.div(k, 3)
        source_s = lax.rem(shard + 1 + lax.rem(k, 3), 4)
        pl.semaphore_signal(
            barrier, inc=1, device_id={"ctx": source_c, "shard": source_s}, device_id_type=MESH
        )
        return carry

    lax.fori_loop(0, 24, greet, 0)
    pl.semaphore_wait(barrier, jnp.where(owner == shard, NC - 1, 2 * NC - 1))

    pieces = tuple(zip((g_in, g_qkv, g_out, g_ff), (recv0, recv1, recv2, recv3)))

    def rows_of(index, count=32):
        return pl.ds(pl.multiple_of(index * 32, 32), count)

    for n, (src, recv) in enumerate(pieces):

        def send(k, carry):
            dest = lax.rem(me + k, NC)
            pltpu.make_async_remote_copy(
                src_ref=src.at[rows_of(dest)], dst_ref=recv.at[me],
                send_sem=s0.at[n, k], recv_sem=r0.at[n, k],
                device_id={"ctx": dest}, device_id_type=MESH,
            ).start()
            return carry

        lax.fori_loop(1, NC, send, 0)
        pltpu.make_async_copy(src.at[rows_of(me)], recv.at[me], ls.at[n]).start()

    for n, (src, recv) in enumerate(pieces):
        pltpu.make_async_copy(src.at[rows_of(me)], recv.at[me], ls.at[n]).wait()

        def arrive(k, carry):
            source = lax.rem(me + NC - k, NC)
            copy = pltpu.make_async_remote_copy(
                src_ref=src.at[rows_of(source)], dst_ref=recv.at[source],
                send_sem=s0.at[n, k], recv_sem=r0.at[n, k],
                device_id={"ctx": source}, device_id_type=MESH,
            )
            copy.wait_send()
            copy.wait_recv()
            return carry

        lax.fori_loop(1, NC, arrive, 0)
        total = lax.fori_loop(
            0, NC, lambda k, acc: acc + recv[k].astype(jnp.float32),
            jnp.zeros((32, GW[n]), jnp.float32),
        )
        if n < 3:
            red[:, GO[n] : GO[n] + GW[n]] = total.astype(jnp.bfloat16)
        else:
            redf[...] = total.astype(jnp.bfloat16)
        if n == 2:
            place = cols_out.at[
                rows_of(lax.rem(me, 8)), pl.ds(pl.multiple_of(shard * 2048, 2048), 2048)
            ]
            index = lax.rem(me, 8) * 4 + shard

            def spread(k, carry):
                dest = lax.rem(me + k, NC)

                @pl.when(jnp.logical_or(k > 0, owner != shard))
                def _():
                    pltpu.make_async_remote_copy(
                        src_ref=red, dst_ref=place, send_sem=s1.at[k], recv_sem=r1.at[index],
                        device_id={"ctx": dest, "shard": owner}, device_id_type=MESH,
                    ).start()

                return carry

            lax.fori_loop(0, NC, spread, 0)

            @pl.when(owner == shard)
            def _():
                local = pltpu.make_async_copy(red, place, ls.at[4])
                local.start()
                local.wait()

    def spread_ff(k, carry):
        dest = lax.rem(me + k, NC)
        pltpu.make_async_remote_copy(
            src_ref=redf, dst_ref=ff_out.at[rows_of(me)], send_sem=s2.at[k], recv_sem=r2.at[k],
            device_id={"ctx": dest}, device_id_type=MESH,
        ).start()
        return carry

    lax.fori_loop(1, NC, spread_ff, 0)
    local = pltpu.make_async_copy(redf, ff_out.at[rows_of(me)], ls.at[5])
    local.start()
    local.wait()

    def finish(k, carry):
        source = lax.rem(me + NC - k, NC)
        copy = pltpu.make_async_remote_copy(
            src_ref=redf, dst_ref=ff_out.at[rows_of(source)], send_sem=s2.at[k], recv_sem=r2.at[k],
            device_id={"ctx": source}, device_id_type=MESH,
        )
        copy.wait_send()
        copy.wait_recv()
        return carry

    lax.fori_loop(1, NC, finish, 0)

    def finish_cols(k, carry):
        source_c = shard * 8 + lax.div(k, 4)
        source_s = lax.rem(k, 4)
        copy = pltpu.make_async_remote_copy(
            src_ref=red,
            dst_ref=cols_out.at[
                rows_of(lax.div(k, 4)), pl.ds(pl.multiple_of(source_s * 2048, 2048), 2048)
            ],
            send_sem=s1.at[k], recv_sem=r1.at[k],
            device_id={"ctx": source_c, "shard": source_s}, device_id_type=MESH,
        )

        @pl.when(jnp.logical_or(k > 0, owner != shard))
        def _():
            copy.wait_send()

        @pl.when(jnp.logical_or(source_c != me, source_s != shard))
        def _():
            copy.wait_recv()

        return carry

    lax.fori_loop(0, NC, finish_cols, 0)


def reduce_grads(g_in, g_qkv, g_out, g_ff):
    bf = jnp.bfloat16
    dma = pltpu.SemaphoreType.DMA
    return pl.pallas_call(
        reduce_kernel,
        out_shape=(
            jax.ShapeDtypeStruct((256, 4 * 2048), bf),
            jax.ShapeDtypeStruct((1024, 1024), bf),
        ),
        in_specs=[ANY] * 4,
        out_specs=(ANY, ANY),
        scratch_shapes=[pltpu.VMEM((NC, 32, w), bf) for w in GW]
        + [
            pltpu.VMEM((32, 2048), bf),
            pltpu.VMEM((32, 1024), bf),
            dma((4, NC)), dma((4, NC)), dma((NC,)), dma((NC,)), dma((NC,)), dma((NC,)), dma((6,)),
        ],
        compiler_params=pltpu.CompilerParams(
            collective_id=2, has_side_effects=True, vmem_limit_bytes=VMEM_LIMIT
        ),
    )(g_in, g_qkv, g_out, g_ff)


def local(
    inputs, cotangent, w_qkv, bias_qv, w_out, bias_out, ln1_gain, ln1_bias, w_in, bias_in,
    w_ff_out, bias_ff_out, ln2_gain, ln2_bias,
):
    bf, f32 = jnp.bfloat16, jnp.float32
    shard = lax.axis_index("shard")
    small = jnp.concatenate(
        [
            bias_qv.reshape(512), bias_out, ln1_gain, ln1_bias, bias_ff_out, ln2_gain, ln2_bias,
            bias_in,
        ]
    )
    small_all = lax.all_gather(small, "shard", axis=0).astype(f32)
    w_qkv_all = lax.all_gather(w_qkv, "shard", axis=0, tiled=True)
    w_out_all = lax.all_gather(w_out, "shard", axis=0, tiled=True)
    w_in_all = lax.all_gather(w_in, "shard", axis=0, tiled=True)
    w_ff_all = lax.all_gather(w_ff_out, "shard", axis=0, tiled=True)
    bias_q, bias_v, bias_o, gain_one, shift_one, bias_ff, gain_two, shift_two = (
        small_all[:, 256 * k : 256 * k + 256].reshape(D) for k in range(8)
    )
    bias_i = small_all[:, 2048:].reshape(FF)
    groups, rows_dev = inputs.shape[0], inputs.shape[1]
    token_count = groups * rows_dev
    tokens_in = inputs.reshape(token_count, D)
    bias_full = jnp.concatenate([bias_q, jnp.zeros((D,), f32), bias_v])
    projected = (jnp.dot(tokens_in, w_qkv_all, preferred_element_type=f32) + bias_full).astype(bf)
    flat_context, qkv, o, lse = attn_fwd(projected)
    attended = jnp.dot(flat_context, w_out_all, preferred_element_type=f32) + bias_o
    first_sum = tokens_in.astype(f32) + attended
    hidden = layer_norm(first_sum, gain_one, shift_one)
    hidden_low = hidden.astype(bf)
    pre_act = jnp.dot(hidden_low, w_in_all, preferred_element_type=f32) + bias_i
    act_low = gelu_exact(pre_act).astype(bf)
    branch = jnp.dot(act_low, w_ff_all, preferred_element_type=f32) + bias_ff
    second_sum = hidden + branch
    result_rows = layer_norm(second_sum, gain_two, shift_two)
    upstream = cotangent.reshape(token_count, D).astype(f32)
    unused_two, pull_two = jax.vjp(layer_norm, second_sum, gain_two, shift_two)
    d_second, d_gain_two, d_shift_two = pull_two(upstream)
    d_branch = d_second.astype(bf)
    grad_bias_ff = jnp.sum(d_branch.astype(f32), axis=0)
    d_act = times_transposed(d_branch, w_ff_all)
    unused_act, pull_gelu = jax.vjp(gelu_exact, pre_act)
    d_pre_act = pull_gelu(d_act)[0].astype(bf)
    grad_bias_in = jnp.sum(d_pre_act.astype(f32), axis=0)
    d_hidden = d_second + times_transposed(d_pre_act, w_in_all)
    unused_one, pull_one = jax.vjp(layer_norm, first_sum, gain_one, shift_one)
    d_first, d_gain_one, d_shift_one = pull_one(d_hidden)
    d_attended = d_first.astype(bf)
    grad_bias_out = jnp.sum(d_attended.astype(f32), axis=0)
    d_context = times_transposed(d_attended, w_out_all).astype(bf)
    sums = lax.psum(
        jnp.concatenate(
            [
                grad_bias_out, d_gain_one, d_shift_one, grad_bias_ff, d_gain_two, d_shift_two,
                grad_bias_in,
            ]
        ),
        ("ctx", "shard"),
    )
    d_projected, dproj_g, act_g, dpre_g, datt_g, hid_g, dbr_g, ctx_g, x_g = attn_bwd(
        d_context, qkv, o, lse, act_low, d_pre_act, d_attended, hidden_low, d_branch,
        flat_context, tokens_in,
    )
    column_sums = jnp.sum(d_projected.astype(f32), axis=0)
    sums_qv = lax.psum(
        jnp.concatenate([column_sums[:D], column_sums[2 * D :]]), ("ctx", "shard")
    )

    def flat(a):
        return a.reshape(512, a.shape[-1])

    g_in = outer_sum(flat(hid_g), flat(dpre_g)).astype(bf)
    g_ff = outer_sum(flat(act_g), flat(dbr_g)).astype(bf)
    g_out = outer_sum(flat(ctx_g), flat(datt_g)).astype(bf)
    g_qkv = outer_sum(flat(x_g), flat(dproj_g)).astype(bf)
    cols, own_ff = reduce_grads(g_in, g_qkv, g_out, g_ff)
    cols = cols.reshape(256, 4, 2048)
    own_in = cols[:, :, :1024].reshape(256, FF).astype(f32)
    own_qkv = cols[:, :, 1024:1792].reshape(256, 3 * D).astype(f32)
    own_out = cols[:, :, 1792:].reshape(256, D).astype(f32)
    d_inputs = d_first + times_transposed(d_projected, w_qkv_all)

    def own(k):
        return lax.dynamic_slice_in_dim(sums[k * D : (k + 1) * D], shard * 256, 256)

    own_bias_in = lax.dynamic_slice_in_dim(sums[6 * D :], shard * 1024, 1024)
    own_bias_qv = lax.dynamic_slice_in_dim(sums_qv.reshape(2, D), shard * 256, 256, 1)
    return (
        result_rows.astype(bf).reshape(groups, rows_dev, D),
        d_inputs.reshape(groups, rows_dev, D),
        own_qkv,
        own_bias_qv,
        own_out,
        own(0),
        own(1),
        own(2),
        own_in,
        own_bias_in,
        own_ff.astype(f32),
        own(3),
        own(4),
        own(5),
    )


def solution(mesh):
    specs = (
        P("shard", "ctx", None),
        P("shard", "ctx", None),
        P("shard", None),
        P(None, "shard"),
        P("shard", None),
        P("shard"),
        P("shard"),
        P("shard"),
        P("shard", None),
        P("shard"),
        P("shard", None),
        P("shard"),
        P("shard"),
        P("shard"),
    )
    return jax.shard_map(local, mesh=mesh, in_specs=specs, out_specs=specs, check_vma=False)
```

time: 1310 us -> 631 us (0.48)
  waiting for transfers between devices: 554 us -> 157 us
  Pallas kernels: 0 us -> 301 us
  local copies, waits for them, and re-layouts: 239 us -> 26.4 us
  blocking collectives: 285 us -> 80.1 us
  matrix products: 161 us -> 39.8 us
  other arithmetic: 42.3 us -> 11 us
    pallas_call x0 -> x3, Pallas kernels: none -> 301 us  [the longest x1 197 us: reduce_grads(): pl.pallas_call(reduce_kernel, out_shape=(jax.ShapeDtypeStruct((256, 4 * 2...]
    psum x1 -> x0, waiting for transfers between devices: 248 us -> none  [local(): lax.psum(own_qkv.astype(jnp.bfloat16), 'ctx').astype(jnp.float32)]
    all_gather x9 -> x1, blocking collectives: 194 us -> 6.69 us  [local(): small_all = lax.all_gather(small, 'shard', axis=0).astype(f32)]
    dot_general x32 -> x4, matrix products: 128 us -> 18.2 us  [the longest x1 6.33 us: local(): pre_act = jnp.dot(hidden_low, w_in_all, preferred_element_type=f32) + bias_i]
    all_gather x6 -> x4, waiting for transfers between devices: 241 us -> 154 us  [the longest x1 57 us: local(): w_ff_all = lax.all_gather(w_ff_out, 'shard', axis=0, tiled=True)]
    dynamic_slice x28 -> x8, local copies, waits for them, and re-layouts: 83.9 us -> 4.97 us  [the longest x6 3.8 us: own(): return lax.dynamic_slice_in_dim(sums[k * D:(k + 1) * D], shard * 256, 256)]
    reduce_scatter x3 -> x0, waiting for transfers between devices: 50.4 us -> none  [the longest x1 50.3 us: local(): lax.psum_scatter(grad_qkv.astype(jnp.bfloat16), 'shard', scatter_dimensio...]
    unnamed x97 -> x102, local copies, waits for them, and re-layouts: 61.6 us -> 13.6 us
  transfers between devices with their start and end apart: 11 -> 4, of which waited for: 6 -> 3; matrix products, arithmetic and copies ran while one was open for 31% -> 2% of each run, Pallas kernels for 0% -> 6%
where the time goes in v1:
time: 631 us; the launch traced here: 630 us
  Pallas kernels  301 us (48%)
  waiting for transfers between devices  157 us (25%)
  blocking collectives  80.1 us (13%)
  matrix products  39.8 us (6%)
  local copies, waits for them, and re-layouts  26.4 us (4%)
  between operations  14.4 us (2%)
  other arithmetic  11 us (2%)
    pallas_call x1, Pallas kernels, reduce_grads(): pl.pallas_call(reduce_kernel, out_shape=(jax.ShapeDtypeStruct((256, 4 * 2...  197 us
    psum x1, blocking collectives, local(): lax.psum(jnp.concatenate([column_sums[:D], column_sums[2 * D:]]), ('ctx',...  73.4 us
    pallas_call x1, Pallas kernels, attn_bwd(): pl.pallas_call(attn_bwd_kernel, out_shape=(sds((128, 3 * D), bf), sds((4,...  66.7 us
    all_gather x1, waiting for transfers between devices, local(): w_ff_all = lax.all_gather(w_ff_out, 'shard', axis=0, tiled=True)  57 us
    all_gather x1, waiting for transfers between devices, local(): w_in_all = lax.all_gather(w_in, 'shard', axis=0, tiled=True)  53.4 us
    all_gather x1, waiting for transfers between devices, local(): w_qkv_all = lax.all_gather(w_qkv, 'shard', axis=0, tiled=True)  44 us
    pallas_call x1, Pallas kernels, attn_fwd(): pl.pallas_call(attn_fwd_kernel, out_shape=(jax.ShapeDtypeStruct((128, D),...  36.8 us
    unnamed x102, local copies, waits for them, and re-layouts  13.6 us
  transfers between devices with their start and end apart: 4, of which 3 were waited for; matrix products, arithmetic and copies ran while one was open for 2% of the time, Pallas kernels for 6%

profile of v1, /device:TPU:0, one launch (start us, length us, event | category | flops | bytes accessed | tf_op | source)
XLA Modules:
  0.0 629.6 jit_solution(6233264184247955837)
XLA Ops:
  11.7 6.7 %all-gather = bf16[12288]{0:T(1024)(128)(2,1)S(1)} all-gather(bf16[3072]{0:T(1024)(128)(2,1)S(1)} %constant_dynamic-update-slice_fusion), channel_id=2, replica_groups=mesh['ctx'=32,'shard'=4] {'shard'}, dimensions={0}, use_global_device_ids=true | all-gather | bytes 30720 | tf_op jit(solution)/shard_map/all_gather | solution.py:532
  18.6 44.0 %all-gather.6.cloned.1.call-done = bf16[1024,3072]{1,0:T(8,128)(2,1)} async-done(((bf16[256,3072]{1,0:T(8,128)(2,1)}), bf16[1024,3072]{1,0:T(8,128)(2,1)}) %all-gather.6.cloned.1.call-update) | async-done | bytes 6291472 | tf_op jit(solution)/shard_map/all_gather | solution.py:533
  62.6 4.7 fusion.proj
  67.3 36.8 %shard_map.245 = (bf16[128,1024]{1,0:T(8,128)(2,1)}, bf16[32,96,128]{2,1,0:T(8,128)(2,1)}, f32[1024,128]{1,0:T(8,128)}, f32[4,1,512]{2,1,0:T(1,128)}) custom-call(bf16[128,3072]{1,0:T(8,128)(2,1)} %fusion.proj), custom_call_target="tpu_custom_call" | custom-call | tf_op jit(solution)/shard_map/pallas_call | solution.py:176
  104.2 2.2 fusion.15
  106.8 53.4 %all-gather.10.cloned.1.call-done = bf16[1024,4096]{1,0:T(8,128)(2,1)} async-done(((bf16[256,4096]{1,0:T(8,128)(2,1)}), bf16[1024,4096]{1,0:T(8,128)(2,1)}) %all-gather.10.cloned.1.call-update) | async-done | bytes 8388624 | tf_op jit(solution)/shard_map/all_gather | solution.py:535
  160.2 6.3 %multiply_convert_fusion = (bf16[128,4096]{1,0:T(8,128)(2,1)S(1)}, f32[128,4096]{1,0:T(8,128)}) fusion(f32[4096]{0:T(1024)S(1)} %bitcast.109, bf16[128,1024]{1,0:T(8,128)(2,1)S(1)} %fusion.8.hid, bf16[1024,4096]{1,0:T(8,128)(2,1)} %all-gather.10.cloned.1.call-done), kind=kOutput, calls=%fused_computation.9 | convolution fusion | flops 1076887552 | bytes 11812864 | tf_op jit(solution)/shard_map/dot_general | solution.py:551
  166.5 57.0 %all-gather.12.cloned.1.call-done = bf16[4096,1024]{1,0:T(8,128)(2,1)} async-done(((bf16[1024,1024]{1,0:T(8,128)(2,1)}), bf16[4096,1024]{1,0:T(8,128)(2,1)}) %all-gather.12.cloned.1.call-update) | async-done | bytes 8388624 | tf_op jit(solution)/shard_map/all_gather | solution.py:536
  223.5 4.9 fusion.16
  230.2 3.7 convert_reduce_fusion
  234.0 3.0 multiply_reduce_fusion
  240.4 66.7 %shard_map.246 = (bf16[128,3072]{1,0:T(8,128)(2,1)}, bf16[4,128,768]{2,1,0:T(8,128)(2,1)}, bf16[4,128,1024]{2,1,0:T(8,128)(2,1)}, bf16[4,128,1024]{2,1,0:T(8,128...) custom-call(bf16[128,1024]{1,0:T(8,128)(2,1)} %convolution_convert_f, ...), custom_call_target="tpu_custom_call" | custom-call | tf_op jit(solution)/shard_map/pallas_call | solution.py:324
  307.1 4.3 bitcast_convert_fusion.1.g_in
  311.4 2.2 bitcast_convert_fusion.2.g_qkv
  315.3 2.6 bitcast_convert_fusion.g_ff
  317.9 197.2 %shard_map.247 = (bf16[256,8192]{1,0:T(8,128)(2,1)}, bf16[1024,1024]{1,0:T(8,128)(2,1)}) custom-call(bf16[1024,1024]{1,0:T(8,128)(2,1)} %bitcast_convert_fusion.1.g_in, bf16[1024,768]{1,0:T(8,128)(2,1)} %bitcast_convert_fusion.2.g_qkv, bf16[1024,256]{1,0:T(8,128)(2,1)} %fusion.1.g_out, bf16[1024,1024]{1,0:T(8,128)(2,1)} %bitcast_convert_fusion.g_ff), custom_call_target="tpu_custom_call" | custom-call | tf_op jit(solution)/shard_map/pallas_call | solution.py:500
  515.1 7.8 %reshape.146 = bf16[256,4,2048]{2,1,0:T(4,128)(2,1)} reshape(bf16[256,8192]{1,0:T(8,128)(2,1)} %get-tuple-element.42) | data formatting | bytes 8388608 | tf_op jit(solution)/shard_map/reshape | solution.py:597
  522.9 2.0 slice_convert_fusion.1
  526.8 2.8 slice_convert_fusion
  529.8 73.4 %all-reduce = (f32[2,1024]{1,0:T(2,128)S(1)}, f32[10240]{0:T(1024)S(1)}) all-reduce(f32[2,1024]{1,0:T(2,128)S(1)} %reshape.147, f32[10240]{0:T(1024)S(1)} %constant_dynamic-update-slice_fusion.2), channel_id=1, replica_groups=mesh['ctx'=32,'shard'=4] {'ctx','shard'}, use_global_device_ids=true, to_apply=%region_9.0 | all-reduce | flops 12288 | bytes 98304 | tf_op jit(solution)/shard_map/psum | solution.py:585
  603.3 2.2 copy.50
  609.2 5.8 copy.52
  615.0 2.5 convert_element_type.111
  620.0 3.0 convolution_add_fusion.5
  (152 shorter events, 19.9 us)
Async XLA Ops:
  7.2 55.4 %all-gather.6.cloned.1.call-start = ((), (), s32[]{:S(2)}) async-start(), calls=%async_computation | async-start | bytes 7864320 | tf_op jit(solution)/shard_map/all_gather | solution.py:533
  7.9 96.2 %all-gather.8.cloned.1.call-start = ((), (), s32[]{:S(2)}) async-start(), calls=%async_computation.1 | async-start | bytes 2621440 | tf_op jit(solution)/shard_map/all_gather | solution.py:534
  8.7 2.9 copy-start.17
  8.7 9.8 %copy-start.13 = (bf16[2,64,1024]{2,1,0:T(8,128)(2,1)S(1)}, bf16[2,64,1024]{2,1,0:T(8,128)(2,1)}, u32[]{:S(2)}) copy-start(bf16[2,64,1024]{2,1,0:T(8,128)(2,1)} %param.15) | copy-start | bytes 786436
  8.8 53.9 %copy-start.8 = (bf16[2,64,1024]{2,1,0:T(8,128)(2,1)S(1)}, bf16[2,64,1024]{2,1,0:T(8,128)(2,1)}, u32[]{:S(2)}) copy-start(bf16[2,64,1024]{2,1,0:T(8,128)(2,1)} %param.14) | copy-start | bytes 786436
  8.8 151.4 %all-gather.10.cloned.1.call-start = ((), (), s32[]{:S(2)}) async-start(), calls=%async_computation.2 | async-start | bytes 10485760 | tf_op jit(solution)/shard_map/all_gather | solution.py:535
  9.5 214.0 %all-gather.12.cloned.1.call-start = ((), (), s32[]{:S(2)}) async-start(), calls=%async_computation.3 | async-start | bytes 10485760 | tf_op jit(solution)/shard_map/all_gather | solution.py:536
  106.8 59.7 %copy-start.9 = (bf16[128,1024]{1,0:T(8,128)(2,1)}, bf16[128,1024]{1,0:T(8,128)(2,1)S(1)}, u32[]{:S(2)}) copy-start(bf16[128,1024]{1,0:T(8,128)(2,1)S(1)} %fusion.8.hid) | copy-start | bytes 786436
  166.5 61.9 %copy-start.2 = (bf16[128,4096]{1,0:T(8,128)(2,1)}, bf16[128,4096]{1,0:T(8,128)(2,1)S(1)}, u32[]{:S(2)}) copy-start(bf16[128,4096]{1,0:T(8,128)(2,1)S(1)} %get-tuple-element.80.act) | copy-start | bytes 3145732
  223.5 6.6 %slice-start.4 = ((s8[8388608]{0:T(1024)(128)(4,1)}), s8[4194304]{0:T(1024)(128)(4,1)S(1)}, s32[]{:S(2)}) async-start(s8[8388608]{0:T(1024)(128)(4,1)} %bitcast.92), calls=%async_computation.8 | async-start | bytes 8388608
  223.5 6.6 %slice-start.5 = ((s8[8388608]{0:T(1024)(128)(4,1)}), s8[4194304]{0:T(1024)(128)(4,1)S(1)}, s32[]{:S(2)}) async-start(s8[8388608]{0:T(1024)(128)(4,1)} %bitcast.92), calls=%async_computation.9 | async-start | bytes 8388608
  229.9 4.0 slice-start
  230.1 3.8 copy-start.16
  230.2 3.7 slice-start.1
  233.9 3.1 copy-start.6
  307.1 4.3 copy-start.28
  307.1 4.3 copy-start.29
  526.8 2.8 copy-start.10
  603.3 5.9 copy-start.1
  605.5 14.5 %slice-start.2 = ((s8[6291456]{0:T(1024)(128)(4,1)}), s8[4194304]{0:T(1024)(128)(4,1)S(1)}, s32[]{:S(2)}) async-start(s8[6291456]{0:T(1024)(128)(4,1)} %bitcast.90), calls=%async_computation.6 | async-start | bytes 8388608
  609.2 5.8 copy-start.14
  609.2 10.8 %slice-start.3 = ((s8[6291456]{0:T(1024)(128)(4,1)}), s8[2097152]{0:T(1024)(128)(4,1)S(1)}, s32[]{:S(2)}) async-start(s8[6291456]{0:T(1024)(128)(4,1)} %bitcast.90), calls=%async_computation.7 | async-start | bytes 4194304
  615.0 5.0 copy-start.5
  615.0 5.0 copy-start.11
  (17 other events, 33.6 us)
Sparse Core Ops, SparseCore 0:
  9.7 52.8 all-gather.5
  64.3 35.9 all-gather.7
  101.9 58.2 all-gather.9
  161.7 61.7 all-gather.11

commit v2 on v1

v2 whole, which is shorter than its diff:
```python
import functools

import jax
import jax.numpy as jnp
from jax import lax
from jax.experimental import pallas as pl
from jax.experimental.pallas import tpu as pltpu
from jax.sharding import PartitionSpec as P

D = 1024
H = 16
DH = 64
FF = 4096
NC = 32
SCALE = DH ** (-0.5)
MESH = pl.DeviceIdType.MESH
NORM_EPS = 1e-05
VMEM_LIMIT = 56 * 1024 * 1024
VM = pl.BlockSpec(memory_space=pltpu.VMEM)
ANY = pl.BlockSpec(memory_space=pl.ANY)


def layer_norm(values, norm_gain, norm_shift):
    row_mean = jnp.mean(values, axis=-1, keepdims=True)
    centered = values - row_mean
    row_var = jnp.mean(centered * centered, axis=-1, keepdims=True)
    return centered * lax.rsqrt(row_var + NORM_EPS) * norm_gain + norm_shift


def gelu_exact(values):
    return 0.5 * values * (1.0 + lax.erf(values * 0.7071067811865476))


def outer_sum(left, right):
    return lax.dot_general(
        left, right, (((0,), (0,)), ((), ())), preferred_element_type=jnp.float32
    )


def times_transposed(left, right):
    return lax.dot_general(
        left, right, (((1,), (1,)), ((), ())), preferred_element_type=jnp.float32
    )


def pack_tokens(src, send, parts):
    def step(hp, carry):
        for g in range(2):
            for part in range(parts):
                cols = pl.ds(pl.multiple_of(part * D + hp * 128, 128), 128)
                a = src[pl.ds(g * 64, 32), cols]
                b = src[pl.ds(g * 64 + 32, 32), cols]
                rows = pl.ds(part * 32, 32)
                send[g * 16 + 2 * hp, rows, :] = jnp.concatenate([a[:, :64], b[:, :64]], axis=1)
                send[g * 16 + 2 * hp + 1, rows, :] = jnp.concatenate(
                    [a[:, 64:], b[:, 64:]], axis=1
                )
        return carry

    lax.fori_loop(0, H // 2, step, 0)


def unpack_tokens(recv, dst, parts):
    def step(hp, carry):
        for g in range(2):
            for part in range(parts):
                cols = pl.ds(pl.multiple_of(part * D + hp * 128, 128), 128)
                rows = pl.ds(part * 32, 32)
                even = recv[g * 16 + 2 * hp, rows, :]
                odd = recv[g * 16 + 2 * hp + 1, rows, :]
                dst[pl.ds(g * 64, 32), cols] = jnp.concatenate([even[:, :64], odd[:, :64]], axis=1)
                dst[pl.ds(g * 64 + 32, 32), cols] = jnp.concatenate(
                    [even[:, 64:], odd[:, 64:]], axis=1
                )
        return carry

    lax.fori_loop(0, H // 2, step, 0)


def a2a_start(send, recv, ssem, rsem, me):
    def step(k, carry):
        dest = lax.rem(me + k, NC)
        pltpu.make_async_remote_copy(
            src_ref=send.at[dest],
            dst_ref=recv.at[me],
            send_sem=ssem.at[k],
            recv_sem=rsem.at[k],
            device_id={"ctx": dest},
            device_id_type=MESH,
        ).start()
        return carry

    lax.fori_loop(1, NC, step, 0)


def a2a_wait(send, recv, ssem, rsem, me):
    def step(k, carry):
        source = lax.rem(me + NC - k, NC)
        copy = pltpu.make_async_remote_copy(
            src_ref=send.at[source],
            dst_ref=recv.at[source],
            send_sem=ssem.at[k],
            recv_sem=rsem.at[k],
            device_id={"ctx": source},
            device_id_type=MESH,
        )
        copy.wait_send()
        copy.wait_recv()
        return carry

    lax.fori_loop(1, NC, step, 0)


def signal_ctx_peers(barrier, me):
    def step(k, carry):
        pl.semaphore_signal(
            barrier, inc=1, device_id={"ctx": lax.rem(me + k, NC)}, device_id_type=MESH
        )
        return carry

    lax.fori_loop(1, NC, step, 0)


def halves(packed):
    return jnp.concatenate([packed[:, :64], packed[:, 64:]], axis=0)


def dot_nt(a, b):
    return lax.dot_general(a, b, (((1,), (1,)), ((), ())), preferred_element_type=jnp.float32)


def dot_nn(a, b):
    return jnp.dot(a, b, preferred_element_type=jnp.float32)


def place():
    c = lax.axis_index("ctx")
    return c, lax.axis_index("shard"), lax.div(c, 16), lax.rem(lax.div(c, 4), 4), lax.rem(c, 4)


def remote(src, dst, send_sem, recv_sem, peer):
    return pltpu.make_async_remote_copy(
        src_ref=src, dst_ref=dst, send_sem=send_sem, recv_sem=recv_sem,
        device_id=peer, device_id_type=MESH,
    )


def send(src, dst, send_sem, recv_sem, peer):
    copy = remote(src, dst, send_sem, recv_sem, peer)
    copy.start()
    return copy


def rings():
    c, unused_s, y, z, x = place()
    along_x = (
        x,
        {"ctx": c - x + lax.rem(x + 1, 4)},
        {"ctx": c - x + lax.rem(x + 3, 4)},
    )
    along_z = (
        z,
        {"ctx": y * 16 + lax.rem(z + 1, 4) * 4 + x},
        {"ctx": y * 16 + lax.rem(z + 3, 4) * 4 + x},
    )
    return along_x, along_z


class RingGather:
    def __init__(self, block, first, second, ring, ssem, rsem):
        self.block, self.first, self.second = block, first, second
        self.p, self.up, self.down = ring
        self.ssem, self.rsem = ssem, rsem

    def at(self, k):
        return lax.rem(self.p + k, 4)

    def start(self):
        own = self.block(self.p)
        self.sent = [
            send(own, own, self.ssem(0), self.rsem(0), self.up),
            send(own, own, self.ssem(1), self.rsem(1), self.down),
        ]

    def forward(self):
        from_down, from_up = self.block(self.at(3)), self.block(self.at(1))
        remote(from_down, from_down, self.ssem(0), self.rsem(0), self.up).wait_recv()
        part = self.first(self.at(3))
        self.sent.append(send(part, part, self.ssem(2), self.rsem(2), self.up))
        remote(from_up, from_up, self.ssem(1), self.rsem(1), self.down).wait_recv()
        part = self.second(self.at(1))
        self.sent.append(send(part, part, self.ssem(3), self.rsem(3), self.down))

    def finish(self):
        part = self.first(self.at(2))
        remote(part, part, self.ssem(2), self.rsem(2), self.up).wait_recv()
        part = self.second(self.at(2))
        remote(part, part, self.ssem(3), self.rsem(3), self.down).wait_recv()
        for copy in self.sent:
            copy.wait_send()


def sems(ref, *lead):
    return lambda k: ref.at[(*lead, k)]


def rows16(index):
    return pl.ds(pl.multiple_of(index * 16, 16), 16)


def rows64(index):
    return pl.ds(pl.multiple_of(index * 64, 64), 64)


class WeightGather:
    STEPS = 7

    def __init__(self, src, dst, n, ls, os, orr, cs, cr, gs, gr, fs, fr):
        c, s, y, z, x = place()
        sibling, cross, unused = group_ids()
        self.sibling, self.cross = mesh_id(sibling), mesh_id(cross)
        self.src, self.dst, self.s = src, dst, s
        self.far, self.far_sib = cross[1], unused[1]
        self.sib_shard = sibling[1]
        self.ls, self.os, self.orr = ls.at[n], os.at[n], orr.at[n]
        self.cs, self.cr, self.fs, self.fr = cs, cr, fs, fr
        self.n = n
        width = src.shape[-1]
        self.half, self.quarter = width // 2, width // 4
        along_x, along_z = rings()
        self.streams = []
        for h in range(2):
            one, two = (along_z, along_x) if h == 0 else (along_x, along_z)
            base = x if h == 0 else z
            cols = pl.ds(h * self.half, self.half)
            cols_a = pl.ds(h * self.half, self.quarter)
            cols_b = pl.ds(h * self.half + self.quarter, self.quarter)
            own = self.dst.at[self.far]

            def small_block(p, cols=cols, base=base, own=own):
                return own.at[:, rows16(base * 4 + p), cols]

            def big_block(p, cols=cols, own=own):
                return own.at[:, rows64(p), cols]

            def part_of(make, cols):
                return lambda p: make(p, cols=cols)

            ring1 = RingGather(
                small_block, part_of(small_block, cols_a), part_of(small_block, cols_b), one,
                sems(gs, n, h, 0), sems(gr, n, h, 0),
            )
            ring2 = RingGather(
                big_block, part_of(big_block, cols_a), part_of(big_block, cols_b), two,
                sems(gs, n, h, 1), sems(gr, n, h, 1),
            )
            row = base * 4 + one[0]
            self.streams.append((h, row, cols, cols_a, cols_b, ring1, ring2, two[0]))
        self.sent = []

    def step(self, k):
        if k == 0:
            for h, row, cols, *unused in self.streams:
                self.sent.append(
                    send(
                        self.src.at[:, rows16(row), cols],
                        self.dst.at[self.s].at[:, rows16(row), cols],
                        self.cs.at[self.n, h], self.cr.at[self.n, h], self.cross,
                    )
                )
            self.local = pltpu.make_async_copy(self.src, self.dst.at[self.s], self.ls)
            self.local.start()
            self.own = send(self.src, self.dst.at[self.s], self.os, self.orr, self.sibling)
        elif k == 1:
            for h, row, cols, cols_a, cols_b, ring1, ring2, p in self.streams:
                got = self.dst.at[self.far].at[:, rows16(row), cols]
                remote(got, got, self.cs.at[self.n, h], self.cr.at[self.n, h], self.cross).wait_recv()
                ring1.start()
        elif k == 2:
            for h, row, cols, cols_a, cols_b, ring1, ring2, p in self.streams:
                ring1.forward()
        elif k == 3:
            for h, row, cols, cols_a, cols_b, ring1, ring2, p in self.streams:
                ring1.finish()
                ring2.start()
                self.pass_on(h, 0, rows64(p), cols)
        elif k == 4:
            for h, row, cols, cols_a, cols_b, ring1, ring2, p in self.streams:
                ring2.forward()
                self.pass_on(h, 1, rows64(lax.rem(p + 3, 4)), cols)
                self.pass_on(h, 2, rows64(lax.rem(p + 1, 4)), cols)
        elif k == 5:
            for h, row, cols, cols_a, cols_b, ring1, ring2, p in self.streams:
                ring2.finish()
                self.pass_on(h, 3, rows64(lax.rem(p + 2, 4)), cols)
        else:
            self.local.wait()
            self.own.wait_send()
            got = self.dst.at[self.sib_shard]
            remote(got, got, self.os, self.orr, self.sibling).wait_recv()
            for h, row, cols, cols_a, cols_b, ring1, ring2, p in self.streams:
                for j, shift in enumerate((0, 3, 1, 2)):
                    got = self.dst.at[self.far_sib].at[:, rows64(lax.rem(p + shift, 4)), cols]
                    remote(
                        got, got, self.fs.at[self.n, h, j], self.fr.at[self.n, h, j], self.sibling
                    ).wait_recv()
            for copy in self.sent:
                copy.wait_send()

    def pass_on(self, h, j, rows, cols):
        part = self.dst.at[self.far].at[:, rows, cols]
        self.sent.append(
            send(part, part, self.fs.at[self.n, h, j], self.fr.at[self.n, h, j], self.sibling)
        )


def weight_sems(count):
    dma = pltpu.SemaphoreType.DMA
    return [
        dma((count,)), dma((count,)), dma((count,)), dma((count, 2)), dma((count, 2)),
        dma((count, 2, 2, 4)), dma((count, 2, 2, 4)), dma((count, 2, 4)), dma((count, 2, 4)),
    ]


def group_ids():
    c = lax.axis_index("ctx")
    s = lax.axis_index("shard")
    core = lax.rem(s, 2)
    other = 2 - 2 * lax.div(s, 2)
    sibling = s + 1 - 2 * core
    cross_c = lax.rem(c + NC // 2, NC)
    return ((c, sibling), (cross_c, other + core), (cross_c, other + 1 - core))


def mesh_id(pair):
    return {"ctx": pair[0], "shard": pair[1]}


def first_kernel(w, small, w_all, small_all, ls, os, orr, cs, cr, gs, gr, fs, fr, ss, sr, sl):
    unused_c, s, *unused = place()
    peers = [mesh_id(peer) for peer in group_ids()]
    around = [ring[k] for ring in rings() for k in (1, 2)]
    barrier = pltpu.get_barrier_semaphore()
    for peer in peers + around:
        pl.semaphore_signal(barrier, inc=1, device_id=peer, device_id_type=MESH)
    pl.semaphore_wait(barrier, len(peers) + len(around))
    gather = WeightGather(w, w_all, 0, ls, os, orr, cs, cr, gs, gr, fs, fr)
    gather.step(0)
    pending = [
        send(small, small_all.at[s], ss.at[k], sr.at[k], peer) for k, peer in enumerate(peers)
    ]
    own = pltpu.make_async_copy(small, small_all.at[s], sl)
    own.start()
    for k in range(1, WeightGather.STEPS):
        gather.step(k)
    own.wait()
    for k, peer in enumerate(group_ids()):
        pending[k].wait_send()
        got = small_all.at[peer[1]]
        remote(got, got, ss.at[k], sr.at[k], peers[k]).wait_recv()


def gather_first(w, small):
    dma = pltpu.SemaphoreType.DMA
    return pl.pallas_call(
        first_kernel,
        out_shape=(
            jax.ShapeDtypeStruct((4, *w.shape), w.dtype),
            jax.ShapeDtypeStruct((4, *small.shape), small.dtype),
        ),
        in_specs=[ANY, ANY],
        out_specs=(ANY, ANY),
        scratch_shapes=weight_sems(1) + [dma((3,)), dma((3,)), dma],
        compiler_params=pltpu.CompilerParams(collective_id=3, has_side_effects=True),
    )(w, small)


QB = 256


def attn_fwd_kernel(
    proj, w0, w1, w2, ctx_out, qkv_out, o_out, lse_out, all0, all1, all2,
    send, recv, send2, recv2, keys, vt, ssem, rsem, ssem2, rsem2, *wsems
):
    me = lax.axis_index("ctx")
    barrier = pltpu.get_barrier_semaphore()
    signal_ctx_peers(barrier, me)
    for peer in group_ids()[:2]:
        pl.semaphore_signal(barrier, inc=1, device_id=mesh_id(peer), device_id_type=MESH)
    pack_tokens(proj, send, 3)
    pl.semaphore_wait(barrier, NC + 1)
    a2a_start(send, recv, ssem, rsem, me)
    gathers = [
        WeightGather(w, out, n, *wsems)
        for n, (w, out) in enumerate(((w0, all0), (w1, all1), (w2, all2)))
    ]

    def advance(k):
        for gather in gathers:
            gather.step(k)

    advance(0)
    recv[me] = send[me]
    a2a_wait(send, recv, ssem, rsem, me)
    qkv_out[...] = recv[...]
    keys[...] = halves(recv[:, 32:64, :].reshape(1024, 128))
    vp = recv[:, 64:96, :].reshape(1024, 128).astype(jnp.float32).T.astype(jnp.bfloat16)
    vt[...] = jnp.concatenate([vp[:64], vp[64:]], axis=1)
    advance(1)

    def step(i, carry):
        qp = recv[pl.ds(i * 8, 8), 0:32, :].reshape(QB, 128) * jnp.bfloat16(SCALE)
        s = dot_nt(keys[...], halves(qp))
        m = jnp.max(s, axis=0, keepdims=True)
        p = jnp.exp(s - m)
        total = jnp.sum(p, axis=0, keepdims=True)
        ot = dot_nn(vt[...], p.astype(jnp.bfloat16)) / total
        o = jnp.concatenate([ot[:, :QB], ot[:, QB:]], axis=0).T
        o_out[pl.ds(pl.multiple_of(i * QB, QB), QB), :] = o
        lse_out[i] = m + jnp.log(total)
        send2[pl.ds(i * 8, 8)] = o.astype(jnp.bfloat16).reshape(8, 32, 128)
        return carry

    lax.fori_loop(0, 1, step, 0)
    advance(2)
    lax.fori_loop(1, 2, step, 0)
    advance(3)
    lax.fori_loop(2, 4, step, 0)
    a2a_start(send2, recv2, ssem2, rsem2, me)
    recv2[me] = send2[me]
    advance(4)
    a2a_wait(send2, recv2, ssem2, rsem2, me)
    unpack_tokens(recv2, ctx_out, 1)
    advance(5)
    advance(6)


def attn_fwd(projected, w_out, w_in, w_ff):
    return pl.pallas_call(
        attn_fwd_kernel,
        out_shape=(
            jax.ShapeDtypeStruct((128, D), jnp.bfloat16),
            jax.ShapeDtypeStruct((NC, 96, 128), jnp.bfloat16),
            jax.ShapeDtypeStruct((1024, 128), jnp.float32),
            jax.ShapeDtypeStruct((4, 1, 2 * QB), jnp.float32),
        )
        + tuple(jax.ShapeDtypeStruct((4, *w.shape), w.dtype) for w in (w_out, w_in, w_ff)),
        in_specs=[VM, ANY, ANY, ANY],
        out_specs=(VM, VM, VM, VM, ANY, ANY, ANY),
        scratch_shapes=[
            pltpu.VMEM((NC, 96, 128), jnp.bfloat16),
            pltpu.VMEM((NC, 96, 128), jnp.bfloat16),
            pltpu.VMEM((NC, 32, 128), jnp.bfloat16),
            pltpu.VMEM((NC, 32, 128), jnp.bfloat16),
            pltpu.VMEM((2048, DH), jnp.bfloat16),
            pltpu.VMEM((DH, 2048), jnp.bfloat16),
            pltpu.SemaphoreType.DMA((NC,)),
            pltpu.SemaphoreType.DMA((NC,)),
            pltpu.SemaphoreType.DMA((NC,)),
            pltpu.SemaphoreType.DMA((NC,)),
        ]
        + weight_sems(3),
        compiler_params=pltpu.CompilerParams(
            collective_id=0, has_side_effects=True, vmem_limit_bytes=VMEM_LIMIT
        ),
    )(projected, w_out, w_in, w_ff)


def attn_bwd_kernel(
    dctx, qkv, o_in, lse_in, small_in, act, dpre, datt, hid, dbr, ctx, xin,
    dproj_out, dproj_g, act_g, dpre_g, datt_g, hid_g, dbr_g, ctx_g, x_g, small_g,
    send, recv, send2, recv2, keys, kt, vals, dk, dv, dproj, small,
    ssem, rsem, ssem2, rsem2, xs, xr, fs, fr, ls, ps, pr, pls,
):
    me = lax.axis_index("ctx")
    shard = lax.axis_index("shard")
    peers = group_ids()
    barrier = pltpu.get_barrier_semaphore()
    signal_ctx_peers(barrier, me)
    for peer in peers:
        pl.semaphore_signal(barrier, inc=1, device_id=mesh_id(peer), device_id_type=MESH)
    pack_tokens(dctx, send, 1)
    pl.semaphore_wait(barrier, NC + 2)
    a2a_start(send, recv, ssem, rsem, me)

    def to_peer(src, dst, ssem_, rsem_, peer):
        copy = remote(src, dst, ssem_, rsem_, mesh_id(peer))
        copy.start()
        return copy

    slices = ((act, act_g, 1024), (dpre, dpre_g, 1024), (datt, datt_g, 256))
    whole = ((hid, hid_g), (dbr, dbr_g), (ctx, ctx_g), (xin, x_g))
    pending, arriving = [], []
    for n, (src, dst) in enumerate(whole):
        pending.append(to_peer(src, dst.at[1], xs.at[n, 0], xr.at[n, 0], peers[0]))
        arriving.append(to_peer(src, dst.at[2], xs.at[n, 1], xr.at[n, 1], peers[1]))
        local = pltpu.make_async_copy(src, dst.at[0], ls.at[n])
        local.start()
        pending.append(local)
    for n, (src, dst, width) in enumerate(slices):
        for k, peer in enumerate(peers):
            cols = pl.ds(pl.multiple_of(peer[1] * width, width), width)
            pending.append(
                to_peer(src.at[:, cols], dst.at[k + 1], xs.at[4 + n, k], xr.at[4 + n, k], peer)
            )
        cols = pl.ds(pl.multiple_of(shard * width, width), width)
        local = pltpu.make_async_copy(src.at[:, cols], dst.at[0], ls.at[4 + n])
        local.start()
        pending.append(local)

    recv[me] = send[me]
    keys[...] = halves(qkv[:, 32:64, :].reshape(1024, 128))
    vals[...] = halves(qkv[:, 64:96, :].reshape(1024, 128))
    kp = qkv[:, 32:64, :].reshape(1024, 128).astype(jnp.float32).T.astype(jnp.bfloat16)
    kt[...] = jnp.concatenate([kp[:64], kp[64:]], axis=1)
    dk[...] = jnp.zeros_like(dk)
    dv[...] = jnp.zeros_like(dv)
    a2a_wait(send, recv, ssem, rsem, me)

    def step(i, carry):
        blocks = pl.ds(i * 8, 8)
        qb = halves(qkv[blocks, 0:32, :].reshape(QB, 128) * jnp.bfloat16(SCALE))
        dop = recv[blocks].reshape(QB, 128)
        o = o_in[pl.ds(pl.multiple_of(i * QB, QB), QB), :]
        prod = (dop.astype(jnp.float32) * o).T
        delta = jnp.concatenate(
            [
                jnp.sum(prod[:64], axis=0, keepdims=True),
                jnp.sum(prod[64:], axis=0, keepdims=True),
            ],
            axis=1,
        )
        dob = halves(dop)
        probs = jnp.exp(dot_nt(keys[...], qb) - lse_in[i])
        dv[...] += dot_nn(probs.astype(jnp.bfloat16), dob)
        ds = (probs * (dot_nt(vals[...], dob) - delta)).astype(jnp.bfloat16)
        dk[...] += dot_nn(ds, qb)
        dqt = dot_nn(kt[...], ds) * SCALE
        dq = jnp.concatenate([dqt[:, :QB], dqt[:, QB:]], axis=0).T
        send2[blocks, 0:32, :] = dq.astype(jnp.bfloat16).reshape(8, 32, 128)
        return carry

    lax.fori_loop(0, 4, step, 0)
    for n, total in enumerate((dk, dv)):
        packed = jnp.concatenate([total[0:1024, :], total[1024:2048, :]], axis=1)
        send2[:, 32 + 32 * n : 64 + 32 * n, :] = packed.astype(jnp.bfloat16).reshape(NC, 32, 128)
    a2a_start(send2, recv2, ssem2, rsem2, me)
    recv2[me] = send2[me]
    for n, (src, dst) in enumerate(whole):
        arriving[n].wait()
        pending.append(to_peer(dst.at[2], dst.at[3], fs.at[n], fr.at[n], peers[0]))
    a2a_wait(send2, recv2, ssem2, rsem2, me)
    unpack_tokens(recv2, dproj, 3)
    for k, peer in enumerate(peers):
        cols = pl.ds(pl.multiple_of(peer[1] * 768, 256), 768)
        pending.append(to_peer(dproj.at[:, cols], dproj_g.at[k + 1], ps.at[k], pr.at[k], peer))
    cols = pl.ds(pl.multiple_of(shard * 768, 256), 768)
    small[...] = small_in[...]
    for n, part in enumerate((0, 2 * D)):
        sums = jnp.sum(dproj[:, part : part + D].astype(jnp.float32), axis=0, keepdims=True)
        for j in range(8):
            row = 20 + 2 * n + j % 2
            small[j // 2, row : row + 1, :] = sums[:, 128 * j : 128 * j + 128]
    for k, peer in enumerate(peers):
        pending.append(
            to_peer(small.at[peer[1]], small_g.at[k + 1], ps.at[3 + k], pr.at[3 + k], peer)
        )
    local = pltpu.make_async_copy(small.at[shard], small_g.at[0], pls.at[2])
    local.start()
    pending.append(local)
    local = pltpu.make_async_copy(dproj.at[:, cols], dproj_g.at[0], pls.at[0])
    local.start()
    pending.append(local)
    local = pltpu.make_async_copy(dproj, dproj_out, pls.at[1])
    local.start()
    pending.append(local)
    for copy in pending:
        copy.wait()


def attn_bwd(dctx, qkv, o, lse, small, act, dpre, datt, hid, dbr, ctx, xin):
    bf = jnp.bfloat16
    sds = jax.ShapeDtypeStruct
    dma = pltpu.SemaphoreType.DMA
    return pl.pallas_call(
        attn_bwd_kernel,
        out_shape=(
            sds((128, 3 * D), bf), sds((4, 128, 768), bf), sds((4, 128, 1024), bf),
            sds((4, 128, 1024), bf), sds((4, 128, 256), bf), sds((4, 128, 1024), bf),
            sds((4, 128, 1024), bf), sds((4, 128, 1024), bf), sds((4, 128, 1024), bf),
            sds((4, 24, 128), jnp.float32),
        ),
        in_specs=[VM] * 5 + [ANY] * 7,
        out_specs=(ANY,) * 10,
        scratch_shapes=[
            pltpu.VMEM((NC, 32, 128), bf),
            pltpu.VMEM((NC, 32, 128), bf),
            pltpu.VMEM((NC, 96, 128), bf),
            pltpu.VMEM((NC, 96, 128), bf),
            pltpu.VMEM((2048, DH), bf),
            pltpu.VMEM((DH, 2048), bf),
            pltpu.VMEM((2048, DH), bf),
            pltpu.VMEM((2048, DH), jnp.float32),
            pltpu.VMEM((2048, DH), jnp.float32),
            pltpu.VMEM((128, 3 * D), bf),
            pltpu.VMEM((4, 24, 128), jnp.float32),
            dma((NC,)), dma((NC,)), dma((NC,)), dma((NC,)),
            dma((7, 3)), dma((7, 3)), dma((4,)), dma((4,)), dma((7,)),
            dma((6,)), dma((6,)), dma((3,)),
        ],
        compiler_params=pltpu.CompilerParams(
            collective_id=1, has_side_effects=True, vmem_limit_bytes=VMEM_LIMIT
        ),
    )(dctx, qkv, o, lse, small, act, dpre, datt, hid, dbr, ctx, xin)


def widen(a):
    return a.astype(jnp.float32)


class RingReduce:
    def __init__(self, part, total, bufs, ring, ssem, rsem):
        self.part, self.total, self.bufs = part, total, bufs
        self.p, self.up, self.down = ring
        self.ssem, self.rsem = ssem, rsem

    def at(self, k):
        return lax.rem(self.p + k, 4)

    def start(self):
        ra, rb, sa, sb, from_down, from_up = self.bufs
        part, at, ssem, rsem = self.part, self.at, self.ssem, self.rsem
        up, down = self.up, self.down
        self.sent = [
            send(part(at(2), 0), ra, ssem(0), rsem(0), up),
            send(part(at(2), 1), rb, ssem(1), rsem(1), down),
            send(part(at(1), 1), from_down.at[2:4], ssem(2), rsem(2), up),
            send(part(at(3), 0), from_up.at[0:2], ssem(3), rsem(3), down),
        ]

    def middle(self):
        ra, rb, sa, sb, from_down, from_up = self.bufs
        part, at, ssem, rsem = self.part, self.at, self.ssem, self.rsem
        up, down = self.up, self.down
        self.sent[0].wait_recv()
        sa[...] = (widen(part(at(1), 0)[...]) + widen(ra[...])).astype(jnp.bfloat16)
        self.sent.append(send(sa, from_down.at[0:2], ssem(4), rsem(4), up))
        self.sent[1].wait_recv()
        sb[...] = (widen(part(at(3), 1)[...]) + widen(rb[...])).astype(jnp.bfloat16)
        self.sent.append(send(sb, from_up.at[2:4], ssem(5), rsem(5), down))

    def finish(self):
        from_down, from_up = self.bufs[4:]
        for copy in self.sent[2:]:
            copy.wait_recv()
        for k in range(2):
            half = pl.ds(2 * k, 2)
            self.total[half] = (
                widen(self.part(self.p, k)[...]) + widen(from_down[half]) + widen(from_up[half])
            ).astype(jnp.bfloat16)
        for copy in self.sent:
            copy.wait_send()


class Stream:
    STEPS = 12

    def __init__(self, grad, out, m, h, scratch, dsems):
        (big, t1, small, t2, ybuf, u, v) = scratch
        (p1s, p1r, p2s, p2r, ys, yr, ts, tr, ms, as_, ar, g1s, g1r, g2s, g2r) = dsems
        c, s, y, z, x = place()
        along_x, along_z = rings()
        one, two = (along_x, along_z) if h == 0 else (along_z, along_x)
        n = 2 * m + h
        self.m, self.c, self.s, self.y = m, c, s, y
        self.pair = {"ctx": lax.rem(c + 16, 32)}
        self.t1, self.t2, self.u, self.v = t1.at[n], t2.at[n], u.at[n], v.at[n]
        self.ybuf = ybuf.at[n]
        self.out = out
        self.ys, self.yr, self.ts, self.tr = ys.at[n], yr.at[n], ts.at[n], tr.at[n]
        self.ms, self.as_, self.ar = ms.at[n], as_.at[n], ar.at[n]
        cols = pl.ds(h * 512, 512)
        self.reduce1 = RingReduce(
            lambda p, k: grad.at[pl.ds(2 * k, 2), rows64(p), cols], self.t1,
            [b.at[n] for b in big], one, sems(p1s, n), sems(p1r, n),
        )
        self.reduce2 = RingReduce(
            lambda p, k: self.t1.at[pl.ds(2 * k, 2), rows16(p)], self.t2,
            [b.at[n] for b in small], two, sems(p2s, n), sems(p2r, n),
        )
        row = one[0] * 4 + two[0]

        def mine(who):
            at = pl.multiple_of(h * 512 + who * 256, 256)
            return out.at[:, rows16(row), pl.ds(at, 256)]

        self.mine = mine

        def small_block(p, lead=pl.ds(0, 4)):
            return out.at[lead, rows16(one[0] * 4 + p), cols]

        def big_block(p, lead=pl.ds(0, 4)):
            return out.at[lead, rows64(p), cols]

        def half_of(make, k):
            return lambda p: make(p, lead=pl.ds(2 * k, 2))

        self.gather1 = RingGather(
            small_block, half_of(small_block, 0), half_of(small_block, 1), two,
            sems(g1s, n), sems(g1r, n),
        )
        self.gather2 = RingGather(
            big_block, half_of(big_block, 0), half_of(big_block, 1), one,
            sems(g2s, n), sems(g2r, n),
        )

    def step(self, k):
        if k == 0:
            self.reduce1.start()
        elif k == 1:
            self.reduce1.middle()
        elif k == 2:
            self.reduce1.finish()
            self.reduce2.start()
        elif k == 3:
            self.reduce2.middle()
        elif k == 4:
            self.reduce2.finish()
            other = pl.ds(pl.multiple_of(256 - self.y * 256, 256), 256)
            self.sent_y = send(self.t2.at[:, :, other], self.ybuf, self.ys, self.yr, self.pair)
        elif k == 5:
            self.sent_y.wait()
            own = pl.ds(pl.multiple_of(self.y * 256, 256), 256)
            total = (widen(self.t2[:, :, own]) + widen(self.ybuf[...])).astype(jnp.bfloat16)
            if self.m == 0:
                self.v[...] = total
            else:
                self.u[...] = total
                self.turned = []
                for j in range(1, 4):
                    owner = lax.rem(self.s + j, 4)
                    self.turned.append(
                        send(
                            self.u.at[owner], self.v.at[self.s], self.ts.at[j], self.tr.at[j],
                            {"shard": owner},
                        )
                    )
                self.v[self.s] = self.u[self.s]
        elif k == 6:
            if self.m > 0:
                for j in range(1, 4):
                    source = lax.rem(self.s + 4 - j, 4)
                    got = self.v.at[source]
                    remote(got, got, self.ts.at[j], self.tr.at[j], {"shard": source}).wait_recv()
                    self.turned[j - 1].wait_send()
            self.kept = pltpu.make_async_copy(self.v, self.mine(self.y), self.ms)
            self.kept.start()
            self.shared = send(self.v, self.mine(self.y), self.as_, self.ar, self.pair)
        elif k == 7:
            self.kept.wait()
            self.shared.wait_send()
            got = self.mine(1 - self.y)
            remote(got, got, self.as_, self.ar, self.pair).wait_recv()
            self.gather1.start()
        elif k == 8:
            self.gather1.forward()
        elif k == 9:
            self.gather1.finish()
            self.gather2.start()
        elif k == 10:
            self.gather2.forward()
        else:
            self.gather2.finish()


def reduce_kernel(
    act, dbr, hid, dpre, x, dproj, ctx, datt, small_g, ff_out, in_out, qo_out, small_out,
    grads, ra, rb, sa, sb, fd, fu, ra2, rb2, sa2, sb2, fd2, fu2, t1, t2, ybuf, u, v,
    small, small_all, small_s, small_r, *dsems
):
    c, s, *unused = place()
    barrier = pltpu.get_barrier_semaphore()
    signal_ctx_peers(barrier, c)
    for j in range(1, 4):
        pl.semaphore_signal(
            barrier, inc=1, device_id={"shard": lax.rem(s + j, 4)}, device_id_type=MESH
        )
    small[...] = small_g[0] + small_g[1] + small_g[2] + small_g[3]
    pl.semaphore_wait(barrier, NC + 2)
    scratch = ((ra, rb, sa, sb, fd, fu), t1, (ra2, rb2, sa2, sb2, fd2, fu2), t2, ybuf, u, v)
    streams = []
    products = (((act, dbr, 0),), ((hid, dpre, 0),), ((x, dproj, 0), (ctx, datt, 768)))
    for m, (terms, out) in enumerate(zip(products, (ff_out, in_out, qo_out))):
        for left, right, at in terms:
            width = right.shape[-1]

            def block(q, carry):
                part = left[:, :, pl.ds(pl.multiple_of(q * 256, 256), 256)].reshape(512, 256)
                grads[m, q, :, at : at + width] = lax.dot_general(
                    part, right[...].reshape(512, width), (((0,), (0,)), ((), ())),
                    preferred_element_type=jnp.float32,
                ).astype(jnp.bfloat16)
                return carry

            lax.fori_loop(0, 4, block, 0)
        for h in range(2):
            streams.append(Stream(grads.at[m], out, m, h, scratch, dsems))
            streams[-1].step(0)

    def spread(k, carry):
        dest = lax.rem(c + k, NC)
        remote(small, small_all.at[c], small_s.at[k], small_r.at[k], {"ctx": dest}).start()
        return carry

    lax.fori_loop(1, NC, spread, 0)
    for k in range(1, Stream.STEPS):
        for stream in streams:
            stream.step(k)

    def arrive(k, carry):
        source = lax.rem(c + NC - k, NC)
        copy = remote(small, small_all.at[source], small_s.at[k], small_r.at[k], {"ctx": source})
        copy.wait_send()
        copy.wait_recv()
        return carry

    lax.fori_loop(1, NC, arrive, 0)
    small_all[c] = small[...]
    small_out[...] = lax.fori_loop(
        0, NC, lambda k, acc: acc + small_all[k], jnp.zeros((24, 128), jnp.float32)
    )


def reduce_grads(act, dbr, hid, dpre, x, dproj, ctx, datt, small):
    bf, f32 = jnp.bfloat16, jnp.float32
    dma = pltpu.SemaphoreType.DMA
    vm = pltpu.VMEM
    full = jax.ShapeDtypeStruct((4, 256, 1024), bf)

    def ring_bufs(rows):
        return [vm((6, 2, rows, 512), bf)] * 4 + [vm((6, 4, rows, 512), bf)] * 2

    return pl.pallas_call(
        reduce_kernel,
        out_shape=(full, full, full, jax.ShapeDtypeStruct((24, 128), f32)),
        in_specs=[VM] * 9,
        out_specs=(ANY, ANY, ANY, VM),
        scratch_shapes=[vm((3, 4, 256, 1024), bf)]
        + ring_bufs(64)
        + ring_bufs(16)
        + [
            vm((6, 4, 64, 512), bf), vm((6, 4, 16, 512), bf), vm((6, 4, 16, 256), bf),
            vm((6, 4, 16, 256), bf), vm((6, 4, 16, 256), bf),
            vm((24, 128), f32), vm((NC, 24, 128), f32), dma((NC,)), dma((NC,)),
            dma((6, 6)), dma((6, 6)), dma((6, 6)), dma((6, 6)), dma((6,)), dma((6,)),
            dma((6, 4)), dma((6, 4)), dma((6,)), dma((6,)), dma((6,)),
            dma((6, 4)), dma((6, 4)), dma((6, 4)), dma((6, 4)),
        ],
        compiler_params=pltpu.CompilerParams(
            collective_id=2, has_side_effects=True, vmem_limit_bytes=VMEM_LIMIT
        ),
    )(act, dbr, hid, dpre, x, dproj, ctx, datt, small)


def widen_kernel(ff, in_, qo, ff_out, in_out, qkv_out, w_out):
    ff_out[...] = widen(ff[0])
    in_out[...] = widen(in_[0])
    qkv_out[...] = widen(qo[0, :, :768])
    w_out[...] = widen(qo[0, :, 768:])


def widen_grads(ff, in_, qo):
    sds = jax.ShapeDtypeStruct
    f32 = jnp.float32
    block = pl.BlockSpec((1, 256, 1024), lambda q: (q, 0, 0))
    return pl.pallas_call(
        widen_kernel,
        grid=(4,),
        out_shape=(
            sds((1024, 1024), f32), sds((256, 4096), f32), sds((256, 3072), f32),
            sds((256, 1024), f32),
        ),
        in_specs=[block] * 3,
        out_specs=(
            pl.BlockSpec((256, 1024), lambda q: (q, 0)),
            pl.BlockSpec((256, 1024), lambda q: (0, q)),
            pl.BlockSpec((256, 768), lambda q: (0, q)),
            pl.BlockSpec((256, 256), lambda q: (0, q)),
        ),
        compiler_params=pltpu.CompilerParams(vmem_limit_bytes=VMEM_LIMIT),
    )(ff, in_, qo)


def local(
    inputs, cotangent, w_qkv, bias_qv, w_out, bias_out, ln1_gain, ln1_bias, w_in, bias_in,
    w_ff_out, bias_ff_out, ln2_gain, ln2_bias,
):
    bf, f32 = jnp.bfloat16, jnp.float32
    small = jnp.concatenate(
        [
            bias_qv.reshape(512), bias_out, ln1_gain, ln1_bias, bias_ff_out, ln2_gain, ln2_bias,
            bias_in, jnp.zeros((1024,), bf),
        ]
    )
    w_qkv_all, small_all = gather_first(w_qkv.reshape(1, 256, 3 * D), small.reshape(32, 128))
    w_qkv_all = w_qkv_all.reshape(D, 3 * D)
    small_all = small_all.reshape(4, 4096).astype(f32)
    bias_q, bias_v, bias_o, gain_one, shift_one, bias_ff, gain_two, shift_two = (
        small_all[:, 256 * k : 256 * k + 256].reshape(D) for k in range(8)
    )
    bias_i = small_all[:, 2048:3072].reshape(FF)
    groups, rows_dev = inputs.shape[0], inputs.shape[1]
    token_count = groups * rows_dev
    tokens_in = inputs.reshape(token_count, D)
    bias_full = jnp.concatenate([bias_q, jnp.zeros((D,), f32), bias_v])
    projected = (jnp.dot(tokens_in, w_qkv_all, preferred_element_type=f32) + bias_full).astype(bf)
    flat_context, qkv, o, lse, w_out_all, w_in_all, w_ff_all = attn_fwd(
        projected, w_out.reshape(1, 256, D), w_in.reshape(1, 256, FF), w_ff_out.reshape(4, 256, D)
    )
    w_out_all = w_out_all.reshape(D, D)
    w_in_all = w_in_all.reshape(D, FF)
    w_ff_all = w_ff_all.reshape(FF, D)
    attended = jnp.dot(flat_context, w_out_all, preferred_element_type=f32) + bias_o
    first_sum = tokens_in.astype(f32) + attended
    hidden = layer_norm(first_sum, gain_one, shift_one)
    hidden_low = hidden.astype(bf)
    pre_act = jnp.dot(hidden_low, w_in_all, preferred_element_type=f32) + bias_i
    act_low = gelu_exact(pre_act).astype(bf)
    branch = jnp.dot(act_low, w_ff_all, preferred_element_type=f32) + bias_ff
    second_sum = hidden + branch
    result_rows = layer_norm(second_sum, gain_two, shift_two)
    upstream = cotangent.reshape(token_count, D).astype(f32)
    unused_two, pull_two = jax.vjp(layer_norm, second_sum, gain_two, shift_two)
    d_second, d_gain_two, d_shift_two = pull_two(upstream)
    d_branch = d_second.astype(bf)
    grad_bias_ff = jnp.sum(d_branch.astype(f32), axis=0)
    d_act = times_transposed(d_branch, w_ff_all)
    unused_act, pull_gelu = jax.vjp(gelu_exact, pre_act)
    d_pre_act = pull_gelu(d_act)[0].astype(bf)
    grad_bias_in = jnp.sum(d_pre_act.astype(f32), axis=0)
    d_hidden = d_second + times_transposed(d_pre_act, w_in_all)
    unused_one, pull_one = jax.vjp(layer_norm, first_sum, gain_one, shift_one)
    d_first, d_gain_one, d_shift_one = pull_one(d_hidden)
    d_attended = d_first.astype(bf)
    grad_bias_out = jnp.sum(d_attended.astype(f32), axis=0)
    d_context = times_transposed(d_attended, w_out_all).astype(bf)
    small_sums = jnp.concatenate(
        [
            a.reshape(4, -1)
            for a in (
                grad_bias_out, d_gain_one, d_shift_one, grad_bias_ff, d_gain_two, d_shift_two,
                grad_bias_in, jnp.zeros((2048,), f32),
            )
        ],
        axis=1,
    ).reshape(4, 24, 128)
    d_projected, dproj_g, act_g, dpre_g, datt_g, hid_g, dbr_g, ctx_g, x_g, small_g = attn_bwd(
        d_context, qkv, o, lse, small_sums, act_low, d_pre_act, d_attended, hidden_low, d_branch,
        flat_context, tokens_in,
    )
    red_ff, red_in, red_qo, sums = reduce_grads(
        act_g, dbr_g, hid_g, dpre_g, x_g, dproj_g, ctx_g, datt_g, small_g
    )
    own_ff, own_in, own_qkv, own_out = widen_grads(red_ff, red_in, red_qo)
    d_inputs = d_first + times_transposed(d_projected, w_qkv_all)
    sums = sums.reshape(3072)

    def own(k):
        return sums[256 * k : 256 * k + 256]

    own_bias_in = sums[1536:2560]
    own_bias_qv = sums[2560:].reshape(2, 256)
    return (
        result_rows.astype(bf).reshape(groups, rows_dev, D),
        d_inputs.reshape(groups, rows_dev, D),
        own_qkv,
        own_bias_qv,
        own_out,
        own(0),
        own(1),
        own(2),
        own_in,
        own_bias_in,
        own_ff,
        own(3),
        own(4),
        own(5),
    )


def solution(mesh):
    specs = (
        P("shard", "ctx", None),
        P("shard", "ctx", None),
        P("shard", None),
        P(None, "shard"),
        P("shard", None),
        P("shard"),
        P("shard"),
        P("shard"),
        P("shard", None),
        P("shard"),
        P("shard", None),
        P("shard"),
        P("shard"),
        P("shard"),
    )
    return jax.shard_map(local, mesh=mesh, in_specs=specs, out_specs=specs, check_vma=False)
```

time: 631 us -> 422 us (0.67)
  waiting for transfers between devices: 157 us -> 0 us
  blocking collectives: 80.1 us -> 0 us
  Pallas kernels: 301 us -> 378 us
  local copies, waits for them, and re-layouts: 26.4 us -> 12.3 us
  between operations: 14.4 us -> 1.06 us
  matrix products: 39.8 us -> 27.4 us
  other arithmetic: 11 us -> 3.19 us
    all_gather x4 -> x0, waiting for transfers between devices: 154 us -> none  [the longest x1 57 us: local(): w_ff_all = lax.all_gather(w_ff_out, 'shard', axis=0, tiled=True)]
    pallas_call x1, Pallas kernels: 36.8 us -> 155 us  [attn_fwd(): pl.pallas_call(attn_fwd_kernel, out_shape=(jax.ShapeDtypeStruct((128, D),...]
    psum x1 -> x0, blocking collectives: 73.4 us -> none  [local(): lax.psum(jnp.concatenate([column_sums[:D], column_sums[2 * D:]]), ('ctx',...]
    pallas_call x1 -> x3, Pallas kernels: 197 us -> 158 us  [the longest x1 96.5 us: reduce_grads(): pl.pallas_call(reduce_kernel, out_shape=(full, full, full, jax.ShapeDtype...]
    dot_general x4 -> x0, matrix products: 10.4 us -> none  [outer_sum(): lax.dot_general(left, right, (((0,), (0,)), ((), ())), preferred_element_...]
    convert_element_type x4 -> x0, other arithmetic: 8.4 us -> none  [the longest x1 2.78 us: local(): own_in = cols[:, :, :1024].reshape(256, FF).astype(f32)]
    reshape x2 -> x8, local copies, waits for them, and re-layouts: 7.83 us -> 0.65 us  [the longest x1 0.59 us: local(): own_bias_qv = sums[2560:].reshape(2, 256)]
    all_gather x1 -> x0, blocking collectives: 6.69 us -> none  [local(): small_all = lax.all_gather(small, 'shard', axis=0).astype(f32)]
  transfers between devices with their start and end apart: 4 -> 0, of which waited for: 3 -> 0; matrix products, arithmetic and copies ran while one was open for 2% -> 0% of each run, Pallas kernels for 6% -> 0%
where the time goes in v2:
time: 422 us
  Pallas kernels  378 us (90%)
  matrix products  27.4 us (6%)
  local copies, waits for them, and re-layouts  12.3 us (3%)
    pallas_call x1, Pallas kernels, attn_fwd(): pl.pallas_call(attn_fwd_kernel, out_shape=(jax.ShapeDtypeStruct((128, D),...  155 us
    pallas_call x1, Pallas kernels, reduce_grads(): pl.pallas_call(reduce_kernel, out_shape=(full, full, full, jax.ShapeDtype...  96.5 us
    pallas_call x1, Pallas kernels, attn_bwd(): pl.pallas_call(attn_bwd_kernel, out_shape=(sds((128, 3 * D), bf), sds((4,...  65.2 us
    pallas_call x1, Pallas kernels, gather_first(): pl.pallas_call(first_kernel, out_shape=(jax.ShapeDtypeStruct((4, *w.shape...  53.7 us
    dot_general x4, matrix products, times_transposed(): lax.dot_general(left, right, (((1,), (1,)), ((), ())), preferred_element_...  14.4 us
    unnamed x57, local copies, waits for them, and re-layouts  10.4 us

profile of v2, /device:TPU:0, one launch (start us, length us, event | category | flops | bytes accessed | tf_op | source)
XLA Modules:
  0.0 421.6 jit_solution(5165331900043551212)
XLA Ops:
  0.7 0.7 copy.30
  1.6 0.8 dynamic-update-slice.9
  2.4 0.8 dynamic-update-slice.10
  3.2 0.8 dynamic-update-slice.11
  4.1 0.8 dynamic-update-slice.12
  4.9 0.8 dynamic-update-slice.13
  5.7 0.8 dynamic-update-slice.14
  7.9 53.7 %shard_map.245 = (bf16[4,1,256,3072]{3,2,1,0:T(8,128)(2,1)}, bf16[4,32,128]{2,1,0:T(8,128)(2,1)}) custom-call(bf16[1,256,3072]{2,1,0:T(8,128)(2,1)} %bitcast.115, bf16[32,128]{1,0:T(8,128)(2,1)} %bitcast.137), custom_call_target="tpu_custom_call" | custom-call | tf_op jit(solution)/shard_map/pallas_call | solution.py:365
  61.6 0.8 convert_bitcast_fusion
  62.5 4.7 %fusion.1.proj = bf16[128,3072]{1,0:T(8,128)(2,1)} fusion(bf16[128,1024]{1,0:T(8,128)(2,1)S(1)} %bitcast.111, bf16[1024,3072]{1,0:T(8,128)(2,1)} %bitcast.102, f32[3072]{0:T(1024)S(1)} %pad_maximum_fusion), kind=kOutput, calls=%fused_computation.3 | convolution fusion | flops 806092800 | bytes 7352320 | tf_op jit(solution)/shard_map/dot_general | solution.py:916
  67.1 154.7 %shard_map.246 = (bf16[128,1024]{1,0:T(8,128)(2,1)}, bf16[32,96,128]{2,1,0:T(8,128)(2,1)}, f32[1024,128]{1,0:T(8,128)}, f32[4,1,512]{2,1,0:T(1,128)}, bf16[4,1,2...) custom-call(bf16[128,3072]{1,0:T(8,128)(2,1)} %fusion.1.proj, ...), custom_call_target="tpu_custom_call" | custom-call | tf_op jit(solution)/shard_map/pallas_call | solution.py:439
  221.9 2.2 fusion.13
  224.6 4.7 %multiply_convert_fusion = (bf16[128,4096]{1,0:T(8,128)(2,1)S(1)}, f32[128,4096]{1,0:T(8,128)S(1)}) fusion(f32[4096]{0:T(1024)S(1)} %bitcast.126, bf16[128,1024]{1,0:T(8,128)(2,1)S(1)} %fusion.8.hid, bf16[1024,4096]{1,0:T(8,128)(2,1)} %bitcast.98), kind=kOutput, calls=%fused_computation.6 | convolution fusion | flops 1076887552 | bytes 11812864 | tf_op jit(solution)/shard_map/dot_general | solution.py:927
  229.3 1.2 slice-done.3
  230.5 1.4 fusion.14
  232.5 1.0 fusion.12
  233.6 3.7 convert_reduce_fusion
  237.3 3.0 multiply_reduce_fusion
  240.8 1.3 copy-done.1
  242.1 1.6 convolution_convert_fusion.dctx
  244.5 65.2 %shard_map.247 = (bf16[128,3072]{1,0:T(8,128)(2,1)}, bf16[4,128,768]{2,1,0:T(8,128)(2,1)}, bf16[4,128,1024]{2,1,0:T(8,128)(2,1)}, bf16[4,128,1024]{2,1,0:T(8,128...) custom-call(bf16[128,1024]{1,0:T(8,128)(2,1)} %convolution_convert_f, ...), custom_call_target="tpu_custom_call" | custom-call | tf_op jit(solution)/shard_map/pallas_call | solution.py:585
  309.7 6.1 %convolution_add_fusion.5 = f32[128,1024]{1,0:T(8,128)} fusion(bf16[128,3072]{1,0:T(8,128)(2,1)} %get-tuple-element.50, bf16[1024,3072]{1,0:T(8,128)(2,1)} %bitcast.103, f32[128,1024]{1,0:T(8,128)S(1)} %get-tuple-element.80, f32[128]{0:T(128)S(1)} %negate_multiply_fusion), kind=kOutput, calls=%fused_computation.13 | convolution fusion | flops 805568512 | bytes 8126976 | tf_op jit(solution)/shard_map/dot_general | solution.py:41
  315.8 96.5 %shard_map.248 = (bf16[4,256,1024]{2,1,0:T(8,128)(2,1)}, bf16[4,256,1024]{2,1,0:T(8,128)(2,1)}, bf16[4,256,1024]{2,1,0:T(8,128)(2,1)}, f32[24,128]{1,0:T(8,128)}) custom-call(bf16[4,128,1024]{2,1,0:T(8,128)(2,1)} %get-tuple-element.51.act, bf16[4,128,1024]{2,1,0:T(8,128)(2,1)} %get-tuple-element.52.dbr, bf16[4,128,1024]{2,1,0:T(8,128)(2,1)} %get-tuple-element.53.hid, ...), custom_call_target="tpu_custom_call" | custom-call | tf_op jit(solution)/shard_map/pallas_call | solution.py:843
  412.3 7.5 %shard_map.249 = (f32[1024,1024]{1,0:T(8,128)}, f32[256,4096]{1,0:T(8,128)}, f32[256,3072]{1,0:T(8,128)}, f32[256,1024]{1,0:T(8,128)}) custom-call(bf16[4,256,1024]{2,1,0:T(8,128)(2,1)} %get-tuple-element.60.ff, bf16[4,256,1024]{2,1,0:T(8,128)(2,1)} %get-tuple-element.61.in_, bf16[4,256,1024]{2,1,0:T(8,128)(2,1)} %get-tuple-element.62.qo), custom_call_target="tpu_custom_call" | custom-call | tf_op jit(solution)/shard_map/pallas_call | solution.py:876
  (82 shorter events, 5.6 us)
Async XLA Ops:
  0.6 61.8 %copy-start.3 = (bf16[2,64,1024]{2,1,0:T(8,128)(2,1)S(1)}, bf16[2,64,1024]{2,1,0:T(8,128)(2,1)}, u32[]{:S(2)}) copy-start(bf16[2,64,1024]{2,1,0:T(8,128)(2,1)} %param.14) | copy-start | bytes 786436
  7.3 0.6 copy-start.9
  224.4 5.0 %slice-start.2 = ((s8[8388608]{0:T(1024)(128)(4,1)}), s8[4194304]{0:T(1024)(128)(4,1)S(1)}, s32[]{:S(2)}) async-start(s8[8388608]{0:T(1024)(128)(4,1)} %bitcast.104), calls=%async_computation.2 | async-start | bytes 8388608
  224.5 4.8 %copy-start.4 = (bf16[128,1024]{1,0:T(8,128)(2,1)}, bf16[128,1024]{1,0:T(8,128)(2,1)S(1)}, u32[]{:S(2)}) copy-start(bf16[128,1024]{1,0:T(8,128)(2,1)S(1)} %fusion.8.hid) | copy-start | bytes 786436
  224.6 6.0 %slice-start.3 = ((s8[8388608]{0:T(1024)(128)(4,1)}), s8[4194304]{0:T(1024)(128)(4,1)S(1)}, s32[]{:S(2)}) async-start(s8[8388608]{0:T(1024)(128)(4,1)} %bitcast.104), calls=%async_computation.3 | async-start | bytes 8388608
  229.3 2.6 copy-start
  230.5 1.6 copy-start.6
  233.4 3.9 slice-start
  233.6 3.7 copy-start.7
  233.6 3.7 slice-start.1
  237.3 3.1 copy-start.2
  240.4 1.7 copy-start.1
  240.8 3.7 copy-start.5
  412.3 7.5 %copy-start.8 = (f32[24,128]{1,0:T(8,128)S(1)}, f32[24,128]{1,0:T(8,128)}, u32[]{:S(2)}) copy-start(f32[24,128]{1,0:T(8,128)} %get-tuple-element.64) | copy-start | bytes 36868

commit v3 on v2

--- a/solution.py
+++ b/solution.py
@@ -368,10 +368,12 @@
             jax.ShapeDtypeStruct((4, *w.shape), w.dtype),
             jax.ShapeDtypeStruct((4, *small.shape), small.dtype),
         ),
-        in_specs=[ANY, ANY],
-        out_specs=(ANY, ANY),
+        in_specs=[ANY, VM],
+        out_specs=(VM, VM),
         scratch_shapes=weight_sems(1) + [dma((3,)), dma((3,)), dma],
-        compiler_params=pltpu.CompilerParams(collective_id=3, has_side_effects=True),
+        compiler_params=pltpu.CompilerParams(
+            collective_id=3, has_side_effects=True, vmem_limit_bytes=VMEM_LIMIT
+        ),
     )(w, small)
 
 
@@ -446,7 +448,7 @@
         )
         + tuple(jax.ShapeDtypeStruct((4, *w.shape), w.dtype) for w in (w_out, w_in, w_ff)),
         in_specs=[VM, ANY, ANY, ANY],
-        out_specs=(VM, VM, VM, VM, ANY, ANY, ANY),
+        out_specs=(VM,) * 7,
         scratch_shapes=[
             pltpu.VMEM((NC, 96, 128), jnp.bfloat16),
             pltpu.VMEM((NC, 96, 128), jnp.bfloat16),
@@ -591,7 +593,7 @@
             sds((4, 24, 128), jnp.float32),
         ),
         in_specs=[VM] * 5 + [ANY] * 7,
-        out_specs=(ANY,) * 10,
+        out_specs=(VM,) * 10,
         scratch_shapes=[
             pltpu.VMEM((NC, 32, 128), bf),
             pltpu.VMEM((NC, 32, 128), bf),
@@ -844,7 +846,7 @@
         reduce_kernel,
         out_shape=(full, full, full, jax.ShapeDtypeStruct((24, 128), f32)),
         in_specs=[VM] * 9,
-        out_specs=(ANY, ANY, ANY, VM),
+        out_specs=(VM,) * 4,
         scratch_shapes=[vm((3, 4, 256, 1024), bf)]
         + ring_bufs(64)
         + ring_bufs(16)

time: 422 us -> 312 us (0.74)
  Pallas kernels: 378 us -> 268 us
    pallas_call x1, Pallas kernels: 155 us -> 61 us  [attn_fwd(): pl.pallas_call(attn_fwd_kernel, out_shape=(jax.ShapeDtypeStruct((128, D),...]
    pallas_call x1, Pallas kernels: 53.7 us -> 32.9 us  [gather_first(): pl.pallas_call(first_kernel, out_shape=(jax.ShapeDtypeStruct((4, *w.shape...]
where the time goes in v3:
time: 312 us
  Pallas kernels  268 us (86%)
  matrix products  27.4 us (9%)
  local copies, waits for them, and re-layouts  12.3 us (4%)
  other arithmetic  3.19 us (1%)
    pallas_call x1, Pallas kernels, reduce_grads(): pl.pallas_call(reduce_kernel, out_shape=(full, full, full, jax.ShapeDtype...  97.5 us
    pallas_call x1, Pallas kernels, attn_bwd(): pl.pallas_call(attn_bwd_kernel, out_shape=(sds((128, 3 * D), bf), sds((4,...  69 us
    pallas_call x1, Pallas kernels, attn_fwd(): pl.pallas_call(attn_fwd_kernel, out_shape=(jax.ShapeDtypeStruct((128, D),...  61 us
    pallas_call x1, Pallas kernels, gather_first(): pl.pallas_call(first_kernel, out_shape=(jax.ShapeDtypeStruct((4, *w.shape...  32.9 us
    dot_general x4, matrix products, times_transposed(): lax.dot_general(left, right, (((1,), (1,)), ((), ())), preferred_element_...  14.4 us
    unnamed x57, local copies, waits for them, and re-layouts  10.4 us
    pallas_call x1, Pallas kernels, widen_grads(): pl.pallas_call(widen_kernel, grid=(4,), out_shape=(sds((1024, 1024), f32)...  7.52 us

profile of v3, /device:TPU:0, one launch (start us, length us, event | category | flops | bytes accessed | tf_op | source)
XLA Modules:
  0.0 311.7 jit_solution(4049438942975998427)
XLA Ops:
  0.7 0.7 copy.30
  1.6 0.8 dynamic-update-slice.9
  2.4 0.8 dynamic-update-slice.10
  3.2 0.8 dynamic-update-slice.11
  4.1 0.8 dynamic-update-slice.12
  4.9 0.8 dynamic-update-slice.13
  5.7 0.8 dynamic-update-slice.14
  7.9 32.9 %shard_map.245 = (bf16[4,1,256,3072]{3,2,1,0:T(8,128)(2,1)}, bf16[4,32,128]{2,1,0:T(8,128)(2,1)}) custom-call(bf16[1,256,3072]{2,1,0:T(8,128)(2,1)} %bitcast.115, bf16[32,128]{1,0:T(8,128)(2,1)} %bitcast.137), custom_call_target="tpu_custom_call" | custom-call | tf_op jit(solution)/shard_map/pallas_call | solution.py:365
  40.8 0.8 convert_bitcast_fusion
  41.7 4.7 %fusion.1.proj = bf16[128,3072]{1,0:T(8,128)(2,1)} fusion(bf16[128,1024]{1,0:T(8,128)(2,1)S(1)} %bitcast.111, bf16[1024,3072]{1,0:T(8,128)(2,1)} %bitcast.102, f32[3072]{0:T(1024)S(1)} %pad_maximum_fusion), kind=kOutput, calls=%fused_computation.3 | convolution fusion | flops 806092800 | bytes 7352320 | tf_op jit(solution)/shard_map/dot_general | solution.py:918
  46.3 61.0 %shard_map.246 = (bf16[128,1024]{1,0:T(8,128)(2,1)}, bf16[32,96,128]{2,1,0:T(8,128)(2,1)}, f32[1024,128]{1,0:T(8,128)}, f32[4,1,512]{2,1,0:T(1,128)}, bf16[4,1,2...) custom-call(bf16[128,3072]{1,0:T(8,128)(2,1)} %fusion.1.proj, ...), custom_call_target="tpu_custom_call" | custom-call | tf_op jit(solution)/shard_map/pallas_call | solution.py:441
  107.3 2.2 fusion.13
  110.0 4.7 %multiply_convert_fusion = (bf16[128,4096]{1,0:T(8,128)(2,1)S(1)}, f32[128,4096]{1,0:T(8,128)S(1)}) fusion(f32[4096]{0:T(1024)S(1)} %bitcast.126, bf16[128,1024]{1,0:T(8,128)(2,1)S(1)} %fusion.8.hid, bf16[1024,4096]{1,0:T(8,128)(2,1)} %bitcast.98), kind=kOutput, calls=%fused_computation.6 | convolution fusion | flops 1076887552 | bytes 11812864 | tf_op jit(solution)/shard_map/dot_general | solution.py:929
  114.8 1.1 slice-done.3
  115.9 1.4 fusion.14
  117.9 1.0 fusion.12
  119.0 3.7 %convert_reduce_fusion = (f32[4096]{0:T(1024)S(1)}, bf16[128,4096]{1,0:T(8,128)(2,1)S(1)}) fusion(f32[128,4096]{1,0:T(8,128)S(1)} %get-tuple-element.101, bf16[128,1024]{1,0:T(8,128)(2,1)S(1)} %get-tuple-element.76.dbr, bf16[4096,1024]{1,0:T(8,128)(2,1)S(1)} %bitcast.107), kind=kOutput, calls=%fused_computation.4 | convolution fusion | flops 1081602048 | bytes 11812864 | tf_op jit(solution)/shard_map/dot_general | solution.py:41
  122.7 3.0 multiply_reduce_fusion
  126.2 1.3 copy-done.1
  127.5 1.6 convolution_convert_fusion.dctx
  129.9 69.0 %shard_map.247 = (bf16[128,3072]{1,0:T(8,128)(2,1)}, bf16[4,128,768]{2,1,0:T(8,128)(2,1)}, bf16[4,128,1024]{2,1,0:T(8,128)(2,1)}, bf16[4,128,1024]{2,1,0:T(8,128...) custom-call(bf16[128,1024]{1,0:T(8,128)(2,1)} %convolution_convert_f, ...), custom_call_target="tpu_custom_call" | custom-call | tf_op jit(solution)/shard_map/pallas_call | solution.py:587
  198.8 6.1 %convolution_add_fusion.5 = f32[128,1024]{1,0:T(8,128)} fusion(bf16[128,3072]{1,0:T(8,128)(2,1)} %get-tuple-element.50, bf16[1024,3072]{1,0:T(8,128)(2,1)} %bitcast.103, f32[128,1024]{1,0:T(8,128)S(1)} %get-tuple-element.80, f32[128]{0:T(128)S(1)} %negate_multiply_fusion), kind=kOutput, calls=%fused_computation.13 | convolution fusion | flops 805568512 | bytes 8126976 | tf_op jit(solution)/shard_map/dot_general | solution.py:41
  204.9 97.5 %shard_map.248 = (bf16[4,256,1024]{2,1,0:T(8,128)(2,1)}, bf16[4,256,1024]{2,1,0:T(8,128)(2,1)}, bf16[4,256,1024]{2,1,0:T(8,128)(2,1)}, f32[24,128]{1,0:T(8,128)}) custom-call(bf16[4,128,1024]{2,1,0:T(8,128)(2,1)} %get-tuple-element.51.act, bf16[4,128,1024]{2,1,0:T(8,128)(2,1)} %get-tuple-element.52.dbr, bf16[4,128,1024]{2,1,0:T(8,128)(2,1)} %get-tuple-element.53.hid, ...), custom_call_target="tpu_custom_call" | custom-call | tf_op jit(solution)/shard_map/pallas_call | solution.py:845
  302.4 7.5 %shard_map.249 = (f32[1024,1024]{1,0:T(8,128)}, f32[256,4096]{1,0:T(8,128)}, f32[256,3072]{1,0:T(8,128)}, f32[256,1024]{1,0:T(8,128)}) custom-call(bf16[4,256,1024]{2,1,0:T(8,128)(2,1)} %get-tuple-element.60.ff, bf16[4,256,1024]{2,1,0:T(8,128)(2,1)} %get-tuple-element.61.in_, bf16[4,256,1024]{2,1,0:T(8,128)(2,1)} %get-tuple-element.62.qo), custom_call_target="tpu_custom_call" | custom-call | tf_op jit(solution)/shard_map/pallas_call | solution.py:878
  (82 shorter events, 5.6 us)
Async XLA Ops:
  0.6 41.0 %copy-start.3 = (bf16[2,64,1024]{2,1,0:T(8,128)(2,1)S(1)}, bf16[2,64,1024]{2,1,0:T(8,128)(2,1)}, u32[]{:S(2)}) copy-start(bf16[2,64,1024]{2,1,0:T(8,128)(2,1)} %param.14) | copy-start | bytes 786436
  7.3 0.6 copy-start.9
  109.8 5.0 %slice-start.2 = ((s8[8388608]{0:T(1024)(128)(4,1)}), s8[4194304]{0:T(1024)(128)(4,1)S(1)}, s32[]{:S(2)}) async-start(s8[8388608]{0:T(1024)(128)(4,1)} %bitcast.104), calls=%async_computation.2 | async-start | bytes 8388608
  110.0 4.8 %copy-start.4 = (bf16[128,1024]{1,0:T(8,128)(2,1)}, bf16[128,1024]{1,0:T(8,128)(2,1)S(1)}, u32[]{:S(2)}) copy-start(bf16[128,1024]{1,0:T(8,128)(2,1)S(1)} %fusion.8.hid) | copy-start | bytes 786436
  110.0 5.9 %slice-start.3 = ((s8[8388608]{0:T(1024)(128)(4,1)}), s8[4194304]{0:T(1024)(128)(4,1)S(1)}, s32[]{:S(2)}) async-start(s8[8388608]{0:T(1024)(128)(4,1)} %bitcast.104), calls=%async_computation.3 | async-start | bytes 8388608
  114.8 2.6 copy-start
  115.9 1.6 copy-start.6
  118.8 3.9 %slice-start = ((s8[8388608]{0:T(1024)(128)(4,1)}), s8[4194304]{0:T(1024)(128)(4,1)S(1)}, s32[]{:S(2)}) async-start(s8[8388608]{0:T(1024)(128)(4,1)} %bitcast.99), calls=%async_computation | async-start | bytes 8388608
  119.0 3.7 %copy-start.7 = (bf16[128,1024]{1,0:T(8,128)(2,1)}, bf16[128,1024]{1,0:T(8,128)(2,1)S(1)}, u32[]{:S(2)}) copy-start(bf16[128,1024]{1,0:T(8,128)(2,1)S(1)} %get-tuple-element.76.dbr) | copy-start | bytes 786436
  119.0 3.7 %slice-start.1 = ((s8[8388608]{0:T(1024)(128)(4,1)}), s8[4194304]{0:T(1024)(128)(4,1)S(1)}, s32[]{:S(2)}) async-start(s8[8388608]{0:T(1024)(128)(4,1)} %bitcast.99), calls=%async_computation.1 | async-start | bytes 8388608
  122.7 3.1 copy-start.2
  125.8 1.7 copy-start.1
  126.2 3.7 %copy-start.5 = (bf16[128,1024]{1,0:T(8,128)(2,1)}, bf16[128,1024]{1,0:T(8,128)(2,1)S(1)}, u32[]{:S(2)}) copy-start(bf16[128,1024]{1,0:T(8,128)(2,1)S(1)} %get-tuple-element.78.datt) | copy-start | bytes 786436
  302.4 7.5 %copy-start.8 = (f32[24,128]{1,0:T(8,128)S(1)}, f32[24,128]{1,0:T(8,128)}, u32[]{:S(2)}) copy-start(f32[24,128]{1,0:T(8,128)} %get-tuple-element.64) | copy-start | bytes 36868

commit v4 on v3

--- a/solution.py
+++ b/solution.py
@@ -1,5 +1,3 @@
-import functools
-
 import jax
 import jax.numpy as jnp
 from jax import lax
@@ -18,29 +16,6 @@
 VMEM_LIMIT = 56 * 1024 * 1024
 VM = pl.BlockSpec(memory_space=pltpu.VMEM)
 ANY = pl.BlockSpec(memory_space=pl.ANY)
-
-
-def layer_norm(values, norm_gain, norm_shift):
-    row_mean = jnp.mean(values, axis=-1, keepdims=True)
-    centered = values - row_mean
-    row_var = jnp.mean(centered * centered, axis=-1, keepdims=True)
-    return centered * lax.rsqrt(row_var + NORM_EPS) * norm_gain + norm_shift
-
-
-def gelu_exact(values):
-    return 0.5 * values * (1.0 + lax.erf(values * 0.7071067811865476))
-
-
-def outer_sum(left, right):
-    return lax.dot_general(
-        left, right, (((0,), (0,)), ((), ())), preferred_element_type=jnp.float32
-    )
-
-
-def times_transposed(left, right):
-    return lax.dot_general(
-        left, right, (((1,), (1,)), ((), ())), preferred_element_type=jnp.float32
-    )
 
 
 def pack_tokens(src, send, parts):
@@ -336,144 +311,30 @@
     return {"ctx": pair[0], "shard": pair[1]}
 
 
-def first_kernel(w, small, w_all, small_all, ls, os, orr, cs, cr, gs, gr, fs, fr, ss, sr, sl):
-    unused_c, s, *unused = place()
-    peers = [mesh_id(peer) for peer in group_ids()]
-    around = [ring[k] for ring in rings() for k in (1, 2)]
-    barrier = pltpu.get_barrier_semaphore()
-    for peer in peers + around:
-        pl.semaphore_signal(barrier, inc=1, device_id=peer, device_id_type=MESH)
-    pl.semaphore_wait(barrier, len(peers) + len(around))
-    gather = WeightGather(w, w_all, 0, ls, os, orr, cs, cr, gs, gr, fs, fr)
-    gather.step(0)
-    pending = [
-        send(small, small_all.at[s], ss.at[k], sr.at[k], peer) for k, peer in enumerate(peers)
-    ]
-    own = pltpu.make_async_copy(small, small_all.at[s], sl)
-    own.start()
-    for k in range(1, WeightGather.STEPS):
-        gather.step(k)
-    own.wait()
-    for k, peer in enumerate(group_ids()):
-        pending[k].wait_send()
-        got = small_all.at[peer[1]]
-        remote(got, got, ss.at[k], sr.at[k], peers[k]).wait_recv()
-
-
-def gather_first(w, small):
-    dma = pltpu.SemaphoreType.DMA
-    return pl.pallas_call(
-        first_kernel,
-        out_shape=(
-            jax.ShapeDtypeStruct((4, *w.shape), w.dtype),
-            jax.ShapeDtypeStruct((4, *small.shape), small.dtype),
-        ),
-        in_specs=[ANY, VM],
-        out_specs=(VM, VM),
-        scratch_shapes=weight_sems(1) + [dma((3,)), dma((3,)), dma],
-        compiler_params=pltpu.CompilerParams(
-            collective_id=3, has_side_effects=True, vmem_limit_bytes=VMEM_LIMIT
-        ),
-    )(w, small)
-
-
-QB = 256
-
-
-def attn_fwd_kernel(
-    proj, w0, w1, w2, ctx_out, qkv_out, o_out, lse_out, all0, all1, all2,
-    send, recv, send2, recv2, keys, vt, ssem, rsem, ssem2, rsem2, *wsems
+QB = 128
+
+
+def normalized(values):
+    centered = values - jnp.mean(values, axis=-1, keepdims=True)
+    scale = lax.rsqrt(jnp.mean(centered * centered, axis=-1, keepdims=True) + NORM_EPS)
+    return centered * scale, scale
+
+
+def norm_back(upstream, unit, scale):
+    mean = jnp.mean(upstream, axis=-1, keepdims=True)
+    along = jnp.mean(upstream * unit, axis=-1, keepdims=True)
+    return scale * (upstream - mean - unit * along)
+
+
+def layer_kernel(
+    x, cot, b_qv, b_out, g_one, s_one, b_ff, g_two, s_two, b_in, w_qkv, w_out, w_in, w_ff,
+    result, d_inputs, dproj_g, act_g, dpre_g, datt_g, hid_g, dbr_g, ctx_g, x_g, small_g,
+    wq, wo, wi, wf, params, params_all, proj, q_send, q_recv, c_send, c_recv, g_send, g_recv,
+    p_send, p_recv, keys, vt, kt, vals, dk, dv, o_s, lse_s, act, gelu_d, dpre, datt, dctx, dproj,
+    hidden, unit_one, d_first, small,
+    qss, qrs, css, crs, gss, grs, pss, prs, xs, xr, fs, fr, ls, es, er, els, ms, mr, ml, *wsems
 ):
-    me = lax.axis_index("ctx")
-    barrier = pltpu.get_barrier_semaphore()
-    signal_ctx_peers(barrier, me)
-    for peer in group_ids()[:2]:
-        pl.semaphore_signal(barrier, inc=1, device_id=mesh_id(peer), device_id_type=MESH)
-    pack_tokens(proj, send, 3)
-    pl.semaphore_wait(barrier, NC + 1)
-    a2a_start(send, recv, ssem, rsem, me)
-    gathers = [
-        WeightGather(w, out, n, *wsems)
-        for n, (w, out) in enumerate(((w0, all0), (w1, all1), (w2, all2)))
-    ]
-
-    def advance(k):
-        for gather in gathers:
-            gather.step(k)
-
-    advance(0)
-    recv[me] = send[me]
-    a2a_wait(send, recv, ssem, rsem, me)
-    qkv_out[...] = recv[...]
-    keys[...] = halves(recv[:, 32:64, :].reshape(1024, 128))
-    vp = recv[:, 64:96, :].reshape(1024, 128).astype(jnp.float32).T.astype(jnp.bfloat16)
-    vt[...] = jnp.concatenate([vp[:64], vp[64:]], axis=1)
-    advance(1)
-
-    def step(i, carry):
-        qp = recv[pl.ds(i * 8, 8), 0:32, :].reshape(QB, 128) * jnp.bfloat16(SCALE)
-        s = dot_nt(keys[...], halves(qp))
-        m = jnp.max(s, axis=0, keepdims=True)
-        p = jnp.exp(s - m)
-        total = jnp.sum(p, axis=0, keepdims=True)
-        ot = dot_nn(vt[...], p.astype(jnp.bfloat16)) / total
-        o = jnp.concatenate([ot[:, :QB], ot[:, QB:]], axis=0).T
-        o_out[pl.ds(pl.multiple_of(i * QB, QB), QB), :] = o
-        lse_out[i] = m + jnp.log(total)
-        send2[pl.ds(i * 8, 8)] = o.astype(jnp.bfloat16).reshape(8, 32, 128)
-        return carry
-
-    lax.fori_loop(0, 1, step, 0)
-    advance(2)
-    lax.fori_loop(1, 2, step, 0)
-    advance(3)
-    lax.fori_loop(2, 4, step, 0)
-    a2a_start(send2, recv2, ssem2, rsem2, me)
-    recv2[me] = send2[me]
-    advance(4)
-    a2a_wait(send2, recv2, ssem2, rsem2, me)
-    unpack_tokens(recv2, ctx_out, 1)
-    advance(5)
-    advance(6)
-
-
-def attn_fwd(projected, w_out, w_in, w_ff):
-    return pl.pallas_call(
-        attn_fwd_kernel,
-        out_shape=(
-            jax.ShapeDtypeStruct((128, D), jnp.bfloat16),
-            jax.ShapeDtypeStruct((NC, 96, 128), jnp.bfloat16),
-            jax.ShapeDtypeStruct((1024, 128), jnp.float32),
-            jax.ShapeDtypeStruct((4, 1, 2 * QB), jnp.float32),
-        )
-        + tuple(jax.ShapeDtypeStruct((4, *w.shape), w.dtype) for w in (w_out, w_in, w_ff)),
-        in_specs=[VM, ANY, ANY, ANY],
-        out_specs=(VM,) * 7,
-        scratch_shapes=[
-            pltpu.VMEM((NC, 96, 128), jnp.bfloat16),
-            pltpu.VMEM((NC, 96, 128), jnp.bfloat16),
-            pltpu.VMEM((NC, 32, 128), jnp.bfloat16),
-            pltpu.VMEM((NC, 32, 128), jnp.bfloat16),
-            pltpu.VMEM((2048, DH), jnp.bfloat16),
-            pltpu.VMEM((DH, 2048), jnp.bfloat16),
-            pltpu.SemaphoreType.DMA((NC,)),
-            pltpu.SemaphoreType.DMA((NC,)),
-            pltpu.SemaphoreType.DMA((NC,)),
-            pltpu.SemaphoreType.DMA((NC,)),
-        ]
-        + weight_sems(3),
-        compiler_params=pltpu.CompilerParams(
-            collective_id=0, has_side_effects=True, vmem_limit_bytes=VMEM_LIMIT
-        ),
-    )(projected, w_out, w_in, w_ff)
-
-
-def attn_bwd_kernel(
-    dctx, qkv, o_in, lse_in, small_in, act, dpre, datt, hid, dbr, ctx, xin,
-    dproj_out, dproj_g, act_g, dpre_g, datt_g, hid_g, dbr_g, ctx_g, x_g, small_g,
-    send, recv, send2, recv2, keys, kt, vals, dk, dv, dproj, small,
-    ssem, rsem, ssem2, rsem2, xs, xr, fs, fr, ls, ps, pr, pls,
-):
+    bf, f32 = jnp.bfloat16, jnp.float32
     me = lax.axis_index("ctx")
     shard = lax.axis_index("shard")
     peers = group_ids()
@@ -481,50 +342,203 @@
     signal_ctx_peers(barrier, me)
     for peer in peers:
         pl.semaphore_signal(barrier, inc=1, device_id=mesh_id(peer), device_id_type=MESH)
-    pack_tokens(dctx, send, 1)
+    x_g[0] = x[...]
+    for n, ref in enumerate((b_out, g_one, s_one, b_ff, g_two, s_two)):
+        params[2 * n : 2 * n + 2, :] = widen(ref[...])
+    params[12:20, :] = widen(b_in[...])
+    for n in range(2):
+        for k in range(2):
+            row = 20 + 2 * n + k
+            params[row : row + 1, :] = widen(b_qv[n : n + 1, 128 * k : 128 * k + 128])
+    params_all[shard] = params[...]
     pl.semaphore_wait(barrier, NC + 2)
-    a2a_start(send, recv, ssem, rsem, me)
-
-    def to_peer(src, dst, ssem_, rsem_, peer):
-        copy = remote(src, dst, ssem_, rsem_, mesh_id(peer))
-        copy.start()
-        return copy
-
-    slices = ((act, act_g, 1024), (dpre, dpre_g, 1024), (datt, datt_g, 256))
-    whole = ((hid, hid_g), (dbr, dbr_g), (ctx, ctx_g), (xin, x_g))
-    pending, arriving = [], []
-    for n, (src, dst) in enumerate(whole):
-        pending.append(to_peer(src, dst.at[1], xs.at[n, 0], xr.at[n, 0], peers[0]))
-        arriving.append(to_peer(src, dst.at[2], xs.at[n, 1], xr.at[n, 1], peers[1]))
-        local = pltpu.make_async_copy(src, dst.at[0], ls.at[n])
-        local.start()
-        pending.append(local)
-    for n, (src, dst, width) in enumerate(slices):
+
+    gather_q, *gathers = [
+        WeightGather(w, out, n, *wsems)
+        for n, (w, out) in enumerate(((w_qkv, wq), (w_out, wo), (w_in, wi), (w_ff, wf)))
+    ]
+    early, late = gathers[:2], gathers[2:]
+
+    def advance(group, k):
+        for gather in group:
+            gather.step(k)
+
+    def to_peer(src, dst, send_sem, recv_sem, peer):
+        return send(src, dst, send_sem, recv_sem, mesh_id(peer))
+
+    pending, arriving = [], {}
+
+    def share_whole(n, ref):
+        pending.append(to_peer(ref.at[0], ref.at[1], xs.at[n, 0], xr.at[n, 0], peers[0]))
+        arriving[n] = to_peer(ref.at[0], ref.at[2], xs.at[n, 1], xr.at[n, 1], peers[1])
+
+    def pass_on(n, ref):
+        arriving[n].wait()
+        pending.append(to_peer(ref.at[2], ref.at[3], fs.at[n], fr.at[n], peers[0]))
+
+    def share_slices(n, src, dst, width):
         for k, peer in enumerate(peers):
             cols = pl.ds(pl.multiple_of(peer[1] * width, width), width)
             pending.append(
                 to_peer(src.at[:, cols], dst.at[k + 1], xs.at[4 + n, k], xr.at[4 + n, k], peer)
             )
         cols = pl.ds(pl.multiple_of(shard * width, width), width)
-        local = pltpu.make_async_copy(src.at[:, cols], dst.at[0], ls.at[4 + n])
-        local.start()
-        pending.append(local)
-
-    recv[me] = send[me]
-    keys[...] = halves(qkv[:, 32:64, :].reshape(1024, 128))
-    vals[...] = halves(qkv[:, 64:96, :].reshape(1024, 128))
-    kp = qkv[:, 32:64, :].reshape(1024, 128).astype(jnp.float32).T.astype(jnp.bfloat16)
+        own = pltpu.make_async_copy(src.at[:, cols], dst.at[0], ls.at[n])
+        own.start()
+        pending.append(own)
+
+    gather_q.step(0)
+    sent_params = [
+        to_peer(params, params_all.at[shard], ms.at[k], mr.at[k], peer)
+        for k, peer in enumerate(peers)
+    ]
+    advance(gathers, 0)
+    share_whole(3, x_g)
+    gather_q.step(1)
+    gather_q.step(2)
+    gather_q.step(3)
+    advance(gathers, 1)
+    gather_q.step(4)
+    advance(gathers, 2)
+    gather_q.step(5)
+    gather_q.step(6)
+    advance(early, 3)
+    for k, peer in enumerate(peers):
+        sent_params[k].wait_send()
+        got = params_all.at[peer[1]]
+        remote(got, got, ms.at[k], mr.at[k], mesh_id(peer)).wait_recv()
+
+    def vector(n):
+        return jnp.concatenate(
+            [params_all[k // 2, 2 * n + k % 2 : 2 * n + k % 2 + 1, :] for k in range(8)], axis=1
+        )
+
+    def cols_of(j):
+        return pl.ds(pl.multiple_of(j * D, D), D)
+
+    def project(j, carry):
+        part = jnp.where(j == 0, 1.0, 0.0) * vector(10) + jnp.where(j == 2, 1.0, 0.0) * vector(11)
+        weight = wq[:, 0, :, cols_of(j)].reshape(D, D)
+        proj[:, cols_of(j)] = (dot_nn(x[...], weight) + part).astype(bf)
+        return carry
+
+    lax.fori_loop(0, 3, project, 0)
+    pack_tokens(proj, q_send, 3)
+    a2a_start(q_send, q_recv, qss, qrs, me)
+    q_recv[me] = q_send[me]
+    a2a_wait(q_send, q_recv, qss, qrs, me)
+    advance(early, 4)
+    advance(late, 3)
+    keys[...] = halves(q_recv[:, 32:64, :].reshape(1024, 128))
+    vals[...] = halves(q_recv[:, 64:96, :].reshape(1024, 128))
+    vp = widen(q_recv[:, 64:96, :].reshape(1024, 128)).T.astype(bf)
+    vt[...] = jnp.concatenate([vp[:64], vp[64:]], axis=1)
+    kp = widen(q_recv[:, 32:64, :].reshape(1024, 128)).T.astype(bf)
     kt[...] = jnp.concatenate([kp[:64], kp[64:]], axis=1)
+    steps = 1024 // QB
+    blocks_of = QB // 32
+
+    def attend(i, carry):
+        blocks = pl.ds(i * blocks_of, blocks_of)
+        qb = halves(q_recv[blocks, 0:32, :].reshape(QB, 128) * bf(SCALE))
+        s = dot_nt(keys[...], qb)
+        m = jnp.max(s, axis=0, keepdims=True)
+        p = jnp.exp(s - m)
+        total = jnp.sum(p, axis=0, keepdims=True)
+        ot = dot_nn(vt[...], p.astype(bf)) / total
+        o = jnp.concatenate([ot[:, :QB], ot[:, QB:]], axis=0).T
+        o_s[pl.ds(pl.multiple_of(i * QB, QB), QB), :] = o
+        lse_s[i] = m + jnp.log(total)
+        c_send[blocks] = o.astype(bf).reshape(blocks_of, 32, 128)
+        return carry
+
+    lax.fori_loop(0, steps // 2, attend, 0)
+    advance(early, 5)
+    advance(late, 4)
+    lax.fori_loop(steps // 2, steps, attend, 0)
+    a2a_start(c_send, c_recv, css, crs, me)
+    c_recv[me] = c_send[me]
+    a2a_wait(c_send, c_recv, css, crs, me)
+    unpack_tokens(c_recv, ctx_g.at[0], 1)
+    share_whole(2, ctx_g)
+    advance(early, 6)
+
+    w_out_whole = wo[...].reshape(D, D)
+    first_sum = widen(x[...]) + (dot_nn(ctx_g[0], w_out_whole) + vector(0))
+    unit, scale_one = normalized(first_sum)
+    unit_one[...] = unit
+    hidden[...] = unit * vector(1) + vector(2)
+    hid_g[0] = hidden[...].astype(bf)
+    share_whole(0, hid_g)
+    pass_on(3, x_g)
+
+    def feed(j, carry):
+        bias = jnp.concatenate([params_all[j, 12 + k : 13 + k, :] for k in range(8)], axis=1)
+        pre = dot_nn(hid_g[0], wi[:, 0, :, cols_of(j)].reshape(D, D)) + bias
+        grown = 0.5 * (1.0 + lax.erf(pre * 0.7071067811865476))
+        act[:, cols_of(j)] = (pre * grown).astype(bf)
+        gelu_d[:, cols_of(j)] = grown + pre * (0.3989422804014327 * jnp.exp(-0.5 * pre * pre))
+        return carry
+
+    lax.fori_loop(0, 4, feed, 0)
+    share_slices(0, act, act_g, 1024)
+    advance(late, 5)
+    advance(late, 6)
+
+    def feed_out(j, total):
+        return total + dot_nn(act[:, cols_of(j)], wf[j].reshape(D, D))
+
+    branch = lax.fori_loop(0, 4, feed_out, jnp.zeros((128, D), f32))
+    unit_two, scale_two = normalized(hidden[...] + (branch + vector(3)))
+    result[...] = (unit_two * vector(4) + vector(5)).astype(bf)
+
+    def put_sums(n, values):
+        sums = jnp.sum(values, axis=0, keepdims=True)
+        for k in range(8):
+            row = 2 * n + k % 2
+            small[k // 2, row : row + 1, :] = sums[:, 128 * k : 128 * k + 128]
+
+    upstream = widen(cot[...])
+    put_sums(4, upstream * unit_two)
+    put_sums(5, upstream)
+    d_second = norm_back(upstream * vector(4), unit_two, scale_two)
+    dbr_g[0] = d_second.astype(bf)
+    share_whole(1, dbr_g)
+    put_sums(3, widen(dbr_g[0]))
+
+    def feed_back(j, total):
+        d_act = dot_nt(dbr_g[0], wf[j].reshape(D, D))
+        part = (d_act * gelu_d[:, cols_of(j)]).astype(bf)
+        dpre[:, cols_of(j)] = part
+        sums = jnp.sum(widen(part), axis=0, keepdims=True)
+        for k in range(8):
+            small[j, 12 + k : 13 + k, :] = sums[:, 128 * k : 128 * k + 128]
+        return total + dot_nt(part, wi[:, 0, :, cols_of(j)].reshape(D, D))
+
+    d_hidden = lax.fori_loop(0, 4, feed_back, d_second)
+    share_slices(1, dpre, dpre_g, 1024)
+    put_sums(1, d_hidden * unit_one[...])
+    put_sums(2, d_hidden)
+    d_first[...] = norm_back(d_hidden * vector(1), unit_one[...], scale_one)
+    datt[...] = d_first[...].astype(bf)
+    put_sums(0, widen(datt[...]))
+    dctx[...] = dot_nt(datt[...], wo[...].reshape(D, D)).astype(bf)
+    pack_tokens(dctx, g_send, 1)
+    a2a_start(g_send, g_recv, gss, grs, me)
+    share_slices(2, datt, datt_g, 256)
+    g_recv[me] = g_send[me]
     dk[...] = jnp.zeros_like(dk)
     dv[...] = jnp.zeros_like(dv)
-    a2a_wait(send, recv, ssem, rsem, me)
-
-    def step(i, carry):
-        blocks = pl.ds(i * 8, 8)
-        qb = halves(qkv[blocks, 0:32, :].reshape(QB, 128) * jnp.bfloat16(SCALE))
-        dop = recv[blocks].reshape(QB, 128)
-        o = o_in[pl.ds(pl.multiple_of(i * QB, QB), QB), :]
-        prod = (dop.astype(jnp.float32) * o).T
+    pass_on(2, ctx_g)
+    pass_on(0, hid_g)
+    a2a_wait(g_send, g_recv, gss, grs, me)
+
+    def attend_back(i, carry):
+        blocks = pl.ds(i * blocks_of, blocks_of)
+        qb = halves(q_recv[blocks, 0:32, :].reshape(QB, 128) * bf(SCALE))
+        dop = g_recv[blocks].reshape(QB, 128)
+        o = o_s[pl.ds(pl.multiple_of(i * QB, QB), QB), :]
+        prod = (widen(dop) * o).T
         delta = jnp.concatenate(
             [
                 jnp.sum(prod[:64], axis=0, keepdims=True),
@@ -533,87 +547,85 @@
             axis=1,
         )
         dob = halves(dop)
-        probs = jnp.exp(dot_nt(keys[...], qb) - lse_in[i])
-        dv[...] += dot_nn(probs.astype(jnp.bfloat16), dob)
-        ds = (probs * (dot_nt(vals[...], dob) - delta)).astype(jnp.bfloat16)
+        probs = jnp.exp(dot_nt(keys[...], qb) - lse_s[i])
+        dv[...] += dot_nn(probs.astype(bf), dob)
+        ds = (probs * (dot_nt(vals[...], dob) - delta)).astype(bf)
         dk[...] += dot_nn(ds, qb)
         dqt = dot_nn(kt[...], ds) * SCALE
         dq = jnp.concatenate([dqt[:, :QB], dqt[:, QB:]], axis=0).T
-        send2[blocks, 0:32, :] = dq.astype(jnp.bfloat16).reshape(8, 32, 128)
-        return carry
-
-    lax.fori_loop(0, 4, step, 0)
+        p_send[blocks, 0:32, :] = dq.astype(bf).reshape(blocks_of, 32, 128)
+        return carry
+
+    lax.fori_loop(0, steps, attend_back, 0)
     for n, total in enumerate((dk, dv)):
         packed = jnp.concatenate([total[0:1024, :], total[1024:2048, :]], axis=1)
-        send2[:, 32 + 32 * n : 64 + 32 * n, :] = packed.astype(jnp.bfloat16).reshape(NC, 32, 128)
-    a2a_start(send2, recv2, ssem2, rsem2, me)
-    recv2[me] = send2[me]
-    for n, (src, dst) in enumerate(whole):
-        arriving[n].wait()
-        pending.append(to_peer(dst.at[2], dst.at[3], fs.at[n], fr.at[n], peers[0]))
-    a2a_wait(send2, recv2, ssem2, rsem2, me)
-    unpack_tokens(recv2, dproj, 3)
+        p_send[:, 32 + 32 * n : 64 + 32 * n, :] = packed.astype(bf).reshape(NC, 32, 128)
+    a2a_start(p_send, p_recv, pss, prs, me)
+    p_recv[me] = p_send[me]
+    pass_on(1, dbr_g)
+    a2a_wait(p_send, p_recv, pss, prs, me)
+    unpack_tokens(p_recv, dproj, 3)
     for k, peer in enumerate(peers):
         cols = pl.ds(pl.multiple_of(peer[1] * 768, 256), 768)
-        pending.append(to_peer(dproj.at[:, cols], dproj_g.at[k + 1], ps.at[k], pr.at[k], peer))
+        pending.append(to_peer(dproj.at[:, cols], dproj_g.at[k + 1], es.at[k], er.at[k], peer))
     cols = pl.ds(pl.multiple_of(shard * 768, 256), 768)
-    small[...] = small_in[...]
-    for n, part in enumerate((0, 2 * D)):
-        sums = jnp.sum(dproj[:, part : part + D].astype(jnp.float32), axis=0, keepdims=True)
-        for j in range(8):
-            row = 20 + 2 * n + j % 2
-            small[j // 2, row : row + 1, :] = sums[:, 128 * j : 128 * j + 128]
+    own = pltpu.make_async_copy(dproj.at[:, cols], dproj_g.at[0], els.at[0])
+    own.start()
+    pending.append(own)
+    put_sums(10, widen(dproj[:, 0:D]))
+    put_sums(11, widen(dproj[:, 2 * D : 3 * D]))
     for k, peer in enumerate(peers):
         pending.append(
-            to_peer(small.at[peer[1]], small_g.at[k + 1], ps.at[3 + k], pr.at[3 + k], peer)
-        )
-    local = pltpu.make_async_copy(small.at[shard], small_g.at[0], pls.at[2])
-    local.start()
-    pending.append(local)
-    local = pltpu.make_async_copy(dproj.at[:, cols], dproj_g.at[0], pls.at[0])
-    local.start()
-    pending.append(local)
-    local = pltpu.make_async_copy(dproj, dproj_out, pls.at[1])
-    local.start()
-    pending.append(local)
+            to_peer(small.at[peer[1]], small_g.at[k + 1], es.at[3 + k], er.at[3 + k], peer)
+        )
+    small_g[0] = small[shard]
+
+    def back_in(j, total):
+        weight = wq[:, 0, :, cols_of(j)].reshape(D, D)
+        return total + dot_nt(dproj[:, cols_of(j)], weight)
+
+    d_inputs[...] = lax.fori_loop(0, 3, back_in, d_first[...])
     for copy in pending:
         copy.wait()
 
 
-def attn_bwd(dctx, qkv, o, lse, small, act, dpre, datt, hid, dbr, ctx, xin):
-    bf = jnp.bfloat16
+def layer(x, cot, smalls, weights):
+    bf, f32 = jnp.bfloat16, jnp.float32
     sds = jax.ShapeDtypeStruct
     dma = pltpu.SemaphoreType.DMA
+    vm = pltpu.VMEM
+    rows = (128, D)
     return pl.pallas_call(
-        attn_bwd_kernel,
+        layer_kernel,
         out_shape=(
-            sds((128, 3 * D), bf), sds((4, 128, 768), bf), sds((4, 128, 1024), bf),
-            sds((4, 128, 1024), bf), sds((4, 128, 256), bf), sds((4, 128, 1024), bf),
-            sds((4, 128, 1024), bf), sds((4, 128, 1024), bf), sds((4, 128, 1024), bf),
-            sds((4, 24, 128), jnp.float32),
+            sds(rows, bf), sds(rows, f32), sds((4, 128, 768), bf), sds((4, *rows), bf),
+            sds((4, *rows), bf), sds((4, 128, 256), bf), sds((4, *rows), bf), sds((4, *rows), bf),
+            sds((4, *rows), bf), sds((4, *rows), bf), sds((4, 24, 128), f32),
         ),
-        in_specs=[VM] * 5 + [ANY] * 7,
-        out_specs=(VM,) * 10,
-        scratch_shapes=[
-            pltpu.VMEM((NC, 32, 128), bf),
-            pltpu.VMEM((NC, 32, 128), bf),
-            pltpu.VMEM((NC, 96, 128), bf),
-            pltpu.VMEM((NC, 96, 128), bf),
-            pltpu.VMEM((2048, DH), bf),
-            pltpu.VMEM((DH, 2048), bf),
-            pltpu.VMEM((2048, DH), bf),
-            pltpu.VMEM((2048, DH), jnp.float32),
-            pltpu.VMEM((2048, DH), jnp.float32),
-            pltpu.VMEM((128, 3 * D), bf),
-            pltpu.VMEM((4, 24, 128), jnp.float32),
-            dma((NC,)), dma((NC,)), dma((NC,)), dma((NC,)),
-            dma((7, 3)), dma((7, 3)), dma((4,)), dma((4,)), dma((7,)),
-            dma((6,)), dma((6,)), dma((3,)),
-        ],
+        in_specs=[VM] * 10 + [ANY] * 4,
+        out_specs=(VM,) * 11,
+        scratch_shapes=[vm((4, *w.shape), bf) for w in weights]
+        + [
+            vm((24, 128), f32), vm((4, 24, 128), f32), vm((128, 3 * D), bf),
+            vm((NC, 96, 128), bf), vm((NC, 96, 128), bf), vm((NC, 32, 128), bf),
+            vm((NC, 32, 128), bf), vm((NC, 32, 128), bf), vm((NC, 32, 128), bf),
+            vm((NC, 96, 128), bf), vm((NC, 96, 128), bf), vm((2048, DH), bf),
+            vm((DH, 2048), bf), vm((DH, 2048), bf), vm((2048, DH), bf), vm((2048, DH), f32),
+            vm((2048, DH), f32), vm((1024, 128), f32), vm((1024 // QB, 1, 2 * QB), f32),
+            vm((128, FF), bf), vm((128, FF), f32), vm((128, FF), bf), vm(rows, bf), vm(rows, bf),
+            vm((128, 3 * D), bf), vm(rows, f32), vm(rows, f32), vm(rows, f32),
+            vm((4, 24, 128), f32),
+        ]
+        + [dma((NC,))] * 8
+        + [
+            dma((7, 3)), dma((7, 3)), dma((4,)), dma((4,)), dma((3,)),
+            dma((6,)), dma((6,)), dma((1,)), dma((3,)), dma((3,)), dma,
+        ]
+        + weight_sems(4),
         compiler_params=pltpu.CompilerParams(
-            collective_id=1, has_side_effects=True, vmem_limit_bytes=VMEM_LIMIT
+            collective_id=0, has_side_effects=True, vmem_limit_bytes=62 * 1024 * 1024
         ),
-    )(dctx, qkv, o, lse, small, act, dpre, datt, hid, dbr, ctx, xin)
+    )(x, cot, *smalls, *weights)
 
 
 def widen(a):
@@ -897,92 +909,36 @@
     inputs, cotangent, w_qkv, bias_qv, w_out, bias_out, ln1_gain, ln1_bias, w_in, bias_in,
     w_ff_out, bias_ff_out, ln2_gain, ln2_bias,
 ):
-    bf, f32 = jnp.bfloat16, jnp.float32
-    small = jnp.concatenate(
-        [
-            bias_qv.reshape(512), bias_out, ln1_gain, ln1_bias, bias_ff_out, ln2_gain, ln2_bias,
-            bias_in, jnp.zeros((1024,), bf),
-        ]
-    )
-    w_qkv_all, small_all = gather_first(w_qkv.reshape(1, 256, 3 * D), small.reshape(32, 128))
-    w_qkv_all = w_qkv_all.reshape(D, 3 * D)
-    small_all = small_all.reshape(4, 4096).astype(f32)
-    bias_q, bias_v, bias_o, gain_one, shift_one, bias_ff, gain_two, shift_two = (
-        small_all[:, 256 * k : 256 * k + 256].reshape(D) for k in range(8)
-    )
-    bias_i = small_all[:, 2048:3072].reshape(FF)
-    groups, rows_dev = inputs.shape[0], inputs.shape[1]
-    token_count = groups * rows_dev
-    tokens_in = inputs.reshape(token_count, D)
-    bias_full = jnp.concatenate([bias_q, jnp.zeros((D,), f32), bias_v])
-    projected = (jnp.dot(tokens_in, w_qkv_all, preferred_element_type=f32) + bias_full).astype(bf)
-    flat_context, qkv, o, lse, w_out_all, w_in_all, w_ff_all = attn_fwd(
-        projected, w_out.reshape(1, 256, D), w_in.reshape(1, 256, FF), w_ff_out.reshape(4, 256, D)
-    )
-    w_out_all = w_out_all.reshape(D, D)
-    w_in_all = w_in_all.reshape(D, FF)
-    w_ff_all = w_ff_all.reshape(FF, D)
-    attended = jnp.dot(flat_context, w_out_all, preferred_element_type=f32) + bias_o
-    first_sum = tokens_in.astype(f32) + attended
-    hidden = layer_norm(first_sum, gain_one, shift_one)
-    hidden_low = hidden.astype(bf)
-    pre_act = jnp.dot(hidden_low, w_in_all, preferred_element_type=f32) + bias_i
-    act_low = gelu_exact(pre_act).astype(bf)
-    branch = jnp.dot(act_low, w_ff_all, preferred_element_type=f32) + bias_ff
-    second_sum = hidden + branch
-    result_rows = layer_norm(second_sum, gain_two, shift_two)
-    upstream = cotangent.reshape(token_count, D).astype(f32)
-    unused_two, pull_two = jax.vjp(layer_norm, second_sum, gain_two, shift_two)
-    d_second, d_gain_two, d_shift_two = pull_two(upstream)
-    d_branch = d_second.astype(bf)
-    grad_bias_ff = jnp.sum(d_branch.astype(f32), axis=0)
-    d_act = times_transposed(d_branch, w_ff_all)
-    unused_act, pull_gelu = jax.vjp(gelu_exact, pre_act)
-    d_pre_act = pull_gelu(d_act)[0].astype(bf)
-    grad_bias_in = jnp.sum(d_pre_act.astype(f32), axis=0)
-    d_hidden = d_second + times_transposed(d_pre_act, w_in_all)
-    unused_one, pull_one = jax.vjp(layer_norm, first_sum, gain_one, shift_one)
-    d_first, d_gain_one, d_shift_one = pull_one(d_hidden)
-    d_attended = d_first.astype(bf)
-    grad_bias_out = jnp.sum(d_attended.astype(f32), axis=0)
-    d_context = times_transposed(d_attended, w_out_all).astype(bf)
-    small_sums = jnp.concatenate(
-        [
-            a.reshape(4, -1)
-            for a in (
-                grad_bias_out, d_gain_one, d_shift_one, grad_bias_ff, d_gain_two, d_shift_two,
-                grad_bias_in, jnp.zeros((2048,), f32),
-            )
-        ],
-        axis=1,
-    ).reshape(4, 24, 128)
-    d_projected, dproj_g, act_g, dpre_g, datt_g, hid_g, dbr_g, ctx_g, x_g, small_g = attn_bwd(
-        d_context, qkv, o, lse, small_sums, act_low, d_pre_act, d_attended, hidden_low, d_branch,
-        flat_context, tokens_in,
+    smalls = (bias_out, ln1_gain, ln1_bias, bias_ff_out, ln2_gain, ln2_bias)
+    result, d_inputs, dproj_g, act_g, dpre_g, datt_g, hid_g, dbr_g, ctx_g, x_g, small_g = layer(
+        inputs.reshape(128, D),
+        cotangent.reshape(128, D),
+        (bias_qv, *(a.reshape(2, 128) for a in smalls), bias_in.reshape(8, 128)),
+        (
+            w_qkv.reshape(1, 256, 3 * D), w_out.reshape(1, 256, D), w_in.reshape(1, 256, FF),
+            w_ff_out.reshape(4, 256, D),
+        ),
     )
     red_ff, red_in, red_qo, sums = reduce_grads(
         act_g, dbr_g, hid_g, dpre_g, x_g, dproj_g, ctx_g, datt_g, small_g
     )
     own_ff, own_in, own_qkv, own_out = widen_grads(red_ff, red_in, red_qo)
-    d_inputs = d_first + times_transposed(d_projected, w_qkv_all)
     sums = sums.reshape(3072)
 
     def own(k):
         return sums[256 * k : 256 * k + 256]
 
-    own_bias_in = sums[1536:2560]
-    own_bias_qv = sums[2560:].reshape(2, 256)
     return (
-        result_rows.astype(bf).reshape(groups, rows_dev, D),
-        d_inputs.reshape(groups, rows_dev, D),
+        result.reshape(inputs.shape),
+        d_inputs.reshape(inputs.shape),
         own_qkv,
-        own_bias_qv,
+        sums[2560:].reshape(2, 256),
         own_out,
         own(0),
         own(1),
         own(2),
         own_in,
-        own_bias_in,
+        sums[1536:2560],
         own_ff,
         own(3),
         own(4),

time: 312 us -> 255 us (0.82)
  matrix products: 27.4 us -> 0 us
  Pallas kernels: 268 us -> 248 us
  local copies, waits for them, and re-layouts: 12.3 us -> 5.49 us
  other arithmetic: 3.19 us -> 0 us
    dot_general x8 -> x0, matrix products: 27.4 us -> none  [the longest x4 14.4 us: times_transposed(): lax.dot_general(left, right, (((1,), (1,)), ((), ())), preferred_element_...]
    pallas_call x3 -> x1, Pallas kernels: 163 us -> 142 us  [layer(): pl.pallas_call(layer_kernel, out_shape=(sds(rows, bf), sds(rows, f32), sd...]
    unnamed x57 -> x6, local copies, waits for them, and re-layouts: 10.4 us -> 1.5 us
where the time goes in v4:
time: 255 us; the launch traced here: 254 us
  Pallas kernels  248 us (97%)
  local copies, waits for them, and re-layouts  5.49 us (2%)
    pallas_call x1, Pallas kernels, layer(): pl.pallas_call(layer_kernel, out_shape=(sds(rows, bf), sds(rows, f32), sd...  142 us
    pallas_call x1, Pallas kernels, reduce_grads(): pl.pallas_call(reduce_kernel, out_shape=(full, full, full, jax.ShapeDtype...  98.8 us
    pallas_call x1, Pallas kernels, widen_grads(): pl.pallas_call(widen_kernel, grid=(4,), out_shape=(sds((1024, 1024), f32)...  7.59 us

profile of v4, /device:TPU:0, one launch (start us, length us, event | category | flops | bytes accessed | tf_op | source)
XLA Modules:
  0.0 254.4 jit_solution(1037282983015296123)
XLA Ops:
  0.7 141.9 %shard_map.245 = (bf16[128,1024]{1,0:T(8,128)(2,1)}, f32[128,1024]{1,0:T(8,128)}, bf16[4,128,768]{2,1,0:T(8,128)(2,1)}, bf16[4,128,1024]{2,1,0:T(8,128)(2,1)}, b...) custom-call(bf16[128,1024]{1,0:T(8,128)(2,1)} %bitcast.34, ...), custom_call_target="tpu_custom_call" | custom-call | tf_op jit(solution)/shard_map/pallas_call | solution.py:598
  142.5 98.8 %shard_map.246 = (bf16[4,256,1024]{2,1,0:T(8,128)(2,1)}, bf16[4,256,1024]{2,1,0:T(8,128)(2,1)}, bf16[4,256,1024]{2,1,0:T(8,128)(2,1)}, f32[24,128]{1,0:T(8,128)}) custom-call(bf16[4,128,1024]{2,1,0:T(8,128)(2,1)} %get-tuple-element.35.act, bf16[4,128,1024]{2,1,0:T(8,128)(2,1)} %get-tuple-element.36.dbr, bf16[4,128,1024]{2,1,0:T(8,128)(2,1)} %get-tuple-element.37.hid, ...), custom_call_target="tpu_custom_call" | custom-call | tf_op jit(solution)/shard_map/pallas_call | solution.py:857
  241.4 0.7 slice.46
  242.0 0.6 reshape.101
  242.6 1.3 slice_bitcast_fusion
  243.9 1.4 slice_bitcast_fusion.1
  245.3 0.0 copy-start.1
  245.4 0.0 copy-start
  245.4 7.6 %shard_map.247 = (f32[1024,1024]{1,0:T(8,128)}, f32[256,4096]{1,0:T(8,128)}, f32[256,3072]{1,0:T(8,128)}, f32[256,1024]{1,0:T(8,128)}) custom-call(bf16[4,256,1024]{2,1,0:T(8,128)(2,1)} %get-tuple-element.44.ff, bf16[4,256,1024]{2,1,0:T(8,128)(2,1)} %get-tuple-element.45.in_, bf16[4,256,1024]{2,1,0:T(8,128)(2,1)} %get-tuple-element.46.qo), custom_call_target="tpu_custom_call" | custom-call | tf_op jit(solution)/shard_map/pallas_call | solution.py:890
  252.9 0.0 copy-done.1
  252.9 0.7 copy.30
  253.6 0.0 copy-done
  253.7 0.8 copy.31
Async XLA Ops:
  245.3 7.6 %copy-start.1 = (bf16[128,1024]{1,0:T(8,128)(2,1)S(1)}, bf16[128,1024]{1,0:T(8,128)(2,1)}, u32[]{:S(2)}) copy-start(bf16[128,1024]{1,0:T(8,128)(2,1)} %get-tuple-element.33) | copy-start | bytes 786436
  245.4 8.3 %copy-start = (f32[128,1024]{1,0:T(8,128)S(1)}, f32[128,1024]{1,0:T(8,128)}, u32[]{:S(2)}) copy-start(f32[128,1024]{1,0:T(8,128)} %get-tuple-element.34) | copy-start | bytes 1572868

commit v5 on v4

--- a/solution.py
+++ b/solution.py
@@ -314,320 +314,6 @@
 QB = 128
 
 
-def normalized(values):
-    centered = values - jnp.mean(values, axis=-1, keepdims=True)
-    scale = lax.rsqrt(jnp.mean(centered * centered, axis=-1, keepdims=True) + NORM_EPS)
-    return centered * scale, scale
-
-
-def norm_back(upstream, unit, scale):
-    mean = jnp.mean(upstream, axis=-1, keepdims=True)
-    along = jnp.mean(upstream * unit, axis=-1, keepdims=True)
-    return scale * (upstream - mean - unit * along)
-
-
-def layer_kernel(
-    x, cot, b_qv, b_out, g_one, s_one, b_ff, g_two, s_two, b_in, w_qkv, w_out, w_in, w_ff,
-    result, d_inputs, dproj_g, act_g, dpre_g, datt_g, hid_g, dbr_g, ctx_g, x_g, small_g,
-    wq, wo, wi, wf, params, params_all, proj, q_send, q_recv, c_send, c_recv, g_send, g_recv,
-    p_send, p_recv, keys, vt, kt, vals, dk, dv, o_s, lse_s, act, gelu_d, dpre, datt, dctx, dproj,
-    hidden, unit_one, d_first, small,
-    qss, qrs, css, crs, gss, grs, pss, prs, xs, xr, fs, fr, ls, es, er, els, ms, mr, ml, *wsems
-):
-    bf, f32 = jnp.bfloat16, jnp.float32
-    me = lax.axis_index("ctx")
-    shard = lax.axis_index("shard")
-    peers = group_ids()
-    barrier = pltpu.get_barrier_semaphore()
-    signal_ctx_peers(barrier, me)
-    for peer in peers:
-        pl.semaphore_signal(barrier, inc=1, device_id=mesh_id(peer), device_id_type=MESH)
-    x_g[0] = x[...]
-    for n, ref in enumerate((b_out, g_one, s_one, b_ff, g_two, s_two)):
-        params[2 * n : 2 * n + 2, :] = widen(ref[...])
-    params[12:20, :] = widen(b_in[...])
-    for n in range(2):
-        for k in range(2):
-            row = 20 + 2 * n + k
-            params[row : row + 1, :] = widen(b_qv[n : n + 1, 128 * k : 128 * k + 128])
-    params_all[shard] = params[...]
-    pl.semaphore_wait(barrier, NC + 2)
-
-    gather_q, *gathers = [
-        WeightGather(w, out, n, *wsems)
-        for n, (w, out) in enumerate(((w_qkv, wq), (w_out, wo), (w_in, wi), (w_ff, wf)))
-    ]
-    early, late = gathers[:2], gathers[2:]
-
-    def advance(group, k):
-        for gather in group:
-            gather.step(k)
-
-    def to_peer(src, dst, send_sem, recv_sem, peer):
-        return send(src, dst, send_sem, recv_sem, mesh_id(peer))
-
-    pending, arriving = [], {}
-
-    def share_whole(n, ref):
-        pending.append(to_peer(ref.at[0], ref.at[1], xs.at[n, 0], xr.at[n, 0], peers[0]))
-        arriving[n] = to_peer(ref.at[0], ref.at[2], xs.at[n, 1], xr.at[n, 1], peers[1])
-
-    def pass_on(n, ref):
-        arriving[n].wait()
-        pending.append(to_peer(ref.at[2], ref.at[3], fs.at[n], fr.at[n], peers[0]))
-
-    def share_slices(n, src, dst, width):
-        for k, peer in enumerate(peers):
-            cols = pl.ds(pl.multiple_of(peer[1] * width, width), width)
-            pending.append(
-                to_peer(src.at[:, cols], dst.at[k + 1], xs.at[4 + n, k], xr.at[4 + n, k], peer)
-            )
-        cols = pl.ds(pl.multiple_of(shard * width, width), width)
-        own = pltpu.make_async_copy(src.at[:, cols], dst.at[0], ls.at[n])
-        own.start()
-        pending.append(own)
-
-    gather_q.step(0)
-    sent_params = [
-        to_peer(params, params_all.at[shard], ms.at[k], mr.at[k], peer)
-        for k, peer in enumerate(peers)
-    ]
-    advance(gathers, 0)
-    share_whole(3, x_g)
-    gather_q.step(1)
-    gather_q.step(2)
-    gather_q.step(3)
-    advance(gathers, 1)
-    gather_q.step(4)
-    advance(gathers, 2)
-    gather_q.step(5)
-    gather_q.step(6)
-    advance(early, 3)
-    for k, peer in enumerate(peers):
-        sent_params[k].wait_send()
-        got = params_all.at[peer[1]]
-        remote(got, got, ms.at[k], mr.at[k], mesh_id(peer)).wait_recv()
-
-    def vector(n):
-        return jnp.concatenate(
-            [params_all[k // 2, 2 * n + k % 2 : 2 * n + k % 2 + 1, :] for k in range(8)], axis=1
-        )
-
-    def cols_of(j):
-        return pl.ds(pl.multiple_of(j * D, D), D)
-
-    def project(j, carry):
-        part = jnp.where(j == 0, 1.0, 0.0) * vector(10) + jnp.where(j == 2, 1.0, 0.0) * vector(11)
-        weight = wq[:, 0, :, cols_of(j)].reshape(D, D)
-        proj[:, cols_of(j)] = (dot_nn(x[...], weight) + part).astype(bf)
-        return carry
-
-    lax.fori_loop(0, 3, project, 0)
-    pack_tokens(proj, q_send, 3)
-    a2a_start(q_send, q_recv, qss, qrs, me)
-    q_recv[me] = q_send[me]
-    a2a_wait(q_send, q_recv, qss, qrs, me)
-    advance(early, 4)
-    advance(late, 3)
-    keys[...] = halves(q_recv[:, 32:64, :].reshape(1024, 128))
-    vals[...] = halves(q_recv[:, 64:96, :].reshape(1024, 128))
-    vp = widen(q_recv[:, 64:96, :].reshape(1024, 128)).T.astype(bf)
-    vt[...] = jnp.concatenate([vp[:64], vp[64:]], axis=1)
-    kp = widen(q_recv[:, 32:64, :].reshape(1024, 128)).T.astype(bf)
-    kt[...] = jnp.concatenate([kp[:64], kp[64:]], axis=1)
-    steps = 1024 // QB
-    blocks_of = QB // 32
-
-    def attend(i, carry):
-        blocks = pl.ds(i * blocks_of, blocks_of)
-        qb = halves(q_recv[blocks, 0:32, :].reshape(QB, 128) * bf(SCALE))
-        s = dot_nt(keys[...], qb)
-        m = jnp.max(s, axis=0, keepdims=True)
-        p = jnp.exp(s - m)
-        total = jnp.sum(p, axis=0, keepdims=True)
-        ot = dot_nn(vt[...], p.astype(bf)) / total
-        o = jnp.concatenate([ot[:, :QB], ot[:, QB:]], axis=0).T
-        o_s[pl.ds(pl.multiple_of(i * QB, QB), QB), :] = o
-        lse_s[i] = m + jnp.log(total)
-        c_send[blocks] = o.astype(bf).reshape(blocks_of, 32, 128)
-        return carry
-
-    lax.fori_loop(0, steps // 2, attend, 0)
-    advance(early, 5)
-    advance(late, 4)
-    lax.fori_loop(steps // 2, steps, attend, 0)
-    a2a_start(c_send, c_recv, css, crs, me)
-    c_recv[me] = c_send[me]
-    a2a_wait(c_send, c_recv, css, crs, me)
-    unpack_tokens(c_recv, ctx_g.at[0], 1)
-    share_whole(2, ctx_g)
-    advance(early, 6)
-
-    w_out_whole = wo[...].reshape(D, D)
-    first_sum = widen(x[...]) + (dot_nn(ctx_g[0], w_out_whole) + vector(0))
-    unit, scale_one = normalized(first_sum)
-    unit_one[...] = unit
-    hidden[...] = unit * vector(1) + vector(2)
-    hid_g[0] = hidden[...].astype(bf)
-    share_whole(0, hid_g)
-    pass_on(3, x_g)
-
-    def feed(j, carry):
-        bias = jnp.concatenate([params_all[j, 12 + k : 13 + k, :] for k in range(8)], axis=1)
-        pre = dot_nn(hid_g[0], wi[:, 0, :, cols_of(j)].reshape(D, D)) + bias
-        grown = 0.5 * (1.0 + lax.erf(pre * 0.7071067811865476))
-        act[:, cols_of(j)] = (pre * grown).astype(bf)
-        gelu_d[:, cols_of(j)] = grown + pre * (0.3989422804014327 * jnp.exp(-0.5 * pre * pre))
-        return carry
-
-    lax.fori_loop(0, 4, feed, 0)
-    share_slices(0, act, act_g, 1024)
-    advance(late, 5)
-    advance(late, 6)
-
-    def feed_out(j, total):
-        return total + dot_nn(act[:, cols_of(j)], wf[j].reshape(D, D))
-
-    branch = lax.fori_loop(0, 4, feed_out, jnp.zeros((128, D), f32))
-    unit_two, scale_two = normalized(hidden[...] + (branch + vector(3)))
-    result[...] = (unit_two * vector(4) + vector(5)).astype(bf)
-
-    def put_sums(n, values):
-        sums = jnp.sum(values, axis=0, keepdims=True)
-        for k in range(8):
-            row = 2 * n + k % 2
-            small[k // 2, row : row + 1, :] = sums[:, 128 * k : 128 * k + 128]
-
-    upstream = widen(cot[...])
-    put_sums(4, upstream * unit_two)
-    put_sums(5, upstream)
-    d_second = norm_back(upstream * vector(4), unit_two, scale_two)
-    dbr_g[0] = d_second.astype(bf)
-    share_whole(1, dbr_g)
-    put_sums(3, widen(dbr_g[0]))
-
-    def feed_back(j, total):
-        d_act = dot_nt(dbr_g[0], wf[j].reshape(D, D))
-        part = (d_act * gelu_d[:, cols_of(j)]).astype(bf)
-        dpre[:, cols_of(j)] = part
-        sums = jnp.sum(widen(part), axis=0, keepdims=True)
-        for k in range(8):
-            small[j, 12 + k : 13 + k, :] = sums[:, 128 * k : 128 * k + 128]
-        return total + dot_nt(part, wi[:, 0, :, cols_of(j)].reshape(D, D))
-
-    d_hidden = lax.fori_loop(0, 4, feed_back, d_second)
-    share_slices(1, dpre, dpre_g, 1024)
-    put_sums(1, d_hidden * unit_one[...])
-    put_sums(2, d_hidden)
-    d_first[...] = norm_back(d_hidden * vector(1), unit_one[...], scale_one)
-    datt[...] = d_first[...].astype(bf)
-    put_sums(0, widen(datt[...]))
-    dctx[...] = dot_nt(datt[...], wo[...].reshape(D, D)).astype(bf)
-    pack_tokens(dctx, g_send, 1)
-    a2a_start(g_send, g_recv, gss, grs, me)
-    share_slices(2, datt, datt_g, 256)
-    g_recv[me] = g_send[me]
-    dk[...] = jnp.zeros_like(dk)
-    dv[...] = jnp.zeros_like(dv)
-    pass_on(2, ctx_g)
-    pass_on(0, hid_g)
-    a2a_wait(g_send, g_recv, gss, grs, me)
-
-    def attend_back(i, carry):
-        blocks = pl.ds(i * blocks_of, blocks_of)
-        qb = halves(q_recv[blocks, 0:32, :].reshape(QB, 128) * bf(SCALE))
-        dop = g_recv[blocks].reshape(QB, 128)
-        o = o_s[pl.ds(pl.multiple_of(i * QB, QB), QB), :]
-        prod = (widen(dop) * o).T
-        delta = jnp.concatenate(
-            [
-                jnp.sum(prod[:64], axis=0, keepdims=True),
-                jnp.sum(prod[64:], axis=0, keepdims=True),
-            ],
-            axis=1,
-        )
-        dob = halves(dop)
-        probs = jnp.exp(dot_nt(keys[...], qb) - lse_s[i])
-        dv[...] += dot_nn(probs.astype(bf), dob)
-        ds = (probs * (dot_nt(vals[...], dob) - delta)).astype(bf)
-        dk[...] += dot_nn(ds, qb)
-        dqt = dot_nn(kt[...], ds) * SCALE
-        dq = jnp.concatenate([dqt[:, :QB], dqt[:, QB:]], axis=0).T
-        p_send[blocks, 0:32, :] = dq.astype(bf).reshape(blocks_of, 32, 128)
-        return carry
-
-    lax.fori_loop(0, steps, attend_back, 0)
-    for n, total in enumerate((dk, dv)):
-        packed = jnp.concatenate([total[0:1024, :], total[1024:2048, :]], axis=1)
-        p_send[:, 32 + 32 * n : 64 + 32 * n, :] = packed.astype(bf).reshape(NC, 32, 128)
-    a2a_start(p_send, p_recv, pss, prs, me)
-    p_recv[me] = p_send[me]
-    pass_on(1, dbr_g)
-    a2a_wait(p_send, p_recv, pss, prs, me)
-    unpack_tokens(p_recv, dproj, 3)
-    for k, peer in enumerate(peers):
-        cols = pl.ds(pl.multiple_of(peer[1] * 768, 256), 768)
-        pending.append(to_peer(dproj.at[:, cols], dproj_g.at[k + 1], es.at[k], er.at[k], peer))
-    cols = pl.ds(pl.multiple_of(shard * 768, 256), 768)
-    own = pltpu.make_async_copy(dproj.at[:, cols], dproj_g.at[0], els.at[0])
-    own.start()
-    pending.append(own)
-    put_sums(10, widen(dproj[:, 0:D]))
-    put_sums(11, widen(dproj[:, 2 * D : 3 * D]))
-    for k, peer in enumerate(peers):
-        pending.append(
-            to_peer(small.at[peer[1]], small_g.at[k + 1], es.at[3 + k], er.at[3 + k], peer)
-        )
-    small_g[0] = small[shard]
-
-    def back_in(j, total):
-        weight = wq[:, 0, :, cols_of(j)].reshape(D, D)
-        return total + dot_nt(dproj[:, cols_of(j)], weight)
-
-    d_inputs[...] = lax.fori_loop(0, 3, back_in, d_first[...])
-    for copy in pending:
-        copy.wait()
-
-
-def layer(x, cot, smalls, weights):
-    bf, f32 = jnp.bfloat16, jnp.float32
-    sds = jax.ShapeDtypeStruct
-    dma = pltpu.SemaphoreType.DMA
-    vm = pltpu.VMEM
-    rows = (128, D)
-    return pl.pallas_call(
-        layer_kernel,
-        out_shape=(
-            sds(rows, bf), sds(rows, f32), sds((4, 128, 768), bf), sds((4, *rows), bf),
-            sds((4, *rows), bf), sds((4, 128, 256), bf), sds((4, *rows), bf), sds((4, *rows), bf),
-            sds((4, *rows), bf), sds((4, *rows), bf), sds((4, 24, 128), f32),
-        ),
-        in_specs=[VM] * 10 + [ANY] * 4,
-        out_specs=(VM,) * 11,
-        scratch_shapes=[vm((4, *w.shape), bf) for w in weights]
-        + [
-            vm((24, 128), f32), vm((4, 24, 128), f32), vm((128, 3 * D), bf),
-            vm((NC, 96, 128), bf), vm((NC, 96, 128), bf), vm((NC, 32, 128), bf),
-            vm((NC, 32, 128), bf), vm((NC, 32, 128), bf), vm((NC, 32, 128), bf),
-            vm((NC, 96, 128), bf), vm((NC, 96, 128), bf), vm((2048, DH), bf),
-            vm((DH, 2048), bf), vm((DH, 2048), bf), vm((2048, DH), bf), vm((2048, DH), f32),
-            vm((2048, DH), f32), vm((1024, 128), f32), vm((1024 // QB, 1, 2 * QB), f32),
-            vm((128, FF), bf), vm((128, FF), f32), vm((128, FF), bf), vm(rows, bf), vm(rows, bf),
-            vm((128, 3 * D), bf), vm(rows, f32), vm(rows, f32), vm(rows, f32),
-            vm((4, 24, 128), f32),
-        ]
-        + [dma((NC,))] * 8
-        + [
-            dma((7, 3)), dma((7, 3)), dma((4,)), dma((4,)), dma((3,)),
-            dma((6,)), dma((6,)), dma((1,)), dma((3,)), dma((3,)), dma,
-        ]
-        + weight_sems(4),
-        compiler_params=pltpu.CompilerParams(
-            collective_id=0, has_side_effects=True, vmem_limit_bytes=62 * 1024 * 1024
-        ),
-    )(x, cot, *smalls, *weights)
-
-
 def widen(a):
     return a.astype(jnp.float32)
 
@@ -676,11 +362,48 @@
             copy.wait_send()
 
 
+class SmallSums:
+    STEPS = 4
+
+    def __init__(self, parts, totals, landed, out, send_sem, recv_sem):
+        c, unused_s, y, z, x = place()
+        self.parts, self.totals, self.landed, self.out = parts, totals, landed, out
+        self.ss, self.rs = send_sem, recv_sem
+        self.targets = (
+            [{"ctx": c - x + lax.rem(x + j, 4)} for j in range(1, 4)],
+            [{"ctx": y * 16 + lax.rem(z + j, 4) * 4 + x} for j in range(1, 4)],
+            [{"ctx": lax.rem(c + 16, 32)}],
+        )
+
+    def spread(self, k):
+        self.sent = [
+            send(
+                self.totals.at[k], self.landed.at[k, j], self.ss.at[k, j], self.rs.at[k, j], target
+            )
+            for j, target in enumerate(self.targets[k])
+        ]
+
+    def step(self, k):
+        if k == 0:
+            self.totals[0] = self.parts[0] + self.parts[1] + self.parts[2] + self.parts[3]
+            self.spread(0)
+            return
+        total = self.totals[k - 1]
+        for j, copy in enumerate(self.sent):
+            copy.wait()
+            total = total + self.landed[k - 1, j]
+        if k < 3:
+            self.totals[k] = total
+            self.spread(k)
+        else:
+            self.out[...] = total
+
+
 class Stream:
     STEPS = 12
 
     def __init__(self, grad, out, m, h, scratch, dsems):
-        (big, t1, small, t2, ybuf, u, v) = scratch
+        (room, small, t2, ybuf, u, v) = scratch
         (p1s, p1r, p2s, p2r, ys, yr, ts, tr, ms, as_, ar, g1s, g1r, g2s, g2r) = dsems
         c, s, y, z, x = place()
         along_x, along_z = rings()
@@ -688,7 +411,9 @@
         n = 2 * m + h
         self.m, self.c, self.s, self.y = m, c, s, y
         self.pair = {"ctx": lax.rem(c + 16, 32)}
-        self.t1, self.t2, self.u, self.v = t1.at[n], t2.at[n], u.at[n], v.at[n]
+        self.t1, self.t2, self.u, self.v = room(24 + n), t2.at[n], u.at[n], v.at[n]
+        down, up, first, second = (room(4 * n + k) for k in range(4))
+        big = (first.at[0:2], first.at[2:4], second.at[0:2], second.at[2:4], down, up)
         self.ybuf = ybuf.at[n]
         self.out = out
         self.ys, self.yr, self.ts, self.tr = ys.at[n], yr.at[n], ts.at[n], tr.at[n]
@@ -696,7 +421,7 @@
         cols = pl.ds(h * 512, 512)
         self.reduce1 = RingReduce(
             lambda p, k: grad.at[pl.ds(2 * k, 2), rows64(p), cols], self.t1,
-            [b.at[n] for b in big], one, sems(p1s, n), sems(p1r, n),
+            big, one, sems(p1s, n), sems(p1r, n),
         )
         self.reduce2 = RingReduce(
             lambda p, k: self.t1.at[pl.ds(2 * k, 2), rows16(p)], self.t2,
@@ -787,93 +512,392 @@
             self.gather2.finish()
 
 
-def reduce_kernel(
-    act, dbr, hid, dpre, x, dproj, ctx, datt, small_g, ff_out, in_out, qo_out, small_out,
-    grads, ra, rb, sa, sb, fd, fu, ra2, rb2, sa2, sb2, fd2, fu2, t1, t2, ybuf, u, v,
-    small, small_all, small_s, small_r, *dsems
+def normalized(values):
+    centered = values - jnp.mean(values, axis=-1, keepdims=True)
+    scale = lax.rsqrt(jnp.mean(centered * centered, axis=-1, keepdims=True) + NORM_EPS)
+    return centered * scale, scale
+
+
+def norm_back(upstream, unit, scale):
+    mean = jnp.mean(upstream, axis=-1, keepdims=True)
+    along = jnp.mean(upstream * unit, axis=-1, keepdims=True)
+    return scale * (upstream - mean - unit * along)
+
+
+def layer_kernel(
+    x, cot, b_qv, b_out, g_one, s_one, b_ff, g_two, s_two, b_in, w_qkv, w_out, w_in, w_ff,
+    result, d_inputs, ff_out, in_out, qo_out, small_out,
+    dproj_g, act_g, dpre_g, datt_g, hid_g, dbr_g, ctx_g, x_g, small_g,
+    wq, wo, wi, wf, params, params_all, proj, q_send, q_recv, c_send, c_recv, g_send, g_recv,
+    p_send, p_recv, keys, vt, kt, vals, dk, dv, o_s, lse_s, act, gelu_d, dpre, datt, dctx, dproj,
+    hidden, unit_one, d_first, small, small_totals, small_landed,
+    ra2, rb2, sa2, sb2, fd2, fu2, t2, ybuf, u, v,
+    qss, qrs, css, crs, gss, grs, pss, prs, xs, xr, fs, fr, ls, es, er, els, ms, mr, sss, srs, *more
 ):
-    c, s, *unused = place()
+    bf, f32 = jnp.bfloat16, jnp.float32
+    wsems, dsems = more[:9], more[9:]
+    me = lax.axis_index("ctx")
+    shard = lax.axis_index("shard")
+    peers = group_ids()
     barrier = pltpu.get_barrier_semaphore()
-    signal_ctx_peers(barrier, c)
-    for j in range(1, 4):
+    signal_ctx_peers(barrier, me)
+    for peer in peers:
+        pl.semaphore_signal(barrier, inc=1, device_id=mesh_id(peer), device_id_type=MESH)
+    for peer in peers[1:]:
         pl.semaphore_signal(
-            barrier, inc=1, device_id={"shard": lax.rem(s + j, 4)}, device_id_type=MESH
-        )
-    small[...] = small_g[0] + small_g[1] + small_g[2] + small_g[3]
-    pl.semaphore_wait(barrier, NC + 2)
-    scratch = ((ra, rb, sa, sb, fd, fu), t1, (ra2, rb2, sa2, sb2, fd2, fu2), t2, ybuf, u, v)
-    streams = []
-    products = (((act, dbr, 0),), ((hid, dpre, 0),), ((x, dproj, 0), (ctx, datt, 768)))
-    for m, (terms, out) in enumerate(zip(products, (ff_out, in_out, qo_out))):
-        for left, right, at in terms:
-            width = right.shape[-1]
-
-            def block(q, carry):
-                part = left[:, :, pl.ds(pl.multiple_of(q * 256, 256), 256)].reshape(512, 256)
-                grads[m, q, :, at : at + width] = lax.dot_general(
-                    part, right[...].reshape(512, width), (((0,), (0,)), ((), ())),
-                    preferred_element_type=jnp.float32,
-                ).astype(jnp.bfloat16)
-                return carry
-
-            lax.fori_loop(0, 4, block, 0)
-        for h in range(2):
-            streams.append(Stream(grads.at[m], out, m, h, scratch, dsems))
-            streams[-1].step(0)
-
-    def spread(k, carry):
-        dest = lax.rem(c + k, NC)
-        remote(small, small_all.at[c], small_s.at[k], small_r.at[k], {"ctx": dest}).start()
+            barrier, inc=1, device_id=mesh_id((me, peer[1])), device_id_type=MESH
+        )
+    x_g[0] = x[...]
+    for n, ref in enumerate((b_out, g_one, s_one, b_ff, g_two, s_two)):
+        params[2 * n : 2 * n + 2, :] = widen(ref[...])
+    params[12:20, :] = widen(b_in[...])
+    for n in range(2):
+        for k in range(2):
+            row = 20 + 2 * n + k
+            params[row : row + 1, :] = widen(b_qv[n : n + 1, 128 * k : 128 * k + 128])
+    params_all[shard] = params[...]
+    pl.semaphore_wait(barrier, NC + 4)
+
+    gather_q, *gathers = [
+        WeightGather(w, out, n, *wsems)
+        for n, (w, out) in enumerate(((w_qkv, wq), (w_out, wo), (w_in, wi), (w_ff, wf)))
+    ]
+    early, late = gathers[:2], gathers[2:]
+
+    def advance(group, k):
+        for gather in group:
+            gather.step(k)
+
+    def to_peer(src, dst, send_sem, recv_sem, peer):
+        return send(src, dst, send_sem, recv_sem, mesh_id(peer))
+
+    pending, arriving = {}, {}
+
+    def share_whole(n, ref):
+        pending[n] = [to_peer(ref.at[0], ref.at[1], xs.at[n, 0], xr.at[n, 0], peers[0])]
+        arriving[n] = to_peer(ref.at[0], ref.at[2], xs.at[n, 1], xr.at[n, 1], peers[1])
+
+    def pass_on(n, ref):
+        arriving[n].wait()
+        pending[n].append(to_peer(ref.at[2], ref.at[3], fs.at[n], fr.at[n], peers[0]))
+
+    def share_slices(n, src, dst, width):
+        cols = pl.ds(pl.multiple_of(shard * width, width), width)
+        own = pltpu.make_async_copy(src.at[:, cols], dst.at[0], ls.at[n - 4])
+        own.start()
+        pending[n] = [own]
+        for k, peer in enumerate(peers):
+            cols = pl.ds(pl.multiple_of(peer[1] * width, 256), width)
+            pending[n].append(
+                to_peer(src.at[:, cols], dst.at[k + 1], xs.at[n, k], xr.at[n, k], peer)
+            )
+
+    def arrived(*which):
+        for n in which:
+            for copy in pending[n]:
+                copy.wait()
+
+    gather_q.step(0)
+    sent_params = [
+        to_peer(params, params_all.at[shard], ms.at[k], mr.at[k], peer)
+        for k, peer in enumerate(peers)
+    ]
+    advance(gathers, 0)
+    share_whole(3, x_g)
+    gather_q.step(1)
+    gather_q.step(2)
+    gather_q.step(3)
+    advance(gathers, 1)
+    gather_q.step(4)
+    advance(gathers, 2)
+    gather_q.step(5)
+    gather_q.step(6)
+    advance(early, 3)
+    for k, peer in enumerate(peers):
+        sent_params[k].wait_send()
+        got = params_all.at[peer[1]]
+        remote(got, got, ms.at[k], mr.at[k], mesh_id(peer)).wait_recv()
+
+    def vector(n):
+        return jnp.concatenate(
+            [params_all[k // 2, 2 * n + k % 2 : 2 * n + k % 2 + 1, :] for k in range(8)], axis=1
+        )
+
+    def cols_of(j):
+        return pl.ds(pl.multiple_of(j * D, D), D)
+
+    def project(j, carry):
+        part = jnp.where(j == 0, 1.0, 0.0) * vector(10) + jnp.where(j == 2, 1.0, 0.0) * vector(11)
+        weight = wq[:, 0, :, cols_of(j)].reshape(D, D)
+        proj[:, cols_of(j)] = (dot_nn(x[...], weight) + part).astype(bf)
         return carry
 
-    lax.fori_loop(1, NC, spread, 0)
+    lax.fori_loop(0, 3, project, 0)
+    pack_tokens(proj, q_send, 3)
+    a2a_start(q_send, q_recv, qss, qrs, me)
+    q_recv[me] = q_send[me]
+    a2a_wait(q_send, q_recv, qss, qrs, me)
+    advance(early, 4)
+    advance(late, 3)
+    keys[...] = halves(q_recv[:, 32:64, :].reshape(1024, 128))
+    vals[...] = halves(q_recv[:, 64:96, :].reshape(1024, 128))
+    vp = widen(q_recv[:, 64:96, :].reshape(1024, 128)).T.astype(bf)
+    vt[...] = jnp.concatenate([vp[:64], vp[64:]], axis=1)
+    kp = widen(q_recv[:, 32:64, :].reshape(1024, 128)).T.astype(bf)
+    kt[...] = jnp.concatenate([kp[:64], kp[64:]], axis=1)
+    steps = 1024 // QB
+    blocks_of = QB // 32
+
+    def attend(i, carry):
+        blocks = pl.ds(i * blocks_of, blocks_of)
+        qb = halves(q_recv[blocks, 0:32, :].reshape(QB, 128) * bf(SCALE))
+        s = dot_nt(keys[...], qb)
+        m = jnp.max(s, axis=0, keepdims=True)
+        p = jnp.exp(s - m)
+        total = jnp.sum(p, axis=0, keepdims=True)
+        ot = dot_nn(vt[...], p.astype(bf)) / total
+        o = jnp.concatenate([ot[:, :QB], ot[:, QB:]], axis=0).T
+        o_s[pl.ds(pl.multiple_of(i * QB, QB), QB), :] = o
+        lse_s[i] = m + jnp.log(total)
+        c_send[blocks] = o.astype(bf).reshape(blocks_of, 32, 128)
+        return carry
+
+    lax.fori_loop(0, steps // 2, attend, 0)
+    advance(early, 5)
+    advance(late, 4)
+    lax.fori_loop(steps // 2, steps, attend, 0)
+    a2a_start(c_send, c_recv, css, crs, me)
+    c_recv[me] = c_send[me]
+    a2a_wait(c_send, c_recv, css, crs, me)
+    unpack_tokens(c_recv, ctx_g.at[0], 1)
+    share_whole(2, ctx_g)
+    advance(early, 6)
+
+    w_out_whole = wo[...].reshape(D, D)
+    first_sum = widen(x[...]) + (dot_nn(ctx_g[0], w_out_whole) + vector(0))
+    unit, scale_one = normalized(first_sum)
+    unit_one[...] = unit
+    hidden[...] = unit * vector(1) + vector(2)
+    hid_g[0] = hidden[...].astype(bf)
+    share_whole(0, hid_g)
+    pass_on(3, x_g)
+
+    def feed(j, carry):
+        bias = jnp.concatenate([params_all[j, 12 + k : 13 + k, :] for k in range(8)], axis=1)
+        pre = dot_nn(hid_g[0], wi[:, 0, :, cols_of(j)].reshape(D, D)) + bias
+        grown = 0.5 * (1.0 + lax.erf(pre * 0.7071067811865476))
+        act[:, cols_of(j)] = (pre * grown).astype(bf)
+        gelu_d[:, cols_of(j)] = grown + pre * (0.3989422804014327 * jnp.exp(-0.5 * pre * pre))
+        return carry
+
+    lax.fori_loop(0, 4, feed, 0)
+    share_slices(4, act, act_g, 1024)
+    advance(late, 5)
+    advance(late, 6)
+
+    def feed_out(j, total):
+        return total + dot_nn(act[:, cols_of(j)], wf[j].reshape(D, D))
+
+    branch = lax.fori_loop(0, 4, feed_out, jnp.zeros((128, D), f32))
+    unit_two, scale_two = normalized(hidden[...] + (branch + vector(3)))
+    result[...] = (unit_two * vector(4) + vector(5)).astype(bf)
+
+    def put_sums(n, values):
+        sums = jnp.sum(values, axis=0, keepdims=True)
+        for k in range(8):
+            row = 2 * n + k % 2
+            small[k // 2, row : row + 1, :] = sums[:, 128 * k : 128 * k + 128]
+
+    upstream = widen(cot[...])
+    put_sums(4, upstream * unit_two)
+    put_sums(5, upstream)
+    d_second = norm_back(upstream * vector(4), unit_two, scale_two)
+    dbr_g[0] = d_second.astype(bf)
+    share_whole(1, dbr_g)
+    put_sums(3, widen(dbr_g[0]))
+
+    def feed_back(j, total):
+        d_act = dot_nt(dbr_g[0], wf[j].reshape(D, D))
+        part = (d_act * gelu_d[:, cols_of(j)]).astype(bf)
+        dpre[:, cols_of(j)] = part
+        sums = jnp.sum(widen(part), axis=0, keepdims=True)
+        for k in range(8):
+            small[j, 12 + k : 13 + k, :] = sums[:, 128 * k : 128 * k + 128]
+        return total + dot_nt(part, wi[:, 0, :, cols_of(j)].reshape(D, D))
+
+    d_hidden = lax.fori_loop(0, 4, feed_back, d_second)
+    share_slices(5, dpre, dpre_g, 1024)
+    put_sums(1, d_hidden * unit_one[...])
+    put_sums(2, d_hidden)
+    d_first[...] = norm_back(d_hidden * vector(1), unit_one[...], scale_one)
+    datt[...] = d_first[...].astype(bf)
+    put_sums(0, widen(datt[...]))
+    dctx[...] = dot_nt(datt[...], wo[...].reshape(D, D)).astype(bf)
+    pack_tokens(dctx, g_send, 1)
+    a2a_start(g_send, g_recv, gss, grs, me)
+    share_slices(6, datt, datt_g, 256)
+    g_recv[me] = g_send[me]
+    dk[...] = jnp.zeros_like(dk)
+    dv[...] = jnp.zeros_like(dv)
+    pass_on(2, ctx_g)
+    pass_on(0, hid_g)
+    a2a_wait(g_send, g_recv, gss, grs, me)
+
+    def room(k):
+        return wi.at[:, 0, pl.ds(64 * (k % 4), 64), pl.ds(512 * (k // 4), 512)]
+
+    scratch = (room, (ra2, rb2, sa2, sb2, fd2, fu2), t2, ybuf, u, v)
+
+    def product(m, left, right, at):
+        width = right.shape[-1]
+
+        def block(q, carry):
+            part = left[:, :, pl.ds(pl.multiple_of(q * 256, 256), 256)].reshape(512, 256)
+            wf[m, q, :, at : at + width] = lax.dot_general(
+                part, right[...].reshape(512, width), (((0,), (0,)), ((), ())),
+                preferred_element_type=f32,
+            ).astype(bf)
+            return carry
+
+        lax.fori_loop(0, 4, block, 0)
+
+    def streams_of(m, out):
+        streams = [Stream(wf.at[m], out, m, h, scratch, dsems) for h in range(2)]
+        for stream in streams:
+            stream.step(0)
+        return streams
+
+    def attend_back(i, carry):
+        blocks = pl.ds(i * blocks_of, blocks_of)
+        qb = halves(q_recv[blocks, 0:32, :].reshape(QB, 128) * bf(SCALE))
+        dop = g_recv[blocks].reshape(QB, 128)
+        o = o_s[pl.ds(pl.multiple_of(i * QB, QB), QB), :]
+        prod = (widen(dop) * o).T
+        delta = jnp.concatenate(
+            [
+                jnp.sum(prod[:64], axis=0, keepdims=True),
+                jnp.sum(prod[64:], axis=0, keepdims=True),
+            ],
+            axis=1,
+        )
+        dob = halves(dop)
+        probs = jnp.exp(dot_nt(keys[...], qb) - lse_s[i])
+        dv[...] += dot_nn(probs.astype(bf), dob)
+        ds = (probs * (dot_nt(vals[...], dob) - delta)).astype(bf)
+        dk[...] += dot_nn(ds, qb)
+        dqt = dot_nn(kt[...], ds) * SCALE
+        dq = jnp.concatenate([dqt[:, :QB], dqt[:, QB:]], axis=0).T
+        p_send[blocks, 0:32, :] = dq.astype(bf).reshape(blocks_of, 32, 128)
+        return carry
+
+    lax.fori_loop(0, steps // 2, attend_back, 0)
+    pass_on(1, dbr_g)
+    arrived(4, 1)
+    product(0, act_g, dbr_g, 0)
+    ff_streams = streams_of(0, ff_out)
+    lax.fori_loop(steps // 2, steps, attend_back, 0)
+    for n, total in enumerate((dk, dv)):
+        packed = jnp.concatenate([total[0:1024, :], total[1024:2048, :]], axis=1)
+        p_send[:, 32 + 32 * n : 64 + 32 * n, :] = packed.astype(bf).reshape(NC, 32, 128)
+    a2a_start(p_send, p_recv, pss, prs, me)
+    p_recv[me] = p_send[me]
+    for stream in ff_streams:
+        stream.step(1)
+    arrived(0, 5)
+    product(1, hid_g, dpre_g, 0)
+    a2a_wait(p_send, p_recv, pss, prs, me)
+    unpack_tokens(p_recv, dproj, 3)
+    cols = pl.ds(pl.multiple_of(shard * 768, 256), 768)
+    own = pltpu.make_async_copy(dproj.at[:, cols], dproj_g.at[0], els.at[0])
+    own.start()
+    pending[7] = [own]
+    for k, peer in enumerate(peers):
+        cols = pl.ds(pl.multiple_of(peer[1] * 768, 256), 768)
+        pending[7].append(to_peer(dproj.at[:, cols], dproj_g.at[k + 1], es.at[k], er.at[k], peer))
+    in_streams = streams_of(1, in_out)
+    put_sums(10, widen(dproj[:, 0:D]))
+    put_sums(11, widen(dproj[:, 2 * D : 3 * D]))
+    small_g[0] = small[shard]
+    pending[8] = [
+        to_peer(small.at[peer[1]], small_g.at[k + 1], es.at[3 + k], er.at[3 + k], peer)
+        for k, peer in enumerate(peers)
+    ]
+    for stream in ff_streams:
+        stream.step(2)
+
+    def back_in(j, total):
+        weight = wq[:, 0, :, cols_of(j)].reshape(D, D)
+        return total + dot_nt(dproj[:, cols_of(j)], weight)
+
+    d_inputs[...] = lax.fori_loop(0, 3, back_in, d_first[...])
+    for stream in in_streams:
+        stream.step(1)
+    arrived(2, 3, 6)
+    product(2, ctx_g, datt_g, 768)
+    arrived(7)
+    product(2, x_g, dproj_g, 0)
+    qo_streams = streams_of(2, qo_out)
+    arrived(8)
+    sums = SmallSums(small_g, small_totals, small_landed, small_out, sss, srs)
+    sums.step(0)
     for k in range(1, Stream.STEPS):
-        for stream in streams:
-            stream.step(k)
-
-    def arrive(k, carry):
-        source = lax.rem(c + NC - k, NC)
-        copy = remote(small, small_all.at[source], small_s.at[k], small_r.at[k], {"ctx": source})
-        copy.wait_send()
-        copy.wait_recv()
-        return carry
-
-    lax.fori_loop(1, NC, arrive, 0)
-    small_all[c] = small[...]
-    small_out[...] = lax.fori_loop(
-        0, NC, lambda k, acc: acc + small_all[k], jnp.zeros((24, 128), jnp.float32)
-    )
-
-
-def reduce_grads(act, dbr, hid, dpre, x, dproj, ctx, datt, small):
+        for streams, ahead in ((ff_streams, 2), (in_streams, 1), (qo_streams, 0)):
+            if k + ahead < Stream.STEPS:
+                for stream in streams:
+                    stream.step(k + ahead)
+        if k % 2 == 1 and k // 2 + 1 < SmallSums.STEPS:
+            sums.step(k // 2 + 1)
+
+
+def layer(x, cot, smalls, weights):
     bf, f32 = jnp.bfloat16, jnp.float32
+    sds = jax.ShapeDtypeStruct
     dma = pltpu.SemaphoreType.DMA
     vm = pltpu.VMEM
-    full = jax.ShapeDtypeStruct((4, 256, 1024), bf)
-
-    def ring_bufs(rows):
-        return [vm((6, 2, rows, 512), bf)] * 4 + [vm((6, 4, rows, 512), bf)] * 2
-
+    rows = (128, D)
     return pl.pallas_call(
-        reduce_kernel,
-        out_shape=(full, full, full, jax.ShapeDtypeStruct((24, 128), f32)),
-        in_specs=[VM] * 9,
-        out_specs=(VM,) * 4,
-        scratch_shapes=[vm((3, 4, 256, 1024), bf)]
-        + ring_bufs(64)
-        + ring_bufs(16)
+        layer_kernel,
+        out_shape=(
+            sds(rows, bf), sds(rows, f32), sds((4, 256, 1024), bf), sds((4, 256, 1024), bf),
+            sds((4, 256, 1024), bf), sds((24, 128), f32),
+        ),
+        in_specs=[VM] * 10 + [ANY] * 4,
+        out_specs=(VM,) * 6,
+        scratch_shapes=[
+            vm((4, 128, 768), bf), vm((4, *rows), bf), vm((4, *rows), bf), vm((4, 128, 256), bf),
+            vm((4, *rows), bf), vm((4, *rows), bf), vm((4, *rows), bf), vm((4, *rows), bf),
+            vm((4, 24, 128), f32),
+        ]
+        + [vm((4, *w.shape), bf) for w in weights]
         + [
-            vm((6, 4, 64, 512), bf), vm((6, 4, 16, 512), bf), vm((6, 4, 16, 256), bf),
-            vm((6, 4, 16, 256), bf), vm((6, 4, 16, 256), bf),
-            vm((24, 128), f32), vm((NC, 24, 128), f32), dma((NC,)), dma((NC,)),
+            vm((24, 128), f32), vm((4, 24, 128), f32), vm((128, 3 * D), bf),
+            vm((NC, 96, 128), bf), vm((NC, 96, 128), bf), vm((NC, 32, 128), bf),
+            vm((NC, 32, 128), bf), vm((NC, 32, 128), bf), vm((NC, 32, 128), bf),
+            vm((NC, 96, 128), bf), vm((NC, 96, 128), bf), vm((2048, DH), bf),
+            vm((DH, 2048), bf), vm((DH, 2048), bf), vm((2048, DH), bf), vm((2048, DH), f32),
+            vm((2048, DH), f32), vm((1024, 128), f32), vm((1024 // QB, 1, 2 * QB), f32),
+            vm((128, FF), bf), vm((128, FF), f32), vm((128, FF), bf), vm(rows, bf), vm(rows, bf),
+            vm((128, 3 * D), bf), vm(rows, f32), vm(rows, f32), vm(rows, f32),
+            vm((4, 24, 128), f32), vm((3, 24, 128), f32), vm((3, 3, 24, 128), f32),
+        ]
+        + [vm((6, 2, 16, 512), bf)] * 4
+        + [vm((6, 4, 16, 512), bf)] * 3
+        + [vm((6, 4, 16, 256), bf)] * 3
+        + [dma((NC,))] * 8
+        + [
+            dma((7, 3)), dma((7, 3)), dma((4,)), dma((4,)), dma((3,)),
+            dma((6,)), dma((6,)), dma((1,)), dma((3,)), dma((3,)), dma((3, 3)), dma((3, 3)),
+        ]
+        + weight_sems(4)
+        + [
             dma((6, 6)), dma((6, 6)), dma((6, 6)), dma((6, 6)), dma((6,)), dma((6,)),
             dma((6, 4)), dma((6, 4)), dma((6,)), dma((6,)), dma((6,)),
             dma((6, 4)), dma((6, 4)), dma((6, 4)), dma((6, 4)),
         ],
         compiler_params=pltpu.CompilerParams(
-            collective_id=2, has_side_effects=True, vmem_limit_bytes=VMEM_LIMIT
+            collective_id=0, has_side_effects=True, vmem_limit_bytes=62 * 1024 * 1024
         ),
-    )(act, dbr, hid, dpre, x, dproj, ctx, datt, small)
+    )(x, cot, *smalls, *weights)
 
 
 def widen_kernel(ff, in_, qo, ff_out, in_out, qkv_out, w_out):
@@ -910,7 +934,7 @@
     w_ff_out, bias_ff_out, ln2_gain, ln2_bias,
 ):
     smalls = (bias_out, ln1_gain, ln1_bias, bias_ff_out, ln2_gain, ln2_bias)
-    result, d_inputs, dproj_g, act_g, dpre_g, datt_g, hid_g, dbr_g, ctx_g, x_g, small_g = layer(
+    result, d_inputs, red_ff, red_in, red_qo, sums = layer(
         inputs.reshape(128, D),
         cotangent.reshape(128, D),
         (bias_qv, *(a.reshape(2, 128) for a in smalls), bias_in.reshape(8, 128)),
@@ -918,9 +942,6 @@
             w_qkv.reshape(1, 256, 3 * D), w_out.reshape(1, 256, D), w_in.reshape(1, 256, FF),
             w_ff_out.reshape(4, 256, D),
         ),
-    )
-    red_ff, red_in, red_qo, sums = reduce_grads(
-        act_g, dbr_g, hid_g, dpre_g, x_g, dproj_g, ctx_g, datt_g, small_g
     )
     own_ff, own_in, own_qkv, own_out = widen_grads(red_ff, red_in, red_qo)
     sums = sums.reshape(3072)

time: 255 us -> 230 us (0.902)
  Pallas kernels: 248 us -> 224 us
    pallas_call x1 -> x0, Pallas kernels: 98.8 us -> none  [reduce_grads(): pl.pallas_call(reduce_kernel, out_shape=(full, full, full, jax.ShapeDtype...]
    pallas_call x1, Pallas kernels: 142 us -> 216 us  [layer(): pl.pallas_call(layer_kernel, out_shape=(sds(rows, bf), sds(rows, f32), sd...]
where the time goes in v5:
time: 230 us
  Pallas kernels  224 us (97%)
  local copies, waits for them, and re-layouts  5.47 us (2%)
    pallas_call x1, Pallas kernels, layer(): pl.pallas_call(layer_kernel, out_shape=(sds(rows, bf), sds(rows, f32), sd...  216 us
    pallas_call x1, Pallas kernels, widen_grads(): pl.pallas_call(widen_kernel, grid=(4,), out_shape=(sds((1024, 1024), f32)...  7.59 us

profile of v5, /device:TPU:0, one launch (start us, length us, event | category | flops | bytes accessed | tf_op | source)
XLA Modules:
  0.0 229.7 jit_solution(10459633458317255953)
XLA Ops:
  0.7 216.0 %shard_map.245 = (bf16[128,1024]{1,0:T(8,128)(2,1)}, f32[128,1024]{1,0:T(8,128)}, bf16[4,256,1024]{2,1,0:T(8,128)(2,1)}, bf16[4,256,1024]{2,1,0:T(8,128)(2,1)}, ...) custom-call(bf16[128,1024]{1,0:T(8,128)(2,1)} %bitcast.34, bf16[128,1024]{1,0:T(8,128)(2,1)} %bitcast.35, ...), custom_call_target="tpu_custom_call" | custom-call | tf_op jit(solution)/shard_map/pallas_call | solution.py:858
  216.7 0.7 slice.46
  217.3 0.6 reshape.101
  217.9 1.3 slice_bitcast_fusion
  219.2 1.4 slice_bitcast_fusion.1
  220.6 0.0 copy-start.1
  220.6 0.0 copy-start
  220.6 7.6 %shard_map.246 = (f32[1024,1024]{1,0:T(8,128)}, f32[256,4096]{1,0:T(8,128)}, f32[256,3072]{1,0:T(8,128)}, f32[256,1024]{1,0:T(8,128)}) custom-call(bf16[4,256,1024]{2,1,0:T(8,128)(2,1)} %get-tuple-element.26.ff, bf16[4,256,1024]{2,1,0:T(8,128)(2,1)} %get-tuple-element.27.in_, bf16[4,256,1024]{2,1,0:T(8,128)(2,1)} %get-tuple-element.28.qo), custom_call_target="tpu_custom_call" | custom-call | tf_op jit(solution)/shard_map/pallas_call | solution.py:914
  228.2 0.0 copy-done.1
  228.2 0.7 copy.30
  228.9 0.0 copy-done
  228.9 0.8 copy.31
Async XLA Ops:
  220.6 7.6 %copy-start.1 = (bf16[128,1024]{1,0:T(8,128)(2,1)S(1)}, bf16[128,1024]{1,0:T(8,128)(2,1)}, u32[]{:S(2)}) copy-start(bf16[128,1024]{1,0:T(8,128)(2,1)} %get-tuple-element.24) | copy-start | bytes 786436
  220.6 8.3 %copy-start = (f32[128,1024]{1,0:T(8,128)S(1)}, f32[128,1024]{1,0:T(8,128)}, u32[]{:S(2)}) copy-start(f32[128,1024]{1,0:T(8,128)} %get-tuple-element.25) | copy-start | bytes 1572868

commit v6 on v5

--- a/solution.py
+++ b/solution.py
@@ -58,8 +58,8 @@
         pltpu.make_async_remote_copy(
             src_ref=send.at[dest],
             dst_ref=recv.at[me],
-            send_sem=ssem.at[k],
-            recv_sem=rsem.at[k],
+            send_sem=ssem,
+            recv_sem=rsem,
             device_id={"ctx": dest},
             device_id_type=MESH,
         ).start()
@@ -69,21 +69,17 @@
 
 
 def a2a_wait(send, recv, ssem, rsem, me):
-    def step(k, carry):
-        source = lax.rem(me + NC - k, NC)
-        copy = pltpu.make_async_remote_copy(
-            src_ref=send.at[source],
-            dst_ref=recv.at[source],
-            send_sem=ssem.at[k],
-            recv_sem=rsem.at[k],
-            device_id={"ctx": source},
-            device_id_type=MESH,
-        )
-        copy.wait_send()
-        copy.wait_recv()
-        return carry
-
-    lax.fori_loop(1, NC, step, 0)
+    others = pl.ds(0, NC - 1)
+    copy = pltpu.make_async_remote_copy(
+        src_ref=send.at[others],
+        dst_ref=recv.at[others],
+        send_sem=ssem,
+        recv_sem=rsem,
+        device_id={"ctx": lax.rem(me + 1, NC)},
+        device_id_type=MESH,
+    )
+    copy.wait_recv()
+    copy.wait_send()
 
 
 def signal_ctx_peers(barrier, me):
@@ -128,23 +124,15 @@
 
 def rings():
     c, unused_s, y, z, x = place()
-    along_x = (
-        x,
-        {"ctx": c - x + lax.rem(x + 1, 4)},
-        {"ctx": c - x + lax.rem(x + 3, 4)},
-    )
-    along_z = (
-        z,
-        {"ctx": y * 16 + lax.rem(z + 1, 4) * 4 + x},
-        {"ctx": y * 16 + lax.rem(z + 3, 4) * 4 + x},
-    )
+    along_x = (x, *({"ctx": c - x + lax.rem(x + j, 4)} for j in range(1, 4)))
+    along_z = (z, *({"ctx": y * 16 + lax.rem(z + j, 4) * 4 + x} for j in range(1, 4)))
     return along_x, along_z
 
 
 class RingGather:
     def __init__(self, block, first, second, ring, ssem, rsem):
         self.block, self.first, self.second = block, first, second
-        self.p, self.up, self.down = ring
+        self.p, self.up, unused, self.down = ring
         self.ssem, self.rsem = ssem, rsem
 
     def at(self, k):
@@ -175,6 +163,23 @@
             copy.wait_send()
 
 
+class DirectGather:
+    def __init__(self, block, ring, ssem, rsem):
+        self.block, self.ring, self.ssem, self.rsem = block, ring, ssem, rsem
+
+    def start(self):
+        own = self.block(self.ring[0])
+        self.sent = [
+            send(own, own, self.ssem(j), self.rsem(j), self.ring[j]) for j in range(1, 4)
+        ]
+
+    def finish(self):
+        for j in range(1, 4):
+            got = self.block(lax.rem(self.ring[0] + 4 - j, 4))
+            remote(got, got, self.ssem(j), self.rsem(j), self.ring[j]).wait_recv()
+            self.sent[j - 1].wait_send()
+
+
 def sems(ref, *lead):
     return lambda k: ref.at[(*lead, k)]
 
@@ -188,8 +193,6 @@
 
 
 class WeightGather:
-    STEPS = 7
-
     def __init__(self, src, dst, n, ls, os, orr, cs, cr, gs, gr, fs, fr):
         c, s, y, z, x = place()
         sibling, cross, unused = group_ids()
@@ -221,10 +224,7 @@
             def part_of(make, cols):
                 return lambda p: make(p, cols=cols)
 
-            ring1 = RingGather(
-                small_block, part_of(small_block, cols_a), part_of(small_block, cols_b), one,
-                sems(gs, n, h, 0), sems(gr, n, h, 0),
-            )
+            ring1 = DirectGather(small_block, one, sems(gs, n, h, 0), sems(gr, n, h, 0))
             ring2 = RingGather(
                 big_block, part_of(big_block, cols_a), part_of(big_block, cols_b), two,
                 sems(gs, n, h, 1), sems(gr, n, h, 1),
@@ -243,9 +243,6 @@
                         self.cs.at[self.n, h], self.cr.at[self.n, h], self.cross,
                     )
                 )
-            self.local = pltpu.make_async_copy(self.src, self.dst.at[self.s], self.ls)
-            self.local.start()
-            self.own = send(self.src, self.dst.at[self.s], self.os, self.orr, self.sibling)
         elif k == 1:
             for h, row, cols, cols_a, cols_b, ring1, ring2, p in self.streams:
                 got = self.dst.at[self.far].at[:, rows16(row), cols]
@@ -253,18 +250,15 @@
                 ring1.start()
         elif k == 2:
             for h, row, cols, cols_a, cols_b, ring1, ring2, p in self.streams:
-                ring1.forward()
-        elif k == 3:
-            for h, row, cols, cols_a, cols_b, ring1, ring2, p in self.streams:
                 ring1.finish()
                 ring2.start()
                 self.pass_on(h, 0, rows64(p), cols)
-        elif k == 4:
+        elif k == 3:
             for h, row, cols, cols_a, cols_b, ring1, ring2, p in self.streams:
                 ring2.forward()
                 self.pass_on(h, 1, rows64(lax.rem(p + 3, 4)), cols)
                 self.pass_on(h, 2, rows64(lax.rem(p + 1, 4)), cols)
-        elif k == 5:
+        elif k == 4:
             for h, row, cols, cols_a, cols_b, ring1, ring2, p in self.streams:
                 ring2.finish()
                 self.pass_on(h, 3, rows64(lax.rem(p + 2, 4)), cols)
@@ -282,6 +276,11 @@
             for copy in self.sent:
                 copy.wait_send()
 
+    def share_own(self):
+        self.local = pltpu.make_async_copy(self.src, self.dst.at[self.s], self.ls)
+        self.local.start()
+        self.own = send(self.src, self.dst.at[self.s], self.os, self.orr, self.sibling)
+
     def pass_on(self, h, j, rows, cols):
         part = self.dst.at[self.far].at[:, rows, cols]
         self.sent.append(
@@ -321,7 +320,7 @@
 class RingReduce:
     def __init__(self, part, total, bufs, ring, ssem, rsem):
         self.part, self.total, self.bufs = part, total, bufs
-        self.p, self.up, self.down = ring
+        self.p, self.up, unused, self.down = ring
         self.ssem, self.rsem = ssem, rsem
 
     def at(self, k):
@@ -360,6 +359,28 @@
             ).astype(jnp.bfloat16)
         for copy in self.sent:
             copy.wait_send()
+
+
+class DirectReduce:
+    def __init__(self, part, total, landed, ring, ssem, rsem):
+        self.part, self.total, self.landed, self.ring = part, total, landed, ring
+        self.ssem, self.rsem = ssem, rsem
+
+    def start(self):
+        self.sent = [
+            send(
+                self.part(lax.rem(self.ring[0] + j, 4)), self.landed.at[j - 1], self.ssem(j),
+                self.rsem(j), self.ring[j],
+            )
+            for j in range(1, 4)
+        ]
+
+    def finish(self):
+        total = widen(self.part(self.ring[0])[...])
+        for j, copy in enumerate(self.sent):
+            copy.wait()
+            total = total + widen(self.landed[j])
+        self.total[...] = total.astype(jnp.bfloat16)
 
 
 class SmallSums:
@@ -400,57 +421,46 @@
 
 
 class Stream:
-    STEPS = 12
+    STEPS = 9
 
     def __init__(self, grad, out, m, h, scratch, dsems):
-        (room, small, t2, ybuf, u, v) = scratch
-        (p1s, p1r, p2s, p2r, ys, yr, ts, tr, ms, as_, ar, g1s, g1r, g2s, g2r) = dsems
+        (room, landed, t2, ybuf, u, v) = scratch
+        (p1s, p1r, p2s, p2r, ys, yr, ts, tr, ms, g1s, g1r, g2s, g2r) = dsems
         c, s, y, z, x = place()
         along_x, along_z = rings()
         one, two = (along_x, along_z) if h == 0 else (along_z, along_x)
         n = 2 * m + h
-        self.m, self.c, self.s, self.y = m, c, s, y
+        self.s = s
         self.pair = {"ctx": lax.rem(c + 16, 32)}
         self.t1, self.t2, self.u, self.v = room(24 + n), t2.at[n], u.at[n], v.at[n]
         down, up, first, second = (room(4 * n + k) for k in range(4))
         big = (first.at[0:2], first.at[2:4], second.at[0:2], second.at[2:4], down, up)
         self.ybuf = ybuf.at[n]
-        self.out = out
         self.ys, self.yr, self.ts, self.tr = ys.at[n], yr.at[n], ts.at[n], tr.at[n]
-        self.ms, self.as_, self.ar = ms.at[n], as_.at[n], ar.at[n]
+        self.ms = ms.at[n]
         cols = pl.ds(h * 512, 512)
         self.reduce1 = RingReduce(
             lambda p, k: grad.at[pl.ds(2 * k, 2), rows64(p), cols], self.t1,
             big, one, sems(p1s, n), sems(p1r, n),
         )
-        self.reduce2 = RingReduce(
-            lambda p, k: self.t1.at[pl.ds(2 * k, 2), rows16(p)], self.t2,
-            [b.at[n] for b in small], two, sems(p2s, n), sems(p2r, n),
-        )
-        row = one[0] * 4 + two[0]
-
-        def mine(who):
-            at = pl.multiple_of(h * 512 + who * 256, 256)
-            return out.at[:, rows16(row), pl.ds(at, 256)]
-
-        self.mine = mine
-
-        def small_block(p, lead=pl.ds(0, 4)):
-            return out.at[lead, rows16(one[0] * 4 + p), cols]
+        self.reduce2 = DirectReduce(
+            lambda p: self.t1.at[:, rows16(p)], self.t2, landed.at[n], two,
+            sems(p2s, n), sems(p2r, n),
+        )
+        self.mine = out.at[:, rows16(one[0] * 4 + two[0]), cols]
+
+        def small_block(p):
+            return out.at[:, rows16(one[0] * 4 + p), cols]
 
         def big_block(p, lead=pl.ds(0, 4)):
             return out.at[lead, rows64(p), cols]
 
-        def half_of(make, k):
-            return lambda p: make(p, lead=pl.ds(2 * k, 2))
-
-        self.gather1 = RingGather(
-            small_block, half_of(small_block, 0), half_of(small_block, 1), two,
-            sems(g1s, n), sems(g1r, n),
-        )
+        def half_of(k):
+            return lambda p: big_block(p, lead=pl.ds(2 * k, 2))
+
+        self.gather1 = DirectGather(small_block, two, sems(g1s, n), sems(g1r, n))
         self.gather2 = RingGather(
-            big_block, half_of(big_block, 0), half_of(big_block, 1), one,
-            sems(g2s, n), sems(g2r, n),
+            big_block, half_of(0), half_of(1), one, sems(g2s, n), sems(g2r, n)
         )
 
     def step(self, k):
@@ -462,54 +472,129 @@
             self.reduce1.finish()
             self.reduce2.start()
         elif k == 3:
-            self.reduce2.middle()
+            self.reduce2.finish()
+            self.sent_y = send(self.t2, self.ybuf, self.ys, self.yr, self.pair)
         elif k == 4:
-            self.reduce2.finish()
-            other = pl.ds(pl.multiple_of(256 - self.y * 256, 256), 256)
-            self.sent_y = send(self.t2.at[:, :, other], self.ybuf, self.ys, self.yr, self.pair)
+            self.sent_y.wait()
+            total = (widen(self.t2[...]) + widen(self.ybuf[...])).astype(jnp.bfloat16)
+            self.u[...] = total
+            self.turned = []
+            for j in range(1, 4):
+                owner = lax.rem(self.s + j, 4)
+                self.turned.append(
+                    send(
+                        self.u.at[owner], self.v.at[self.s], self.ts.at[j], self.tr.at[j],
+                        {"shard": owner},
+                    )
+                )
+            self.v[self.s] = self.u[self.s]
         elif k == 5:
-            self.sent_y.wait()
-            own = pl.ds(pl.multiple_of(self.y * 256, 256), 256)
-            total = (widen(self.t2[:, :, own]) + widen(self.ybuf[...])).astype(jnp.bfloat16)
-            if self.m == 0:
-                self.v[...] = total
-            else:
-                self.u[...] = total
-                self.turned = []
-                for j in range(1, 4):
-                    owner = lax.rem(self.s + j, 4)
-                    self.turned.append(
-                        send(
-                            self.u.at[owner], self.v.at[self.s], self.ts.at[j], self.tr.at[j],
-                            {"shard": owner},
-                        )
-                    )
-                self.v[self.s] = self.u[self.s]
+            for j in range(1, 4):
+                source = lax.rem(self.s + 4 - j, 4)
+                got = self.v.at[source]
+                remote(got, got, self.ts.at[j], self.tr.at[j], {"shard": source}).wait_recv()
+                self.turned[j - 1].wait_send()
+            kept = pltpu.make_async_copy(self.v, self.mine, self.ms)
+            kept.start()
+            kept.wait()
+            self.gather1.start()
         elif k == 6:
-            if self.m > 0:
-                for j in range(1, 4):
-                    source = lax.rem(self.s + 4 - j, 4)
-                    got = self.v.at[source]
-                    remote(got, got, self.ts.at[j], self.tr.at[j], {"shard": source}).wait_recv()
-                    self.turned[j - 1].wait_send()
-            self.kept = pltpu.make_async_copy(self.v, self.mine(self.y), self.ms)
-            self.kept.start()
-            self.shared = send(self.v, self.mine(self.y), self.as_, self.ar, self.pair)
-        elif k == 7:
-            self.kept.wait()
-            self.shared.wait_send()
-            got = self.mine(1 - self.y)
-            remote(got, got, self.as_, self.ar, self.pair).wait_recv()
-            self.gather1.start()
-        elif k == 8:
-            self.gather1.forward()
-        elif k == 9:
             self.gather1.finish()
             self.gather2.start()
-        elif k == 10:
+        elif k == 7:
             self.gather2.forward()
         else:
             self.gather2.finish()
+
+
+class PairFirst:
+    def __init__(self, grad, out, h, scratch, landed, dsems, pass_s, pass_r):
+        (room, landed2, t2, unused_y, unused_u, unused_v) = scratch
+        (p1s, p1r, p2s, p2r, ys, yr, ts, tr, ms, g1s, g1r, g2s, g2r) = dsems
+        c, s, y, z, x = place()
+        along_x, along_z = rings()
+        one, two = (along_x, along_z) if h == 0 else (along_z, along_x)
+        self.p = one[0]
+        self.grad, self.out, self.landed = grad, out, landed.at[h]
+        self.pair = {"ctx": lax.rem(c + 16, 32)}
+        self.own = pl.ds(pl.multiple_of(h * 512 + y * 256, 256), 256)
+        self.other = pl.ds(pl.multiple_of(h * 512 + 256 - y * 256, 256), 256)
+        own, other = self.own, self.other
+        left = pl.ds(0, 256)
+        self.t2 = t2.at[h, :, :, left]
+        self.ys, self.yr, self.ms = ys.at[h], yr.at[h], ms.at[h]
+        self.pass_s, self.pass_r = pass_s, pass_r
+        self.h = h
+        t1 = room(24 + h).at[:, :, left]
+        down, up, first, second = (room(4 * h + k).at[:, :, left] for k in range(4))
+        self.reduce1 = RingReduce(
+            lambda p, k: grad.at[pl.ds(2 * k, 2), rows64(p), own], t1,
+            (first.at[0:2], first.at[2:4], second.at[0:2], second.at[2:4], down, up),
+            one, sems(p1s, h), sems(p1r, h),
+        )
+        self.reduce2 = DirectReduce(
+            lambda p: t1.at[:, rows16(p)], self.t2, landed2.at[h, :, :, :, left], two,
+            sems(p2s, h), sems(p2r, h),
+        )
+        self.mine = out.at[:, rows16(one[0] * 4 + two[0]), own]
+
+        def big_block(p, lead=pl.ds(0, 4)):
+            return out.at[lead, rows64(p), own]
+
+        self.gather1 = DirectGather(
+            lambda p: out.at[:, rows16(one[0] * 4 + p), own], two, sems(g1s, h), sems(g1r, h)
+        )
+        self.gather2 = RingGather(
+            big_block, lambda p: big_block(p, lead=pl.ds(0, 2)),
+            lambda p: big_block(p, lead=pl.ds(2, 2)), one, sems(g2s, h), sems(g2r, h),
+        )
+        self.passed = []
+
+    def pass_on(self, j, shift):
+        part = self.out.at[:, rows64(lax.rem(self.p + shift, 4)), self.own]
+        self.passed.append(
+            send(part, part, self.pass_s.at[self.h, j], self.pass_r.at[self.h, j], self.pair)
+        )
+
+    def step(self, k):
+        if k == 0:
+            self.sent_y = send(
+                self.grad.at[:, :, self.other], self.landed, self.ys, self.yr, self.pair
+            )
+        elif k == 1:
+            self.sent_y.wait()
+            for q in range(4):
+                total = widen(self.grad[q, :, self.own]) + widen(self.landed[q])
+                self.grad[q, :, self.own] = total.astype(jnp.bfloat16)
+            self.reduce1.start()
+        elif k == 2:
+            self.reduce1.middle()
+        elif k == 3:
+            self.reduce1.finish()
+            self.reduce2.start()
+        elif k == 4:
+            self.reduce2.finish()
+            kept = pltpu.make_async_copy(self.t2, self.mine, self.ms)
+            kept.start()
+            kept.wait()
+            self.gather1.start()
+        elif k == 5:
+            self.gather1.finish()
+            self.gather2.start()
+            self.pass_on(0, 0)
+        elif k == 6:
+            self.gather2.forward()
+            self.pass_on(1, 3)
+            self.pass_on(2, 1)
+        elif k == 7:
+            self.gather2.finish()
+            self.pass_on(3, 2)
+        else:
+            for j, shift in enumerate((0, 3, 1, 2)):
+                got = self.out.at[:, rows64(lax.rem(self.p + shift, 4)), self.other]
+                sems_at = self.pass_s.at[self.h, j], self.pass_r.at[self.h, j]
+                remote(got, got, *sems_at, self.pair).wait_recv()
+                self.passed[j].wait_send()
 
 
 def normalized(values):
@@ -531,7 +616,7 @@
     wq, wo, wi, wf, params, params_all, proj, q_send, q_recv, c_send, c_recv, g_send, g_recv,
     p_send, p_recv, keys, vt, kt, vals, dk, dv, o_s, lse_s, act, gelu_d, dpre, datt, dctx, dproj,
     hidden, unit_one, d_first, small, small_totals, small_landed,
-    ra2, rb2, sa2, sb2, fd2, fu2, t2, ybuf, u, v,
+    landed1, landed2, t2, ybuf, u, v, pass_s, pass_r,
     qss, qrs, css, crs, gss, grs, pss, prs, xs, xr, fs, fr, ls, es, er, els, ms, mr, sss, srs, *more
 ):
     bf, f32 = jnp.bfloat16, jnp.float32
@@ -598,21 +683,20 @@
                 copy.wait()
 
     gather_q.step(0)
+    gather_q.share_own()
     sent_params = [
         to_peer(params, params_all.at[shard], ms.at[k], mr.at[k], peer)
         for k, peer in enumerate(peers)
     ]
     advance(gathers, 0)
+    for k in range(1, 5):
+        gather_q.step(k)
+    advance(gathers, 1)
+    gather_q.step(5)
+    for gather in gathers:
+        gather.share_own()
     share_whole(3, x_g)
-    gather_q.step(1)
-    gather_q.step(2)
-    gather_q.step(3)
-    advance(gathers, 1)
-    gather_q.step(4)
-    advance(gathers, 2)
-    gather_q.step(5)
-    gather_q.step(6)
-    advance(early, 3)
+    advance(early, 2)
     for k, peer in enumerate(peers):
         sent_params[k].wait_send()
         got = params_all.at[peer[1]]
@@ -637,8 +721,8 @@
     a2a_start(q_send, q_recv, qss, qrs, me)
     q_recv[me] = q_send[me]
     a2a_wait(q_send, q_recv, qss, qrs, me)
-    advance(early, 4)
-    advance(late, 3)
+    advance(early, 3)
+    advance(late, 2)
     keys[...] = halves(q_recv[:, 32:64, :].reshape(1024, 128))
     vals[...] = halves(q_recv[:, 64:96, :].reshape(1024, 128))
     vp = widen(q_recv[:, 64:96, :].reshape(1024, 128)).T.astype(bf)
@@ -663,15 +747,15 @@
         return carry
 
     lax.fori_loop(0, steps // 2, attend, 0)
-    advance(early, 5)
-    advance(late, 4)
+    advance(early, 4)
+    advance(late, 3)
     lax.fori_loop(steps // 2, steps, attend, 0)
     a2a_start(c_send, c_recv, css, crs, me)
     c_recv[me] = c_send[me]
     a2a_wait(c_send, c_recv, css, crs, me)
     unpack_tokens(c_recv, ctx_g.at[0], 1)
     share_whole(2, ctx_g)
-    advance(early, 6)
+    advance(early, 5)
 
     w_out_whole = wo[...].reshape(D, D)
     first_sum = widen(x[...]) + (dot_nn(ctx_g[0], w_out_whole) + vector(0))
@@ -692,8 +776,8 @@
 
     lax.fori_loop(0, 4, feed, 0)
     share_slices(4, act, act_g, 1024)
+    advance(late, 4)
     advance(late, 5)
-    advance(late, 6)
 
     def feed_out(j, total):
         return total + dot_nn(act[:, cols_of(j)], wf[j].reshape(D, D))
@@ -746,7 +830,7 @@
     def room(k):
         return wi.at[:, 0, pl.ds(64 * (k % 4), 64), pl.ds(512 * (k // 4), 512)]
 
-    scratch = (room, (ra2, rb2, sa2, sb2, fd2, fu2), t2, ybuf, u, v)
+    scratch = (room, landed2, t2, ybuf, u, v)
 
     def product(m, left, right, at):
         width = right.shape[-1]
@@ -762,7 +846,13 @@
         lax.fori_loop(0, 4, block, 0)
 
     def streams_of(m, out):
-        streams = [Stream(wf.at[m], out, m, h, scratch, dsems) for h in range(2)]
+        if m == 0:
+            streams = [
+                PairFirst(wf.at[m], out, h, scratch, landed1, dsems, pass_s, pass_r)
+                for h in range(2)
+            ]
+        else:
+            streams = [Stream(wf.at[m], out, m, h, scratch, dsems) for h in range(2)]
         for stream in streams:
             stream.step(0)
         return streams
@@ -790,21 +880,31 @@
         p_send[blocks, 0:32, :] = dq.astype(bf).reshape(blocks_of, 32, 128)
         return carry
 
-    lax.fori_loop(0, steps // 2, attend_back, 0)
+    def proceed(streams, k):
+        for stream in streams:
+            stream.step(k)
+
+    lax.fori_loop(0, steps // 4, attend_back, 0)
     pass_on(1, dbr_g)
     arrived(4, 1)
     product(0, act_g, dbr_g, 0)
     ff_streams = streams_of(0, ff_out)
-    lax.fori_loop(steps // 2, steps, attend_back, 0)
+    lax.fori_loop(steps // 4, steps // 2, attend_back, 0)
+    proceed(ff_streams, 1)
+    lax.fori_loop(steps // 2, steps // 4 * 3, attend_back, 0)
+    proceed(ff_streams, 2)
+    lax.fori_loop(steps // 4 * 3, steps, attend_back, 0)
+    proceed(ff_streams, 3)
     for n, total in enumerate((dk, dv)):
         packed = jnp.concatenate([total[0:1024, :], total[1024:2048, :]], axis=1)
         p_send[:, 32 + 32 * n : 64 + 32 * n, :] = packed.astype(bf).reshape(NC, 32, 128)
     a2a_start(p_send, p_recv, pss, prs, me)
     p_recv[me] = p_send[me]
-    for stream in ff_streams:
-        stream.step(1)
+    proceed(ff_streams, 4)
     arrived(0, 5)
     product(1, hid_g, dpre_g, 0)
+    in_streams = streams_of(1, in_out)
+    proceed(ff_streams, 5)
     a2a_wait(p_send, p_recv, pss, prs, me)
     unpack_tokens(p_recv, dproj, 3)
     cols = pl.ds(pl.multiple_of(shard * 768, 256), 768)
@@ -814,7 +914,8 @@
     for k, peer in enumerate(peers):
         cols = pl.ds(pl.multiple_of(peer[1] * 768, 256), 768)
         pending[7].append(to_peer(dproj.at[:, cols], dproj_g.at[k + 1], es.at[k], er.at[k], peer))
-    in_streams = streams_of(1, in_out)
+    proceed(in_streams, 1)
+    proceed(ff_streams, 6)
     put_sums(10, widen(dproj[:, 0:D]))
     put_sums(11, widen(dproj[:, 2 * D : 3 * D]))
     small_g[0] = small[shard]
@@ -822,31 +923,40 @@
         to_peer(small.at[peer[1]], small_g.at[k + 1], es.at[3 + k], er.at[3 + k], peer)
         for k, peer in enumerate(peers)
     ]
-    for stream in ff_streams:
-        stream.step(2)
 
     def back_in(j, total):
         weight = wq[:, 0, :, cols_of(j)].reshape(D, D)
         return total + dot_nt(dproj[:, cols_of(j)], weight)
 
     d_inputs[...] = lax.fori_loop(0, 3, back_in, d_first[...])
-    for stream in in_streams:
-        stream.step(1)
+    proceed(in_streams, 2)
+    proceed(ff_streams, 7)
     arrived(2, 3, 6)
     product(2, ctx_g, datt_g, 768)
+    proceed(in_streams, 3)
     arrived(7)
     product(2, x_g, dproj_g, 0)
     qo_streams = streams_of(2, qo_out)
+    proceed(in_streams, 4)
     arrived(8)
     sums = SmallSums(small_g, small_totals, small_landed, small_out, sss, srs)
     sums.step(0)
-    for k in range(1, Stream.STEPS):
-        for streams, ahead in ((ff_streams, 2), (in_streams, 1), (qo_streams, 0)):
-            if k + ahead < Stream.STEPS:
-                for stream in streams:
-                    stream.step(k + ahead)
-        if k % 2 == 1 and k // 2 + 1 < SmallSums.STEPS:
-            sums.step(k // 2 + 1)
+    proceed(qo_streams, 1)
+    proceed(in_streams, 5)
+    proceed(ff_streams, 8)
+    proceed(qo_streams, 2)
+    sums.step(1)
+    proceed(in_streams, 6)
+    proceed(qo_streams, 3)
+    sums.step(2)
+    proceed(qo_streams, 4)
+    proceed(in_streams, 7)
+    proceed(qo_streams, 5)
+    sums.step(3)
+    proceed(qo_streams, 6)
+    proceed(in_streams, 8)
+    proceed(qo_streams, 7)
+    proceed(qo_streams, 8)
 
 
 def layer(x, cot, smalls, weights):
@@ -880,19 +990,19 @@
             vm((128, 3 * D), bf), vm(rows, f32), vm(rows, f32), vm(rows, f32),
             vm((4, 24, 128), f32), vm((3, 24, 128), f32), vm((3, 3, 24, 128), f32),
         ]
-        + [vm((6, 2, 16, 512), bf)] * 4
-        + [vm((6, 4, 16, 512), bf)] * 3
-        + [vm((6, 4, 16, 256), bf)] * 3
-        + [dma((NC,))] * 8
+        + [vm((2, 4, 256, 256), bf), vm((6, 3, 4, 16, 512), bf)]
+        + [vm((6, 4, 16, 512), bf)] * 4
+        + [dma((2, 4)), dma((2, 4))]
+        + [dma] * 8
         + [
             dma((7, 3)), dma((7, 3)), dma((4,)), dma((4,)), dma((3,)),
             dma((6,)), dma((6,)), dma((1,)), dma((3,)), dma((3,)), dma((3, 3)), dma((3, 3)),
         ]
         + weight_sems(4)
         + [
-            dma((6, 6)), dma((6, 6)), dma((6, 6)), dma((6, 6)), dma((6,)), dma((6,)),
-            dma((6, 4)), dma((6, 4)), dma((6,)), dma((6,)), dma((6,)),
-            dma((6, 4)), dma((6, 4)), dma((6, 4)), dma((6, 4)),
+            dma((6, 6)), dma((6, 6)), dma((6, 4)), dma((6, 4)), dma((6,)), dma((6,)),
+            dma((6, 4)), dma((6, 4)), dma((6,)), dma((6, 4)), dma((6, 4)), dma((6, 4)),
+            dma((6, 4)),
         ],
         compiler_params=pltpu.CompilerParams(
             collective_id=0, has_side_effects=True, vmem_limit_bytes=62 * 1024 * 1024
@@ -900,33 +1010,48 @@
     )(x, cot, *smalls, *weights)
 
 
-def widen_kernel(ff, in_, qo, ff_out, in_out, qkv_out, w_out):
+def widen_kernel(ff, in_, qo, sums, ff_out, in_out, qkv_out, w_out, b_in, b_qv, *vectors):
     ff_out[...] = widen(ff[0])
     in_out[...] = widen(in_[0])
     qkv_out[...] = widen(qo[0, :, :768])
     w_out[...] = widen(qo[0, :, 768:])
-
-
-def widen_grads(ff, in_, qo):
+    for n, ref in enumerate(vectors):
+        ref[...] = sums[2 * n : 2 * n + 2, :]
+    b_in[...] = sums[12:20, :]
+    for n in range(2):
+        for k in range(2):
+            row = 20 + 2 * n + k
+            b_qv[n : n + 1, 128 * k : 128 * k + 128] = sums[row : row + 1, :]
+
+
+def widen_grads(ff, in_, qo, sums):
     sds = jax.ShapeDtypeStruct
     f32 = jnp.float32
     block = pl.BlockSpec((1, 256, 1024), lambda q: (q, 0, 0))
+
+    def whole(shape):
+        return pl.BlockSpec(shape, lambda q: (0, 0))
+
     return pl.pallas_call(
         widen_kernel,
         grid=(4,),
         out_shape=(
             sds((1024, 1024), f32), sds((256, 4096), f32), sds((256, 3072), f32),
-            sds((256, 1024), f32),
-        ),
-        in_specs=[block] * 3,
+            sds((256, 1024), f32), sds((8, 128), f32), sds((2, 256), f32),
+        )
+        + (sds((2, 128), f32),) * 6,
+        in_specs=[block] * 3 + [whole((24, 128))],
         out_specs=(
             pl.BlockSpec((256, 1024), lambda q: (q, 0)),
             pl.BlockSpec((256, 1024), lambda q: (0, q)),
             pl.BlockSpec((256, 768), lambda q: (0, q)),
             pl.BlockSpec((256, 256), lambda q: (0, q)),
-        ),
+            whole((8, 128)),
+            whole((2, 256)),
+        )
+        + (whole((2, 128)),) * 6,
         compiler_params=pltpu.CompilerParams(vmem_limit_bytes=VMEM_LIMIT),
-    )(ff, in_, qo)
+    )(ff, in_, qo, sums)
 
 
 def local(
@@ -943,27 +1068,25 @@
             w_ff_out.reshape(4, 256, D),
         ),
     )
-    own_ff, own_in, own_qkv, own_out = widen_grads(red_ff, red_in, red_qo)
-    sums = sums.reshape(3072)
-
-    def own(k):
-        return sums[256 * k : 256 * k + 256]
-
+    own_ff, own_in, own_qkv, own_out, own_b_in, own_b_qv, *own = widen_grads(
+        red_ff, red_in, red_qo, sums
+    )
+    own = [a.reshape(256) for a in own]
     return (
         result.reshape(inputs.shape),
         d_inputs.reshape(inputs.shape),
         own_qkv,
-        sums[2560:].reshape(2, 256),
+        own_b_qv,
         own_out,
-        own(0),
-        own(1),
-        own(2),
+        own[0],
+        own[1],
+        own[2],
         own_in,
-        sums[1536:2560],
+        own_b_in.reshape(1024),
         own_ff,
-        own(3),
-        own(4),
-        own(5),
+        own[3],
+        own[4],
+        own[5],
     )
 
 

time: 230 us -> 244 us (1.061)
  Pallas kernels: 224 us -> 242 us
  local copies, waits for them, and re-layouts: 5.47 us -> 1.51 us
    pallas_call x1, Pallas kernels: 216 us -> 234 us  [layer(): pl.pallas_call(layer_kernel, out_shape=(sds(rows, bf), sds(rows, f32), sd...]
    slice x3 -> x0, local copies, waits for them, and re-layouts: 3.38 us -> none  [the longest x1 1.41 us: own(): return sums[256 * k:256 * k + 256]]
where the time goes in v6:
time: 244 us
  Pallas kernels  242 us (99%)
    pallas_call x1, Pallas kernels, layer(): pl.pallas_call(layer_kernel, out_shape=(sds(rows, bf), sds(rows, f32), sd...  234 us
    pallas_call x1, Pallas kernels, widen_grads(): pl.pallas_call(widen_kernel, grid=(4,), out_shape=(sds((1024, 1024), f32)...  7.79 us

profile of v6, /device:TPU:0, one launch (start us, length us, event | category | flops | bytes accessed | tf_op | source)
XLA Modules:
  0.0 243.8 jit_solution(8467334590282516079)
XLA Ops:
  0.7 233.8 %shard_map.245 = (bf16[128,1024]{1,0:T(8,128)(2,1)}, f32[128,1024]{1,0:T(8,128)}, bf16[4,256,1024]{2,1,0:T(8,128)(2,1)}, bf16[4,256,1024]{2,1,0:T(8,128)(2,1)}, ...) custom-call(bf16[128,1024]{1,0:T(8,128)(2,1)} %bitcast.27, bf16[128,1024]{1,0:T(8,128)(2,1)} %bitcast.28, ...), custom_call_target="tpu_custom_call" | custom-call | tf_op jit(solution)/shard_map/pallas_call | solution.py:968
  234.4 0.0 copy-start.1
  234.4 0.0 copy-start
  234.5 7.8 %shard_map.246 = (f32[1024,1024]{1,0:T(8,128)}, f32[256,4096]{1,0:T(8,128)}, f32[256,3072]{1,0:T(8,128)}, f32[256,1024]{1,0:T(8,128)}, f32[8,128]{1,0:T(8,128)},...) custom-call(bf16[4,256,1024]{2,1,0:T(8,128)(2,1)} %get-tuple-element, ...), custom_call_target="tpu_custom_call" | custom-call | tf_op jit(solution)/shard_map/pallas_call | solution.py:1035
  242.2 0.0 copy-done.1
  242.3 0.7 copy.30
  243.0 0.0 copy-done
  243.0 0.8 copy.31
Async XLA Ops:
  234.4 7.8 %copy-start.1 = (bf16[128,1024]{1,0:T(8,128)(2,1)S(1)}, bf16[128,1024]{1,0:T(8,128)(2,1)}, u32[]{:S(2)}) copy-start(bf16[128,1024]{1,0:T(8,128)(2,1)} %get-tuple-element.32) | copy-start | bytes 786436
  234.4 8.5 %copy-start = (f32[128,1024]{1,0:T(8,128)S(1)}, f32[128,1024]{1,0:T(8,128)}, u32[]{:S(2)}) copy-start(f32[128,1024]{1,0:T(8,128)} %get-tuple-element.33) | copy-start | bytes 1572868
